TPU v7x, 256 devices: a whole 4x4x8 slice. The times are simulated.
256 devices in a mesh: role: 2 (over y_hi), pair: 2 (over core), dev: 64 (over x, z, y_lo).
Axes of the slice: x: 4, y: 4 (y_hi: 2, y_lo: 2; y = y_hi * 2 + y_lo), z: 8, core: 2. Of those that a mesh axis runs over, the one named last changes fastest.
Arguments:
- hidden_in: bfloat16 [2048, 7168], P(('role', 'pair', 'dev')), may hold values from -6 to 6
- queries: bfloat16 [2048, 8192], P(('role', 'pair', 'dev')), may hold values from -8 to 8
- new_kv: bfloat16 [2048, 512], P(('role', 'pair', 'dev')), may hold values from -6 to 6
- kv_cache: bfloat16 [4096, 256, 512], P(('role', 'pair', 'dev')), may hold values from -6 to 6
- block_counts: int32 [256, 8], P(('role', 'pair', 'dev')), may hold values from 1 to 8, 16 in all within a row
- tail_lens: int32 [2048], P(('role', 'pair', 'dev')), may hold values from 1 to 256
- block_order: int32 [256, 16], P(('role', 'pair', 'dev')), may hold values from 0 to 15, each once within a row
- out_weight: bfloat16 [8192, 7168], P(None, 'dev'), may hold values from -0.0625 to 0.0625
- norm_gain: float32 [7168], P('dev'), may hold values from 0.25 to 1.75
- gate_weight: bfloat16 [7168, 9216], P(None, 'dev'), may hold values from -0.0625 to 0.0625
- up_weight: bfloat16 [7168, 9216], P(None, 'dev'), may hold values from -0.0625 to 0.0625
- down_weight: bfloat16 [9216, 7168], P('dev'), may hold values from -0.0625 to 0.0625
Outputs:
- hidden_out: bfloat16 [2048, 7168], P(('role', 'pair', 'dev'))
Inputs may be any that keep to these rules, and one draw needn't show every extreme that they name: `block_counts`: each row sums to 16 and its largest entry is 8. `block_order`: each row is a permutation of 0 .. 15.
All inputs are finite; a program needn't handle non-finite values.
Results may differ from a plain program's by a relative error of at most 0.005.
Values may be sent and summed in bfloat16 or wider, within the bound.
No kernel may reach another device: no remote copies, remote signals or barrier semaphores. Data moves between devices by JAX's collectives and lax.ppermute only.
A program may use at most 128 MiB of HBM per device.

v0:
```python
import jax
import jax.numpy as jnp
from jax import lax
from jax.sharding import PartitionSpec as P

norm_eps = 1e-05


def attend(queries, new_kv, kv_cache, block_counts, tail_lens, block_order):
    row_count = queries.shape[0]
    pool_size, block_len, twice = kv_cache.shape
    head_size = twice // 2
    head_count = queries.shape[1] // head_size
    score_scale = head_size ** (-0.5)
    starts = jnp.cumsum(block_counts) - block_counts
    slot_ids = jnp.arange(pool_size, dtype=jnp.int32)
    position = jnp.sum(
        jnp.where(block_order[None, :] == slot_ids[:, None], slot_ids[None, :], 0), axis=1
    )
    belongs = (starts[None, :] <= position[:, None]) & (
        position[:, None] < (starts + block_counts)[None, :]
    )
    block_rank = position - jnp.sum(jnp.where(belongs, starts[None, :], 0), axis=1)
    context = (block_counts - 1) * block_len + tail_lens
    offsets = block_rank[:, None] * block_len + jnp.arange(block_len, dtype=jnp.int32)[None, :]
    valid = jnp.transpose(belongs)[:, :, None] & (offsets[None, :, :] < context[:, None, None])
    valid = valid.reshape(row_count, pool_size * block_len)
    keys_all = kv_cache[:, :, :head_size].reshape(pool_size * block_len, head_size)
    values_all = kv_cache[:, :, head_size:].reshape(pool_size * block_len, head_size)
    query_rows = queries.reshape(row_count * head_count, head_size)
    scores = lax.dot_general(
        query_rows, keys_all, (((1,), (1,)), ((), ())), preferred_element_type=jnp.float32
    )
    scores = scores.reshape(row_count, head_count, pool_size * block_len) * score_scale
    masked = jnp.where(valid[:, None, :], scores, -jnp.inf)
    new_keys = new_kv[:, :head_size].astype(jnp.float32)
    new_vals = new_kv[:, head_size:].astype(jnp.float32)
    own_score = (
        jnp.sum(
            queries.reshape(row_count, head_count, head_size).astype(jnp.float32)
            * new_keys[:, None, :],
            axis=2,
        )
        * score_scale
    )
    row_max = jnp.maximum(jnp.max(masked, axis=2), own_score)
    weights = jnp.exp(masked - row_max[:, :, None])
    own_weight = jnp.exp(own_score - row_max)
    denom_sum = jnp.sum(weights, axis=2) + own_weight
    probs = (
        (weights / denom_sum[:, :, None])
        .astype(jnp.bfloat16)
        .reshape(row_count * head_count, pool_size * block_len)
    )
    mixed_vals = jnp.dot(probs, values_all, preferred_element_type=jnp.float32).reshape(
        row_count, head_count, head_size
    )
    mixed_vals = mixed_vals + (own_weight / denom_sum)[:, :, None] * new_vals[:, None, :]
    return mixed_vals.reshape(row_count, head_count * head_size).astype(jnp.bfloat16)


def per_device(
    hidden_in,
    queries,
    new_kv,
    kv_cache,
    block_counts,
    tail_lens,
    block_order,
    out_weight,
    norm_gain,
    gate_weight,
    up_weight,
    down_weight,
):
    attended = attend(queries, new_kv, kv_cache, block_counts[0], tail_lens, block_order[0])
    residual_cols = lax.all_to_all(hidden_in, "dev", split_axis=1, concat_axis=0, tiled=True)
    projected = jnp.dot(
        lax.all_gather(attended, "dev", axis=0, tiled=True),
        out_weight,
        preferred_element_type=jnp.float32,
    )
    stream = residual_cols.astype(jnp.float32) + projected
    model_width = hidden_in.shape[1]
    square_sums = lax.psum(jnp.sum(stream * stream, axis=1), "dev")
    row_scale = lax.rsqrt(square_sums / model_width + norm_eps)
    normed = (stream * row_scale[:, None] * norm_gain[None, :]).astype(jnp.bfloat16)
    shard_part = lax.all_gather(normed, "dev", axis=1, tiled=True)
    gate_proj = jnp.dot(shard_part, gate_weight, preferred_element_type=jnp.float32)
    up_proj = jnp.dot(shard_part, up_weight, preferred_element_type=jnp.float32)
    hidden_act = (jax.nn.silu(gate_proj) * up_proj).astype(jnp.bfloat16)
    col_begin = lax.axis_index("dev") * stream.shape[1]
    placed = lax.dynamic_update_slice(
        jnp.zeros((lax.axis_size("dev") * hidden_in.shape[0], model_width), jnp.float32),
        stream,
        (jnp.int32(0), col_begin),
    )
    summed = lax.psum_scatter(
        jnp.dot(hidden_act, down_weight, preferred_element_type=jnp.float32) + placed,
        "dev",
        scatter_dimension=0,
        tiled=True,
    )
    finished = summed.astype(jnp.bfloat16)
    return finished


def solution(mesh):
    return jax.shard_map(
        per_device,
        mesh=mesh,
        in_specs=(
            P(("role", "pair", "dev"), None),
            P(("role", "pair", "dev"), None),
            P(("role", "pair", "dev"), None),
            P(("role", "pair", "dev"), None, None),
            P(("role", "pair", "dev"), None),
            P(("role", "pair", "dev")),
            P(("role", "pair", "dev"), None),
            P(None, "dev"),
            P("dev"),
            P(None, "dev"),
            P(None, "dev"),
            P("dev", None),
        ),
        out_specs=P(("role", "pair", "dev"), None),
        check_vma=False,
    )
```

profile of v0, /device:TPU:16, one launch (start us, length us, event | category | flops | bytes accessed | tf_op | source)
XLA Modules:
  0.0 1181.4 jit_solution(1358439743178306909)
XLA Ops:
  6.5 0.9 select_reduce_fusion
  7.5 0.8 reduce-window.4
  8.3 0.7 fusion.17
  9.1 0.7 bitcast_add_fusion
  9.8 0.7 slice_convert_fusion
  10.5 1.0 multiply_reduce_fusion
  11.6 2.7 fusion.19
  14.6 0.9 fusion.20
  15.5 0.7 fusion.1
  16.2 0.9 fusion.7
  17.2 0.7 copy.44
  18.0 0.2 all_to_all.10
  18.3 23.8 %all_to_all.13 = bf16[8,64,112]{2,0,1:T(8,128)(2,1)S(1)} all-to-all(bf16[8,64,112]{2,0,1:T(8,128)(2,1)S(1)} %copy.36), channel_id=1, replica_groups=mesh['role'=2,'pair'=2,'dev'=64] {'dev'}, dimensions={1} | all-to-all | bytes 229376 | tf_op jit(solution)/shard_map/all_to_all | solution.py:77
  42.2 290.7 %all-gather.3.cloned.1.call-done = bf16[512,8192]{1,0:T(8,128)(2,1)} async-done(((bf16[8,8192]{1,0:T(8,128)(2,1)}), bf16[512,8192]{1,0:T(8,128)(2,1)}) %all-gather.3.cloned.1.call-update) | async-done | bytes 8388624 | tf_op jit(solution)/shard_map/all_gather | solution.py:79
  332.9 6.7 multiply_reduce_fusion.1
  339.7 156.8 %psum.7 = f32[512]{0:T(512)S(1)} all-reduce(f32[512]{0:T(512)S(1)} %get-tuple-element.13), channel_id=1, replica_groups=mesh['role'=2,'pair'=2,'dev'=64] {'dev'}, use_global_device_ids=true, to_apply=%region_7.8 | all-reduce | flops 512 | bytes 4096 | tf_op jit(solution)/shard_map/psum | solution.py:85
  496.5 0.7 multiply_convert_fusion
  497.3 305.5 %all-gather.5.cloned.1.call-done = bf16[512,7168]{0,1:T(8,128)(2,1)} async-done(((bf16[512,112]{0,1:T(8,128)(2,1)}), bf16[512,7168]{0,1:T(8,128)(2,1)}) %all-gather.5.cloned.1.call-update) | async-done | bytes 7340048 | tf_op jit(solution)/shard_map/all_gather | solution.py:88
  802.8 4.9 fusion.21
  807.8 12.3 %fusion.5 = f32[512,7168]{1,0:T(8,128)} fusion(bf16[144,7168]{1,0:T(8,128)(2,1)S(1)} %copy-done, bf16[7168,144]{0,1:T(8,128)(2,1)} %param.22, bf16[512,7168]{0,1:T(8,128)(2,1)} %all-gather.5.cloned.1.call-done, f32[512,144]{0,1:T(8,128)S(1)} %fusion.21), kind=kOutput, calls=%fused_computation.9 | convolution fusion | flops 2114371584 | bytes 26443776 | tf_op jit(solution)/shard_map/dot_general | solution.py:99
  820.1 1.2 constant_dynamic-slice_fusion
  821.6 1.8 add.80
  823.4 349.9 %reduce-scatter.2.cloned.1.call-done = f32[8,7168]{1,0:T(8,128)} async-done(((f32[512,7168]{1,0:T(8,128)}), f32[8,7168]{1,0:T(8,128)}) %reduce-scatter.2.cloned.1.call-update) | async-done | bytes 229392 | tf_op jit(solution)/shard_map/reduce_scatter | solution.py:98
  1173.3 1.6 convert_element_type.47
  (33 shorter events, 1.2 us)
Async XLA Ops:
  6.5 801.2 %copy-start = (bf16[144,7168]{1,0:T(8,128)(2,1)S(1)}, bf16[144,7168]{1,0:T(8,128)(2,1)}, u32[]{:S(2)}) copy-start(bf16[144,7168]{1,0:T(8,128)(2,1)} %param.23) | copy-start | bytes 6193156
  6.5 326.4 %all-gather.3.cloned.1.call-start = ((), (), s32[]{:S(2)}) async-start(), calls=%async_computation.2 | async-start | bytes 8519680 | tf_op jit(solution)/shard_map/all_gather | solution.py:79
  11.6 3.0 copy-start.1
  16.2 1.8 copy-start.2
  17.9 784.9 %all-gather.5.cloned.1.call-start = ((), (), s32[]{:S(2)}) async-start(), calls=%async_computation.3 | async-start | bytes 7454720 | tf_op jit(solution)/shard_map/all_gather | solution.py:88
  42.2 454.3 %copy-start.3 = (f32[112]{0:T(128)S(1)}, f32[112]{0:T(128)}, u32[]{:S(2)}) copy-start(f32[112]{0:T(128)} %param.20) | copy-start | bytes 1348
  497.3 676.0 %reduce-scatter.2.cloned.1.call-start = ((), (), s32[]{:S(2)}) async-start(), calls=%async_computation.4 | async-start | bytes 14909440 | tf_op jit(solution)/shard_map/reduce_scatter | solution.py:98
Sparse Core Ops, SparseCore 0:
  18.0 314.8 all-gather.2
  497.4 305.3 all-gather.4
  823.5 349.6 reduce-scatter.1
where the time goes:
time: 1180 us
  waiting for transfers between devices  946 us (80%)
  blocking collectives  181 us (15%)
  matrix products  25.8 us (2%)
  between operations  13.3 us (1%)
    reduce_scatter x1, waiting for transfers between devices, per_device(): lax.psum_scatter(jnp.dot(hidden_act, down_weight, preferred_element_type=...  350 us
    all_gather x1, waiting for transfers between devices, per_device(): shard_part = lax.all_gather(normed, 'dev', axis=1, tiled=True)  306 us
    all_gather x1, waiting for transfers between devices, per_device(): lax.all_gather(attended, 'dev', axis=0, tiled=True)  291 us
    psum x1, blocking collectives, per_device(): square_sums = lax.psum(jnp.sum(stream * stream, axis=1), 'dev')  157 us
    all_to_all x1, blocking collectives, per_device(): lax.all_to_all(hidden_in, 'dev', split_axis=1, concat_axis=0, tiled=True)  23.8 us
  transfers between devices with their start and end apart: 3, of which 3 were waited for; matrix products, arithmetic and copies ran while one was open for 0% of the time, Pallas kernels for 0%

commit v1 on v0

--- a/solution.py
+++ b/solution.py
@@ -1,7 +1,7 @@
 import jax
 import jax.numpy as jnp
 from jax import lax
-from jax.sharding import PartitionSpec as P
+from jax.sharding import Mesh, PartitionSpec as P
 
 norm_eps = 1e-05
 
@@ -57,6 +57,30 @@
     )
     mixed_vals = mixed_vals + (own_weight / denom_sum)[:, :, None] * new_vals[:, None, :]
     return mixed_vals.reshape(row_count, head_count * head_size).astype(jnp.bfloat16)
+
+
+def shifted(value, axis, step):
+    size = lax.axis_size(axis)
+    return lax.ppermute(value, axis, [(i, (i + step) % size) for i in range(size)])
+
+
+def halves(weight, core):
+    rows = weight.shape[0] // 2
+    mine = lax.dynamic_slice_in_dim(weight, core * rows, rows, 0)
+    other = lax.dynamic_slice_in_dim(weight, (1 - core) * rows, rows, 0)
+    return mine, other
+
+
+def spread(mine, other, pieces_for):
+    got = [jnp.concatenate([pieces_for(mine, 0), pieces_for(other, 0)], axis=0)]
+    for step in range(1, X):
+        near = shifted(pieces_for(mine, step), "x", step)
+        far = shifted(near, "pair", 1)
+        got.append(jnp.concatenate([near, far], axis=0))
+    return got
+
+
+X, Z, Y = 4, 8, 2
 
 
 def per_device(
@@ -73,56 +97,127 @@
     up_weight,
     down_weight,
 ):
+    f32, bf16 = jnp.float32, jnp.bfloat16
+    core, at_x, at_z, at_y = (lax.axis_index(a) for a in ("pair", "x", "z", "y"))
+    rows, width = hidden_in.shape
+    line = Z * Y
+    cols = width // (X * line)
+    chunk = rows * line
+    slab = width // X
+    ff = gate_weight.shape[1]
+
+    out_t = spread(*halves(out_weight.T, core), lambda w, step: w)
+
+    def slab_of(step):
+        begin = ((at_x + step) % X) * slab
+        return lambda w: lax.dynamic_slice_in_dim(w, begin, slab, 1)
+
+    gate_h, up_h = halves(gate_weight.T, core), halves(up_weight.T, core)
+    gate_up = spread(
+        (gate_h[0], up_h[0]),
+        (gate_h[1], up_h[1]),
+        lambda w, step: jnp.concatenate([slab_of(step)(w[0]), slab_of(step)(w[1])], axis=0),
+    )
+    down = spread(*halves(down_weight, core), lambda w, step: w)
+
     attended = attend(queries, new_kv, kv_cache, block_counts[0], tail_lens, block_order[0])
-    residual_cols = lax.all_to_all(hidden_in, "dev", split_axis=1, concat_axis=0, tiled=True)
-    projected = jnp.dot(
-        lax.all_gather(attended, "dev", axis=0, tiled=True),
-        out_weight,
-        preferred_element_type=jnp.float32,
-    )
-    stream = residual_cols.astype(jnp.float32) + projected
-    model_width = hidden_in.shape[1]
-    square_sums = lax.psum(jnp.sum(stream * stream, axis=1), "dev")
-    row_scale = lax.rsqrt(square_sums / model_width + norm_eps)
-    normed = (stream * row_scale[:, None] * norm_gain[None, :]).astype(jnp.bfloat16)
-    shard_part = lax.all_gather(normed, "dev", axis=1, tiled=True)
-    gate_proj = jnp.dot(shard_part, gate_weight, preferred_element_type=jnp.float32)
-    up_proj = jnp.dot(shard_part, up_weight, preferred_element_type=jnp.float32)
-    hidden_act = (jax.nn.silu(gate_proj) * up_proj).astype(jnp.bfloat16)
-    col_begin = lax.axis_index("dev") * stream.shape[1]
-    placed = lax.dynamic_update_slice(
-        jnp.zeros((lax.axis_size("dev") * hidden_in.shape[0], model_width), jnp.float32),
-        stream,
-        (jnp.int32(0), col_begin),
-    )
-    summed = lax.psum_scatter(
-        jnp.dot(hidden_act, down_weight, preferred_element_type=jnp.float32) + placed,
-        "dev",
-        scatter_dimension=0,
-        tiled=True,
-    )
-    finished = summed.astype(jnp.bfloat16)
-    return finished
+
+    resid = hidden_in.reshape(rows, X, line, cols)
+    resid = jnp.stack(
+        [lax.dynamic_index_in_dim(resid, (at_x - d) % X, 1, keepdims=False) for d in range(X)], axis=2
+    )
+    resid = jnp.pad(resid, ((0, 0), (0, 0), (0, 0), (0, 128 - cols)))
+    resid = resid.transpose(1, 0, 2, 3).reshape(line, rows, X * 128)
+    first = jnp.concatenate(
+        [jnp.broadcast_to(attended[None], (line,) + attended.shape), resid], axis=2
+    )
+    first = lax.all_to_all(first, ("z", "y"), 0, 0, tiled=True)
+    heads = first[:, :, : attended.shape[1]].reshape(chunk, attended.shape[1])
+    resid = first[:, :, attended.shape[1] :].reshape(chunk, X, 128)[:, :, :cols]
+    resid = resid.transpose(1, 2, 0).astype(f32)
+
+    proj = lax.dot_general(
+        jnp.concatenate(out_t, axis=0), heads, (((1,), (1,)), ((), ())), preferred_element_type=f32
+    ).reshape(X, 2, cols // 2, chunk)
+    proj = jnp.where(core == 0, proj, proj[:, ::-1]).reshape(X, cols, chunk)
+    part = proj + resid
+    stream = jnp.stack(
+        [part[0]] + [shifted(part[d], "x", -d) for d in range(1, X)], axis=1
+    ).reshape(cols, X * chunk)
+    squares = jnp.sum(stream * stream, axis=0)
+    high = squares.astype(bf16)
+    low = (squares - high.astype(f32)).astype(bf16)
+    scaled = (stream * norm_gain[:, None]).astype(bf16)
+    second = jnp.concatenate(
+        [scaled, high[None], low[None], jnp.zeros((6, X * chunk), bf16)], axis=0
+    )
+    second = lax.all_to_all(
+        jnp.broadcast_to(second[None], (line,) + second.shape), ("z", "y"), 0, 0, tiled=True
+    )
+    squares = jnp.sum(second[:, cols : cols + 2].astype(f32), axis=(0, 1))
+    scaled = second[:, :cols].reshape(slab, X * chunk)
+
+    halved = [
+        jnp.dot(w, scaled, preferred_element_type=f32) for w in gate_up
+    ]
+    total, square_total = 0.0, 0.0
+    for step in range(X):
+        here = slice(step * chunk, (step + 1) * chunk)
+        blocks = [halved[(d - step) % X][:, here] for d in range(X)]
+        sq = squares[here]
+        if step == 0:
+            total = jnp.concatenate(blocks, axis=0)
+            square_total = sq
+        else:
+            high = sq.astype(bf16)
+            low = (sq - high.astype(f32)).astype(bf16)
+            send = jnp.concatenate(
+                [b.astype(bf16) for b in blocks]
+                + [high[None], low[None], jnp.zeros((6, chunk), bf16)],
+                axis=0,
+            )
+            send = shifted(send, "x", step).astype(f32)
+            total = total + send[: X * 2 * ff]
+            square_total = square_total + send[X * 2 * ff] + send[X * 2 * ff + 1]
+    scale = lax.rsqrt(square_total / width + norm_eps)
+    total = (total * scale[None, :]).reshape(X * 2, 2, ff // 2, chunk)
+    hidden = (jax.nn.silu(total[:, 0]) * total[:, 1]).astype(bf16).reshape(X * ff, chunk)
+
+    spots = ((at_x - jnp.arange(X)) % X) * line + at_z * Y + at_y
+    spots = (spots[:, None] * cols + jnp.arange(cols)[None, :]).reshape(X * cols)
+    place = (spots[:, None] == jnp.arange(width)[None, :]).astype(bf16)
+    result = lax.dot_general(
+        jnp.concatenate([hidden, proj.reshape(X * cols, chunk).astype(bf16)], axis=0),
+        jnp.concatenate(down + [place], axis=0),
+        (((0,), (0,)), ((), ())),
+        preferred_element_type=f32,
+    ).astype(bf16)
+    result = lax.all_to_all(result.reshape(line, rows, width), ("z", "y"), 0, 0, tiled=True)
+    result = jnp.sum(result.astype(f32), axis=0) + hidden_in.astype(f32)
+    return result.astype(bf16)
 
 
 def solution(mesh):
+    fine = Mesh(mesh.devices.reshape(2, 2, X, Z, Y), ("role", "pair", "x", "z", "y"))
+    dev = ("x", "z", "y")
+    every = ("role", "pair") + dev
     return jax.shard_map(
         per_device,
-        mesh=mesh,
+        mesh=fine,
         in_specs=(
-            P(("role", "pair", "dev"), None),
-            P(("role", "pair", "dev"), None),
-            P(("role", "pair", "dev"), None),
-            P(("role", "pair", "dev"), None, None),
-            P(("role", "pair", "dev"), None),
-            P(("role", "pair", "dev")),
-            P(("role", "pair", "dev"), None),
-            P(None, "dev"),
-            P("dev"),
-            P(None, "dev"),
-            P(None, "dev"),
-            P("dev", None),
+            P(every, None),
+            P(every, None),
+            P(every, None),
+            P(every, None, None),
+            P(every, None),
+            P(every),
+            P(every, None),
+            P(None, dev),
+            P(dev),
+            P(None, dev),
+            P(None, dev),
+            P(dev, None),
         ),
-        out_specs=P(("role", "pair", "dev"), None),
+        out_specs=P(every, None),
         check_vma=False,
     )

time: 1180 us -> 270 us (0.23)
  waiting for transfers between devices: 946 us -> 88.7 us
  blocking collectives: 181 us -> 52 us
  starting transfers between devices: 0.09 us -> 42.6 us
  local copies, waits for them, and re-layouts: 7.33 us -> 45.6 us
  between operations: 13.3 us -> 0.62 us
    all_gather x2 -> x0, waiting for transfers between devices: 596 us -> none  [the longest x1 306 us: per_device(): shard_part = lax.all_gather(normed, 'dev', axis=1, tiled=True)]
    reduce_scatter x1 -> x0, waiting for transfers between devices: 350 us -> none  [per_device(): lax.psum_scatter(jnp.dot(hidden_act, down_weight, preferred_element_type=...]
    psum x1 -> x0, blocking collectives: 157 us -> none  [per_device(): square_sums = lax.psum(jnp.sum(stream * stream, axis=1), 'dev')]
    ppermute x0 -> x24, waiting for transfers between devices: none -> 59.6 us  [shifted(): lax.ppermute(value, axis, [(i, (i + step) % size) for i in range(size)])]
    all_to_all x0 -> x2, waiting for transfers between devices: none -> 29.1 us  [the longest x1 29.1 us: per_device(): lax.all_to_all(jnp.broadcast_to(second[None], (line,) + second.shape), ('...]
    all_to_all x1, blocking collectives: 23.8 us -> 52 us  [per_device(): lax.all_to_all(result.reshape(line, rows, width), ('z', 'y'), 0, 0, tiled...]
    unnamed x12 -> x47, local copies, waits for them, and re-layouts: 0.89 us -> 28.4 us
    ppermute x0 -> x24, starting transfers between devices: none -> 24 us  [shifted(): lax.ppermute(value, axis, [(i, (i + step) % size) for i in range(size)])]
  transfers between devices with their start and end apart: 3 -> 26, of which waited for: 3 -> 8; matrix products, arithmetic and copies ran while one was open for 0% -> 26% of each run, Pallas kernels for 0% -> 0%
where the time goes in v1:
time: 270 us
  waiting for transfers between devices  88.7 us (33%)
  blocking collectives  52 us (19%)
  local copies, waits for them, and re-layouts  45.6 us (17%)
  starting transfers between devices  42.6 us (16%)
  matrix products  24.7 us (9%)
  other arithmetic  15.2 us (6%)
    ppermute x24, waiting for transfers between devices, shifted(): lax.ppermute(value, axis, [(i, (i + step) % size) for i in range(size)])  59.6 us
    all_to_all x1, blocking collectives, per_device(): lax.all_to_all(result.reshape(line, rows, width), ('z', 'y'), 0, 0, tiled...  52 us
    all_to_all x1, waiting for transfers between devices, per_device(): lax.all_to_all(jnp.broadcast_to(second[None], (line,) + second.shape), ('...  29.1 us
    unnamed x47, local copies, waits for them, and re-layouts  28.4 us
    ppermute x24, starting transfers between devices, shifted(): lax.ppermute(value, axis, [(i, (i + step) % size) for i in range(size)])  24 us
    dot_general x4, matrix products, per_device(): halved = [jnp.dot(w, scaled, preferred_element_type=f32) for w in gate_up]  9.83 us
    all_to_all x1, starting transfers between devices, per_device(): first = lax.all_to_all(first, ('z', 'y'), 0, 0, tiled=True)  9.29 us
    all_to_all x1, starting transfers between devices, per_device(): lax.all_to_all(jnp.broadcast_to(second[None], (line,) + second.shape), ('...  9.29 us
  transfers between devices with their start and end apart: 26, of which 8 were waited for; matrix products, arithmetic and copies ran while one was open for 26% of the time, Pallas kernels for 0%

profile of v1, /device:TPU:16, one launch (start us, length us, event | category | flops | bytes accessed | tf_op | source)
XLA Modules:
  0.0 269.5 jit_solution(741164825586761471)
XLA Ops:
  0.0 2.5 constant_dynamic-update-slice_fusion.13
  4.0 2.7 %collective-permute-start.20 = (bf16[72,7168]{1,0:T(8,128)(2,1)S(1)}, bf16[72,7168]{1,0:T(8,128)(2,1)}, u32[]{:S(2)}, u32[]{:S(2)}) collective-permute-start(bf16[72,7168]{1,0:T(8,128)(2,1)S(1)} %get-tuple-element.10), channel_id=1, source_target_pairs={{0,32},{16,48},{32,0},{48,16},{1,33},{17,49},{33,1},{49,17},{2,34}... | collective-permute-start | bytes 3096584 | tf_op jit(solution)/shard_map/ppermute | solution.py:64
  6.7 2.6 constant_dynamic-update-slice_fusion.6
  9.4 2.9 %collective-permute-start.2 = (bf16[56,8192]{1,0:T(8,128)(2,1)}, bf16[56,8192]{1,0:T(8,128)(2,1)}, u32[]{:S(2)}, u32[]{:S(2)}) collective-permute-start(bf16[56,8192]{1,0:T(8,128)(2,1)} %get-tuple-element.8), channel_id=1, source_target_pairs={{0,32},{16,48},{32,0},{48,16},{1,33},{17,49},{33,1},{49,17},{2,34}... | collective-permute-start | bytes 2752520 | tf_op jit(solution)/shard_map/ppermute | solution.py:64
  13.7 3.9 %fusion.70 = (bf16[16,256,256]{2,1,0:T(8,128)(2,1)S(1)}, bf16[16,256,256]{2,1,0:T(8,128)(2,1)}) fusion(bf16[16,256,512]{2,1,0:T(8,128)(2,1)} %param.15), kind=kLoop, calls=%fused_computation.165 | loop fusion | bytes 8388608 | tf_op jit(solution)/shard_map/slice | solution.py:28
  24.8 9.3 %all-to-all-start = ((bf16[16,8,8704]{2,1,0:T(8,128)(2,1)}), bf16[16,8,8704]{2,1,0:T(8,128)(2,1)S(1)}, u32[]{:S(2)}, u32[]{:S(2)}) async-start(bf16[16,8,8704]{2,1,0:T(8,128)(2,1)} %pad_maximum_fusion), calls=%async_computation | async-start | bytes 4456448 | tf_op jit(solution)/shard_map/all_to_all | solution.py:134
  36.4 4.8 %dynamic-slice_bitcast_fusion.9 = (bf16[72,1792]{1,0:T(8,128)(2,1)}, bf16[72,1792]{1,0:T(8,128)(2,1)S(1)}, bf16[72,1792]{1,0:T(8,128)(2,1)}, bf16[72,1792]{1,0:T...) fusion(bf16[7168,144]{0,1:T(8,128)(2,1)} %param.22, ...), kind=kLoop, calls=%fused_computation.73 | loop fusion | bytes 5160984 | tf_op jit(solution)/shard_map/dynamic_slice | solution.py:113
  44.8 25.4 %collective-permute-done = bf16[56,8192]{1,0:T(8,128)(2,1)} collective-permute-done((bf16[56,8192]{1,0:T(8,128)(2,1)}, bf16[56,8192]{1,0:T(8,128)(2,1)}, u32[]{:S(2)}, u32[]{:S(2)}) %collective-permute-start) | collective-permute-done | bytes 917536 | tf_op jit(solution)/shard_map/ppermute | solution.py:64
  72.4 18.4 %collective-permute-done.2 = bf16[56,8192]{1,0:T(8,128)(2,1)} collective-permute-done((bf16[56,8192]{1,0:T(8,128)(2,1)}, bf16[56,8192]{1,0:T(8,128)(2,1)}, u32[]{:S(2)}, u32[]{:S(2)}) %collective-permute-start.2) | collective-permute-done | bytes 917536 | tf_op jit(solution)/shard_map/ppermute | solution.py:64
  98.8 5.8 %fusion.5 = f32[4,2,56,128]{3,2,1,0:T(8,128)} fusion(bf16[4,2,56,8192]{3,2,1,0:T(8,128)(2,1)} %bitcast.199, bf16[16,8,8704]{2,1,0:T(8,128)(2,1)S(1)} %all-to-all-done), kind=kOutput, calls=%fused_computation.13 | convolution fusion | flops 939524096 | bytes 9666560 | tf_op jit(solution)/shard_map/dot_general | solution.py:139
  111.4 2.7 %collective-permute-done.7 = f32[112,128]{1,0:T(8,128)S(1)} collective-permute-done((f32[112,128]{1,0:T(8,128)S(1)}, f32[112,128]{1,0:T(8,128)S(1)}, u32[]{:S(2)}, u32[]{:S(2)}) %collective-permute-start.7) | collective-permute-done | bytes 57376 | tf_op jit(solution)/shard_map/ppermute | solution.py:64
  114.1 4.8 %collective-permute-start.6 = (f32[112,128]{1,0:T(8,128)S(1)}, f32[112,128]{1,0:T(8,128)S(1)}, u32[]{:S(2)}, u32[]{:S(2)}) collective-permute-start(f32[112,128]{1,0:T(8,128)S(1)} %get-tuple-element.42), channel_id=1, source_target_pairs={{0,48},{16,0},{32,16},{48,32},{1,49},{17,1},{33,17},{49,33},{2,50}... | collective-permute-start | bytes 172040 | tf_op jit(solution)/shard_map/ppermute | solution.py:64
  127.5 9.3 %all-to-all-start.1 = ((bf16[16,120,512]{2,1,0:T(8,128)(2,1)}), bf16[16,120,512]{2,1,0:T(8,128)(2,1)S(1)}, u32[]{:S(2)}, u32[]{:S(2)}) async-start(bf16[16,120,512]{2,1,0:T(8,128)(2,1)} %broadcast_in_dim.59), calls=%async_computation.1 | async-start | bytes 3932160 | tf_op jit(solution)/shard_map/all_to_all | solution.py:154
  136.9 7.4 %collective-permute-done.13 = bf16[144,1792]{1,0:T(8,128)(2,1)} collective-permute-done((bf16[144,1792]{1,0:T(8,128)(2,1)}, bf16[144,1792]{1,0:T(8,128)(2,1)}, u32[]{:S(2)}, u32[]{:S(2)}) %collective-permute-start.13) | collective-permute-done | bytes 516128 | tf_op jit(solution)/shard_map/ppermute | solution.py:64
  147.6 2.3 constant_dynamic-update-slice_fusion.10
  154.3 29.1 %all-to-all-done.1 = bf16[16,120,512]{2,1,0:T(8,128)(2,1)S(1)} async-done(((bf16[16,120,512]{2,1,0:T(8,128)(2,1)}), bf16[16,120,512]{2,1,0:T(8,128)(2,1)S(1)}, u32[]{:S(2)}, u32[]{:S(2)}) %all-to-all-start.1) | async-done | bytes 1966112 | tf_op jit(solution)/shard_map/all_to_all | solution.py:154
  183.7 2.7 %fusion.80 = (bf16[288,512]{1,0:T(8,128)(2,1)S(1)}, f32[288,512]{1,0:T(8,128)}) fusion(bf16[1792,512]{1,0:T(8,128)(2,1)S(1)} %bitcast.188, bf16[144,1792]{1,0:T(8,128)(2,1)} %collective-permute-done.10, bf16[144,1792]{1,0:T(8,128)(2,1)} %copy-done.10), kind=kOutput, calls=%fused_computation.175 | convolution fusion | flops 530694144 | bytes 3751936 | tf_op jit(solution)/shard_map/dot_general | solution.py:161
  186.5 2.8 %fusion.77 = (bf16[288,512]{1,0:T(8,128)(2,1)S(1)}, f32[288,512]{1,0:T(8,128)}) fusion(bf16[1792,512]{1,0:T(8,128)(2,1)S(1)} %bitcast.189, bf16[144,1792]{1,0:T(8,128)(2,1)} %collective-permute-done.12, bf16[144,1792]{1,0:T(8,128)(2,1)} %collective-permute-done.11), kind=kOutput, calls=%fused_computation.172 | convolution fusion | flops 530694144 | bytes 3751936 | tf_op jit(solution)/shard_map/dot_general | solution.py:161
  189.3 2.8 %fusion.78 = (bf16[288,512]{1,0:T(8,128)(2,1)S(1)}, f32[288,512]{1,0:T(8,128)}) fusion(bf16[1792,512]{1,0:T(8,128)(2,1)S(1)} %bitcast.190, bf16[144,1792]{1,0:T(8,128)(2,1)} %collective-permute-done.14, bf16[144,1792]{1,0:T(8,128)(2,1)} %collective-permute-done.13), kind=kOutput, calls=%fused_computation.173 | convolution fusion | flops 530694144 | bytes 3751936 | tf_op jit(solution)/shard_map/dot_general | solution.py:161
  194.5 2.8 %collective-permute-start.16 = (bf16[1160,128]{1,0:T(8,128)(2,1)S(1)}, bf16[1160,128]{1,0:T(8,128)(2,1)S(1)}, u32[]{:S(2)}, u32[]{:S(2)}) collective-permute-start(bf16[1160,128]{1,0:T(8,128)(2,1)S(1)} %concatenate.60), channel_id=1, source_target_pairs={{0,32},{16,48},{32,0},{48,16},{1,33},{17,49},{33,1},{49,17},{2,34}... | collective-permute-start | bytes 890888 | tf_op jit(solution)/shard_map/ppermute | solution.py:64
  197.5 5.2 %fusion.2 = bf16[1024,7168]{1,0:T(8,128)(2,1)} fusion(bf16[1024,7168]{1,0:T(8,128)(2,1)} %constant_dynamic-update-slice_fusion.7, s32[448]{0:T(512)S(1)} %add.301), kind=kLoop, calls=%fused_computation.4 | loop fusion | flops 6422528 | bytes 6424320 | tf_op jit(solution)/shard_map/concatenate | solution.py:191
  206.5 2.4 collective-permute-done.15
  209.2 7.3 %fusion.1 = bf16[16,8,7168]{2,1,0:T(8,128)(2,1)S(1)} fusion(bf16[1024,7168]{1,0:T(8,128)(2,1)} %fusion.2, bf16[448,128]{1,0:T(8,128)(2,1)S(1)} %bitcast.197, bf16[576,128]{1,0:T(8,128)(2,1)S(1)} %fusion.31), kind=kOutput, calls=%fused_computation.3 | convolution fusion | flops 1880489984 | bytes 16777216 | tf_op jit(solution)/shard_map/dot_general | solution.py:189
  216.6 52.0 %all_to_all.15 = bf16[16,8,7168]{2,1,0:T(8,128)(2,1)S(1)} all-to-all(bf16[16,8,7168]{2,1,0:T(8,128)(2,1)S(1)} %fusion.1), channel_id=1, replica_groups=mesh['role'=2,'pair'=2,'x'=4,'z'=8,'y'=2] {'z','y'}, dimensions={0} | all-to-all | bytes 3670016 | tf_op jit(solution)/shard_map/all_to_all | solution.py:195
  (156 shorter events, 56.9 us)
Async XLA Ops:
  2.5 106.6 %collective-permute-start.18 = (bf16[72,7168]{1,0:T(8,128)(2,1)S(1)}, bf16[72,7168]{1,0:T(8,128)(2,1)}, u32[]{:S(2)}, u32[]{:S(2)}) collective-permute-start(bf16[72,7168]{1,0:T(8,128)(2,1)S(1)} %get-tuple-element.10), channel_id=1, source_target_pairs={{0,16},{16,32},{32,48},{48,0},{1,17},{17,33},{33,49},{49,1},{2,18}... | collective-permute-start | bytes 3096584 | tf_op jit(solution)/shard_map/ppermute | solution.py:64
  4.0 140.3 %collective-permute-start.20 = (bf16[72,7168]{1,0:T(8,128)(2,1)S(1)}, bf16[72,7168]{1,0:T(8,128)(2,1)}, u32[]{:S(2)}, u32[]{:S(2)}) collective-permute-start(bf16[72,7168]{1,0:T(8,128)(2,1)S(1)} %get-tuple-element.10), channel_id=1, source_target_pairs={{0,32},{16,48},{32,0},{48,16},{1,33},{17,49},{33,1},{49,17},{2,34}... | collective-permute-start | bytes 3096584 | tf_op jit(solution)/shard_map/ppermute | solution.py:64
  9.3 60.9 %collective-permute-start = (bf16[56,8192]{1,0:T(8,128)(2,1)}, bf16[56,8192]{1,0:T(8,128)(2,1)}, u32[]{:S(2)}, u32[]{:S(2)}) collective-permute-start(bf16[56,8192]{1,0:T(8,128)(2,1)} %get-tuple-element.8), channel_id=1, source_target_pairs={{0,16},{16,32},{32,48},{48,0},{1,17},{17,33},{33,49},{49,1},{2,18}... | collective-permute-start | bytes 2752520 | tf_op jit(solution)/shard_map/ppermute | solution.py:64
  9.4 81.5 %collective-permute-start.2 = (bf16[56,8192]{1,0:T(8,128)(2,1)}, bf16[56,8192]{1,0:T(8,128)(2,1)}, u32[]{:S(2)}, u32[]{:S(2)}) collective-permute-start(bf16[56,8192]{1,0:T(8,128)(2,1)} %get-tuple-element.8), channel_id=1, source_target_pairs={{0,32},{16,48},{32,0},{48,16},{1,33},{17,49},{33,1},{49,17},{2,34}... | collective-permute-start | bytes 2752520 | tf_op jit(solution)/shard_map/ppermute | solution.py:64
  12.2 78.6 %collective-permute-start.4 = (bf16[56,8192]{1,0:T(8,128)(2,1)}, bf16[56,8192]{1,0:T(8,128)(2,1)}, u32[]{:S(2)}, u32[]{:S(2)}) collective-permute-start(bf16[56,8192]{1,0:T(8,128)(2,1)} %get-tuple-element.8), channel_id=1, source_target_pairs={{0,48},{16,0},{32,16},{48,32},{1,49},{17,1},{33,17},{49,33},{2,50}... | collective-permute-start | bytes 2752520 | tf_op jit(solution)/shard_map/ppermute | solution.py:64
  24.8 73.9 %all-to-all-start = ((bf16[16,8,8704]{2,1,0:T(8,128)(2,1)}), bf16[16,8,8704]{2,1,0:T(8,128)(2,1)S(1)}, u32[]{:S(2)}, u32[]{:S(2)}) async-start(bf16[16,8,8704]{2,1,0:T(8,128)(2,1)} %pad_maximum_fusion), calls=%async_computation | async-start | bytes 4456448 | tf_op jit(solution)/shard_map/all_to_all | solution.py:134
  70.2 20.6 %collective-permute-start.1 = (bf16[56,8192]{1,0:T(8,128)(2,1)}, bf16[56,8192]{1,0:T(8,128)(2,1)S(1)}, u32[]{:S(2)}, u32[]{:S(2)}) collective-permute-start(bf16[56,8192]{1,0:T(8,128)(2,1)} %collective-permute-done), channel_id=1, source_target_pairs={{0,64},{64,0},{1,65},{65,1},{2,66},{66,2},{3,67},{67,3},{4,68},{68... | collective-permute-start | bytes 2752520 | tf_op jit(solution)/shard_map/ppermute | solution.py:64
  90.8 54.0 %collective-permute-start.22 = (bf16[72,7168]{1,0:T(8,128)(2,1)S(1)}, bf16[72,7168]{1,0:T(8,128)(2,1)}, u32[]{:S(2)}, u32[]{:S(2)}) collective-permute-start(bf16[72,7168]{1,0:T(8,128)(2,1)S(1)} %get-tuple-element.10), channel_id=1, source_target_pairs={{0,48},{16,0},{32,16},{48,32},{1,49},{17,1},{33,17},{49,33},{2,50}... | collective-permute-start | bytes 3096584 | tf_op jit(solution)/shard_map/ppermute | solution.py:64
  90.8 6.9 %collective-permute-start.5 = (bf16[56,8192]{1,0:T(8,128)(2,1)}, bf16[56,8192]{1,0:T(8,128)(2,1)S(1)}, u32[]{:S(2)}, u32[]{:S(2)}) collective-permute-start(bf16[56,8192]{1,0:T(8,128)(2,1)} %collective-permute-done.4), channel_id=1, source_target_pairs={{0,64},{64,0},{1,65},{65,1},{2,66},{66,2},{3,67},{67,3},{4,68},{68... | collective-permute-start | bytes 2752520 | tf_op jit(solution)/shard_map/ppermute | solution.py:64
  105.9 5.5 %collective-permute-start.8 = (f32[112,128]{1,0:T(8,128)S(1)}, f32[112,128]{1,0:T(8,128)S(1)}, u32[]{:S(2)}, u32[]{:S(2)}) collective-permute-start(f32[112,128]{1,0:T(8,128)S(1)} %get-tuple-element.40), channel_id=1, source_target_pairs={{0,16},{16,32},{32,48},{48,0},{1,17},{17,33},{33,49},{49,1},{2,18}... | collective-permute-start | bytes 172040 | tf_op jit(solution)/shard_map/ppermute | solution.py:64
  108.0 6.1 %collective-permute-start.7 = (f32[112,128]{1,0:T(8,128)S(1)}, f32[112,128]{1,0:T(8,128)S(1)}, u32[]{:S(2)}, u32[]{:S(2)}) collective-permute-start(f32[112,128]{1,0:T(8,128)S(1)} %get-tuple-element.41), channel_id=1, source_target_pairs={{0,32},{16,48},{32,0},{48,16},{1,33},{17,49},{33,1},{49,17},{2,34}... | collective-permute-start | bytes 172040 | tf_op jit(solution)/shard_map/ppermute | solution.py:64
  109.1 15.7 %collective-permute-start.9 = (bf16[144,1792]{1,0:T(8,128)(2,1)}, bf16[144,1792]{1,0:T(8,128)(2,1)S(1)}, u32[]{:S(2)}, u32[]{:S(2)}) collective-permute-start(bf16[144,1792]{1,0:T(8,128)(2,1)} %pad_maximum_fusion.1), channel_id=1, source_target_pairs={{0,16},{16,32},{32,48},{48,0},{1,17},{17,33},{33,49},{49,1},{2,18}... | collective-permute-start | bytes 1548296 | tf_op jit(solution)/shard_map/ppermute | solution.py:64
  111.4 33.5 %collective-permute-start.19 = (bf16[72,7168]{1,0:T(8,128)(2,1)}, bf16[72,7168]{1,0:T(8,128)(2,1)}, u32[]{:S(2)}, u32[]{:S(2)}) collective-permute-start(bf16[72,7168]{1,0:T(8,128)(2,1)} %collective-permute-done.18), channel_id=1, source_target_pairs={{0,64},{64,0},{1,65},{65,1},{2,66},{66,2},{3,67},{67,3},{4,68},{68... | collective-permute-start | bytes 3096584 | tf_op jit(solution)/shard_map/ppermute | solution.py:64
  114.1 7.0 %collective-permute-start.6 = (f32[112,128]{1,0:T(8,128)S(1)}, f32[112,128]{1,0:T(8,128)S(1)}, u32[]{:S(2)}, u32[]{:S(2)}) collective-permute-start(f32[112,128]{1,0:T(8,128)S(1)} %get-tuple-element.42), channel_id=1, source_target_pairs={{0,48},{16,0},{32,16},{48,32},{1,49},{17,1},{33,17},{49,33},{2,50}... | collective-permute-start | bytes 172040 | tf_op jit(solution)/shard_map/ppermute | solution.py:64
  121.2 15.6 %collective-permute-start.11 = (bf16[144,1792]{1,0:T(8,128)(2,1)}, bf16[144,1792]{1,0:T(8,128)(2,1)}, u32[]{:S(2)}, u32[]{:S(2)}) collective-permute-start(bf16[144,1792]{1,0:T(8,128)(2,1)} %pad_maximum_fusion.2), channel_id=1, source_target_pairs={{0,32},{16,48},{32,0},{48,16},{1,33},{17,49},{33,1},{49,17},{2,34}... | collective-permute-start | bytes 1548296 | tf_op jit(solution)/shard_map/ppermute | solution.py:64
  124.8 19.5 %collective-permute-start.13 = (bf16[144,1792]{1,0:T(8,128)(2,1)}, bf16[144,1792]{1,0:T(8,128)(2,1)}, u32[]{:S(2)}, u32[]{:S(2)}) collective-permute-start(bf16[144,1792]{1,0:T(8,128)(2,1)} %pad_maximum_fusion.3), channel_id=1, source_target_pairs={{0,48},{16,0},{32,16},{48,32},{1,49},{17,1},{33,17},{49,33},{2,50}... | collective-permute-start | bytes 1548296 | tf_op jit(solution)/shard_map/ppermute | solution.py:64
  127.5 55.9 %all-to-all-start.1 = ((bf16[16,120,512]{2,1,0:T(8,128)(2,1)}), bf16[16,120,512]{2,1,0:T(8,128)(2,1)S(1)}, u32[]{:S(2)}, u32[]{:S(2)}) async-start(bf16[16,120,512]{2,1,0:T(8,128)(2,1)} %broadcast_in_dim.59), calls=%async_computation.1 | async-start | bytes 3932160 | tf_op jit(solution)/shard_map/all_to_all | solution.py:154
  136.8 46.9 %collective-permute-start.10 = (bf16[144,1792]{1,0:T(8,128)(2,1)}, bf16[144,1792]{1,0:T(8,128)(2,1)}, u32[]{:S(2)}, u32[]{:S(2)}) collective-permute-start(bf16[144,1792]{1,0:T(8,128)(2,1)} %copy-done.10), channel_id=1, source_target_pairs={{0,64},{64,0},{1,65},{65,1},{2,66},{66,2},{3,67},{67,3},{4,68},{68... | collective-permute-start | bytes 1548296 | tf_op jit(solution)/shard_map/ppermute | solution.py:64
  144.3 42.2 %collective-permute-start.12 = (bf16[144,1792]{1,0:T(8,128)(2,1)}, bf16[144,1792]{1,0:T(8,128)(2,1)}, u32[]{:S(2)}, u32[]{:S(2)}) collective-permute-start(bf16[144,1792]{1,0:T(8,128)(2,1)} %collective-permute-done.11), channel_id=1, source_target_pairs={{0,64},{64,0},{1,65},{65,1},{2,66},{66,2},{3,67},{67,3},{4,68},{68... | collective-permute-start | bytes 1548296 | tf_op jit(solution)/shard_map/ppermute | solution.py:64
  144.3 45.0 %collective-permute-start.14 = (bf16[144,1792]{1,0:T(8,128)(2,1)}, bf16[144,1792]{1,0:T(8,128)(2,1)}, u32[]{:S(2)}, u32[]{:S(2)}) collective-permute-start(bf16[144,1792]{1,0:T(8,128)(2,1)} %collective-permute-done.13), channel_id=1, source_target_pairs={{0,64},{64,0},{1,65},{65,1},{2,66},{66,2},{3,67},{67,3},{4,68},{68... | collective-permute-start | bytes 1548296 | tf_op jit(solution)/shard_map/ppermute | solution.py:64
  144.9 8.3 %collective-permute-start.23 = (bf16[72,7168]{1,0:T(8,128)(2,1)}, bf16[72,7168]{1,0:T(8,128)(2,1)S(1)}, u32[]{:S(2)}, u32[]{:S(2)}) collective-permute-start(bf16[72,7168]{1,0:T(8,128)(2,1)} %collective-permute-done.22), channel_id=1, source_target_pairs={{0,64},{64,0},{1,65},{65,1},{2,66},{66,2},{3,67},{67,3},{4,68},{68... | collective-permute-start | bytes 3096584 | tf_op jit(solution)/shard_map/ppermute | solution.py:64
  193.9 12.5 %collective-permute-start.17 = (bf16[1160,128]{1,0:T(8,128)(2,1)S(1)}, bf16[1160,128]{1,0:T(8,128)(2,1)S(1)}, u32[]{:S(2)}, u32[]{:S(2)}) collective-permute-start(bf16[1160,128]{1,0:T(8,128)(2,1)S(1)} %concatenate.61), channel_id=1, source_target_pairs={{0,48},{16,0},{32,16},{48,32},{1,49},{17,1},{33,17},{49,33},{2,50}... | collective-permute-start | bytes 890888 | tf_op jit(solution)/shard_map/ppermute | solution.py:64
  194.5 11.9 %collective-permute-start.16 = (bf16[1160,128]{1,0:T(8,128)(2,1)S(1)}, bf16[1160,128]{1,0:T(8,128)(2,1)S(1)}, u32[]{:S(2)}, u32[]{:S(2)}) collective-permute-start(bf16[1160,128]{1,0:T(8,128)(2,1)S(1)} %concatenate.60), channel_id=1, source_target_pairs={{0,32},{16,48},{32,0},{48,16},{1,33},{17,49},{33,1},{49,17},{2,34}... | collective-permute-start | bytes 890888 | tf_op jit(solution)/shard_map/ppermute | solution.py:64
  197.4 11.5 %collective-permute-start.15 = (bf16[1160,128]{1,0:T(8,128)(2,1)S(1)}, bf16[1160,128]{1,0:T(8,128)(2,1)S(1)}, u32[]{:S(2)}, u32[]{:S(2)}) collective-permute-start(bf16[1160,128]{1,0:T(8,128)(2,1)S(1)} %concatenate.59), channel_id=1, source_target_pairs={{0,16},{16,32},{32,48},{48,0},{1,17},{17,33},{33,49},{49,1},{2,18}... | collective-permute-start | bytes 890888 | tf_op jit(solution)/shard_map/ppermute | solution.py:64
  (16 other events, 107.3 us)

commit v2 on v1

v2 whole, which is shorter than its diff:
```python
import jax
import jax.numpy as jnp
from jax import lax
from jax.experimental import pallas as pl
from jax.experimental.pallas import tpu as pltpu
from jax.sharding import Mesh, PartitionSpec as P

norm_eps = 1e-05
X, Z, Y = 4, 8, 2
LINE = Z * Y
f32, bf16 = jnp.float32, jnp.bfloat16
NT = (((1,), (1,)), ((), ()))
VMEM_LIMIT = 48 * 1024 * 1024


def smem():
    return pl.BlockSpec(memory_space=pltpu.SMEM)


def vmem():
    return pl.BlockSpec(memory_space=pltpu.VMEM)


def anywhere():
    return pl.BlockSpec(memory_space=pl.ANY)


def call(kernel, outs, ins, scratch, cost):
    single = not isinstance(outs, (list, tuple))
    return pl.pallas_call(
        kernel,
        out_shape=outs,
        in_specs=ins,
        out_specs=vmem() if single else [vmem()] * len(outs),
        scratch_shapes=scratch,
        compiler_params=pltpu.CompilerParams(vmem_limit_bytes=VMEM_LIMIT),
        cost_estimate=pl.CostEstimate(flops=cost[0], bytes_accessed=cost[1], transcendentals=0),
    )


def attend_kernel(counts, tails, order, q_ref, new_ref, kv_ref, out_ref, score, top, total, mixed):
    rows, heads, size = q_ref.shape
    pool, block, _ = kv_ref.shape
    scale = size ** (-0.5)
    owner, limit = [], []
    row, rank = jnp.int32(0), jnp.int32(0)
    for p in range(pool):
        last = rank + 1 == counts[0, row]
        owner.append(row)
        limit.append(jnp.where(last, tails[row], block))
        row = jnp.minimum(jnp.where(last, row + 1, row), rows - 1)
        rank = jnp.where(last, 0, rank + 1)
    own = []
    for r in range(rows):
        key = new_ref[r : r + 1, :size].astype(f32)
        own.append(jnp.sum(q_ref[r].astype(f32) * key, axis=1, keepdims=True) * scale)
        top[r] = jnp.broadcast_to(own[r], (heads, 128))
    lane = lax.broadcasted_iota(jnp.int32, (heads, block), 1)
    for p in range(pool):
        s = lax.dot_general(
            q_ref[owner[p]], kv_ref[order[0, p], :, :size], NT, preferred_element_type=f32
        )
        s = jnp.where(lane < limit[p], s * scale, -jnp.inf)
        score[p] = s
        top[owner[p]] = jnp.maximum(top[owner[p]], jnp.max(s, axis=1, keepdims=True))
    for r in range(rows):
        weight = jnp.exp(own[r] - top[r][:, :1])
        total[r] = jnp.broadcast_to(weight, (heads, 128))
        mixed[r] = weight * new_ref[r : r + 1, size:].astype(f32)
    for p in range(pool):
        weight = jnp.exp(score[p] - top[owner[p]][:, :1])
        total[owner[p]] += jnp.sum(weight, axis=1, keepdims=True)
        mixed[owner[p]] += jnp.dot(
            weight.astype(bf16), kv_ref[order[0, p], :, size:], preferred_element_type=f32
        )
    for r in range(rows):
        out_ref[r] = (mixed[r] / total[r][:, :1]).astype(bf16)


def attend(queries, new_kv, kv_cache, block_counts, tail_lens, block_order):
    rows = queries.shape[0]
    pool, block, twice = kv_cache.shape
    size = twice // 2
    heads = queries.shape[1] // size
    mixed = call(
        attend_kernel,
        jax.ShapeDtypeStruct((rows, heads, size), bf16),
        [smem()] * 3 + [vmem()] * 3,
        [
            pltpu.VMEM((pool, heads, block), f32),
            pltpu.VMEM((rows, heads, 128), f32),
            pltpu.VMEM((rows, heads, 128), f32),
            pltpu.VMEM((rows, heads, size), f32),
        ],
        (4 * pool * heads * block * size, pool * block * twice * 2),
    )(block_counts, tail_lens, block_order, queries.reshape(rows, heads, size), new_kv, kv_cache)
    return mixed.reshape(rows, heads * size)


def start_all(copies):
    for copy in copies:
        copy.start()
    return copies


def project_kernel(core, first, w0, w1, w2, w3, w4, w5, w6, proj_out, part_out, weight, sems):
    width = w0.shape[1]
    cols = w0.shape[0]
    half = width // 2
    mine = pl.multiple_of(core[0] * half, 128)
    other = pl.multiple_of((1 - core[0]) * half, 128)
    copies = [pltpu.make_async_copy(w0, weight.at[pl.ds(0, cols)], sems.at[0])]
    for d, (near, far) in enumerate(((w1, w2), (w3, w4), (w5, w6)), 1):
        rows = pl.ds(d * cols, cols)
        copies.append(
            pltpu.make_async_copy(near, weight.at[rows, pl.ds(mine, half)], sems.at[2 * d - 1])
        )
        copies.append(
            pltpu.make_async_copy(far, weight.at[rows, pl.ds(other, half)], sems.at[2 * d])
        )
    start_all(copies)
    for copy in copies:
        copy.wait()
    step = 1024

    def body(i, acc):
        at = pl.ds(pl.multiple_of(i * step, 128), step)
        return acc + lax.dot_general(weight[:, at], first[:, at], NT, preferred_element_type=f32)

    proj = lax.fori_loop(0, width // step, body, jnp.zeros((X * cols, first.shape[0]), f32))
    for d in range(X):
        here = proj[d * cols : (d + 1) * cols]
        proj_out[d] = here.astype(bf16)
        resid = first[:, width + d * 128 : width + (d + 1) * 128].astype(f32).T
        part_out[d] = here + resid[:cols]


def gate_up_kernel(
    place, second, gate, up, w1, w2, w3, w4, w5, w6, own_out, square_out, o1, o2, o3, weight, normed, sems
):
    ff = gate.shape[0]
    cols = normed.shape[0] // LINE
    slab = normed.shape[0]
    half = slab // 2
    chunk = normed.shape[1] // X
    mine = pl.multiple_of(place[0] * half, 128)
    other = pl.multiple_of((1 - place[0]) * half, 128)
    begin = pl.multiple_of(place[1] * slab, 128)
    copies = [
        pltpu.make_async_copy(gate.at[:, pl.ds(begin, slab)], weight.at[pl.ds(0, ff)], sems.at[0]),
        pltpu.make_async_copy(up.at[:, pl.ds(begin, slab)], weight.at[pl.ds(ff, ff)], sems.at[1]),
    ]
    for d, (near, far) in enumerate(((w1, w2), (w3, w4), (w5, w6)), 1):
        rows = pl.ds(d * 2 * ff, 2 * ff)
        copies.append(
            pltpu.make_async_copy(near, weight.at[rows, pl.ds(mine, half)], sems.at[2 * d])
        )
        copies.append(
            pltpu.make_async_copy(far, weight.at[rows, pl.ds(other, half)], sems.at[2 * d + 1])
        )
    for i in range(LINE):
        to = i % Z * Y + i // Z
        copies.append(
            pltpu.make_async_copy(
                second.at[i, pl.ds(0, cols)], normed.at[pl.ds(to * cols, cols)], sems.at[8 + i]
            )
        )
    start_all(copies)
    squares = jnp.sum(second[:, cols : cols + 8].astype(f32), axis=0)
    squares = squares[0:1] + squares[1:2]
    for copy in copies:
        copy.wait()
    outs = (own_out, o1, o2, o3)
    for d in range(X):
        rows = slice(d * 2 * ff, (d + 1) * 2 * ff)
        got = jnp.dot(weight[rows], normed[...], preferred_element_type=f32)
        for e in range(X):
            to = (d + e) % X
            outs[e][to * 2 * ff : (to + 1) * 2 * ff] = got[:, e * chunk : (e + 1) * chunk].astype(
                outs[e].dtype
            )
    square_out[...] = squares[:, :chunk]
    line = lax.broadcasted_iota(jnp.int32, (8, chunk), 0)
    for e in range(1, X):
        here = squares[:, e * chunk : (e + 1) * chunk]
        high = here.astype(bf16).astype(f32)
        both = jnp.where(line == 0, high, jnp.where(line == 1, here - high, 0.0))
        outs[e][X * 2 * ff :] = both.astype(bf16)


def down_kernel(
    place, own, square, r1, r2, r3, proj, w0, w1, w2, w3, w4, w5, w6, out, weight, total, sems
):
    ff, width = w0.shape
    half = width // 2
    chunk = out.shape[0]
    cols = proj.shape[1]
    mine = pl.multiple_of(place[0] * half, 128)
    other = pl.multiple_of((1 - place[0]) * half, 128)
    copies = [pltpu.make_async_copy(w0, weight.at[pl.ds(0, ff)], sems.at[0])]
    for d, (near, far) in enumerate(((w1, w2), (w3, w4), (w5, w6)), 1):
        rows = pl.ds(d * ff, ff)
        copies.append(
            pltpu.make_async_copy(near, weight.at[rows, pl.ds(mine, half)], sems.at[2 * d - 1])
        )
        copies.append(
            pltpu.make_async_copy(far, weight.at[rows, pl.ds(other, half)], sems.at[2 * d])
        )
    start_all(copies)
    end = X * 2 * ff
    squares = square[...]
    for r in (r1, r2, r3):
        tail = r[end:].astype(f32)
        squares = squares + tail[0:1] + tail[1:2]
    scale = lax.rsqrt(squares / width + norm_eps)
    hidden = []
    for d in range(X):
        at = d * 2 * ff
        gate, up = (
            (
                own[a : a + ff]
                + r1[a : a + ff].astype(f32)
                + r2[a : a + ff].astype(f32)
                + r3[a : a + ff].astype(f32)
            )
            * scale
            for a in (at, at + ff)
        )
        hidden.append((gate / (1.0 + jnp.exp(-gate)) * up).T.astype(bf16))
    hidden = jnp.concatenate(hidden, axis=1)
    for copy in copies:
        copy.wait()
    step = 1024

    def body(i, _):
        at = pl.ds(pl.multiple_of(i * step, 128), step)
        total[:, at] = jnp.dot(hidden, weight[:, at], preferred_element_type=f32)
        return 0

    lax.fori_loop(0, width // step, body, 0)
    row = lax.broadcasted_iota(jnp.int32, (cols, 256), 0)
    lane = lax.broadcasted_iota(jnp.int32, (cols, 256), 1)
    for d in range(X):
        spot = place[1 + d]
        base = jnp.minimum(spot // 128 * 128, width - 256)
        pick = (row + (spot - base) == lane).astype(bf16)
        at = pl.ds(pl.multiple_of(base, 128), 256)
        total[:, at] += lax.dot_general(
            proj[d], pick, (((0,), (0,)), ((), ())), preferred_element_type=f32
        )
    out[...] = total[...].astype(bf16)


def shifted(value, axis, step):
    size = lax.axis_size(axis)
    return lax.ppermute(value, axis, [(i, (i + step) % size) for i in range(size)])


def send_along_x(pieces):
    return [shifted(piece, "x", step) for step, piece in enumerate(pieces, 1)]


def with_other_core(near):
    both = []
    for piece in near:
        both += [piece, shifted(piece, "pair", 1)]
    return both


def after(values, *others):
    return lax.optimization_barrier((values, others))[0]


def per_device(
    hidden_in,
    queries,
    new_kv,
    kv_cache,
    block_counts,
    tail_lens,
    block_order,
    out_weight,
    norm_gain,
    gate_weight,
    up_weight,
    down_weight,
):
    core, at_x, at_z, at_y = (lax.axis_index(a) for a in ("pair", "x", "z", "y"))
    rows, width = hidden_in.shape
    cols = width // (X * LINE)
    chunk = rows * LINE
    slab = width // X
    ff = gate_weight.shape[1]
    heads_width = queries.shape[1]
    out_t, gate_t, up_t = out_weight.T, gate_weight.T, up_weight.T

    def lanes(weight, begin, size):
        return lax.dynamic_slice_in_dim(weight, begin, size, 1)

    piece = lanes(out_t, core * (heads_width // 2), heads_width // 2)
    out_near = send_along_x([piece] * (X - 1))

    attended = attend(queries, new_kv, kv_cache, block_counts, tail_lens, block_order)
    resid = hidden_in.reshape(rows, X, LINE, cols)
    resid = jnp.stack(
        [lax.dynamic_index_in_dim(resid, (at_x - d) % X, 1, keepdims=False) for d in range(X)], axis=2
    )
    resid = jnp.pad(resid, ((0, 0), (0, 0), (0, 0), (0, 128 - cols)))
    resid = resid.reshape(rows, Z, Y, X * 128).transpose(2, 1, 0, 3).reshape(LINE, rows, X * 128)
    first = jnp.concatenate(
        [jnp.broadcast_to(attended[None], (LINE,) + attended.shape), resid], axis=2
    )
    first = lax.all_to_all(first, ("y", "z"), 0, 0, tiled=True)
    first = first.reshape(chunk, heads_width + X * 128)

    gate_t, up_t = after((gate_t, up_t), out_near)
    pieces = []
    for step in range(1, X):
        begin = ((at_x + step) % X) * slab + core * (slab // 2)
        pieces.append(
            jnp.concatenate(
                [lanes(gate_t, begin, slab // 2), lanes(up_t, begin, slab // 2)], axis=0
            )
        )
    gate_up_near = send_along_x(pieces)
    down_weight = after(down_weight, gate_up_near)
    piece = lanes(down_weight, core * (width // 2), width // 2)
    down_near = send_along_x([piece] * (X - 1))

    proj, part = call(
        project_kernel,
        [
            jax.ShapeDtypeStruct((X, cols, chunk), bf16),
            jax.ShapeDtypeStruct((X, cols, chunk), f32),
        ],
        [smem(), vmem()] + [anywhere()] * 7,
        [pltpu.VMEM((X * cols, heads_width), bf16), pltpu.SemaphoreType.DMA((7,))],
        (2 * X * cols * chunk * heads_width, X * cols * heads_width * 4),
    )(core.reshape(1), first, out_t, *with_other_core(out_near))

    stream = jnp.stack(
        [part[0]] + [shifted(part[d], "x", -d) for d in range(1, X)], axis=1
    ).reshape(cols, X * chunk)
    squares = jnp.sum(stream * stream, axis=0)
    high = squares.astype(bf16)
    low = (squares - high.astype(f32)).astype(bf16)
    scaled = (stream * norm_gain[:, None]).astype(bf16)
    second = jnp.concatenate(
        [scaled, high[None], low[None], jnp.zeros((6, X * chunk), bf16)], axis=0
    )
    second = lax.all_to_all(
        jnp.broadcast_to(second[None], (LINE,) + second.shape), ("y", "z"), 0, 0, tiled=True
    )

    message = jax.ShapeDtypeStruct((X * 2 * ff + 8, chunk), bf16)
    own, square, *sends = call(
        gate_up_kernel,
        [
            jax.ShapeDtypeStruct((X * 2 * ff, chunk), f32),
            jax.ShapeDtypeStruct((1, chunk), f32),
            message,
            message,
            message,
        ],
        [smem(), vmem()] + [anywhere()] * 8,
        [
            pltpu.VMEM((X * 2 * ff, slab), bf16),
            pltpu.VMEM((slab, X * chunk), bf16),
            pltpu.SemaphoreType.DMA((8 + LINE,)),
        ],
        (4 * X * ff * slab * X * chunk, X * 2 * ff * slab * 4),
    )(jnp.stack([core, at_x]), second, gate_t, up_t, *with_other_core(gate_up_near))
    received = send_along_x(sends)

    spots = [(((at_x - d) % X) * LINE + at_z * Y + at_y) * cols for d in range(X)]
    result = call(
        down_kernel,
        jax.ShapeDtypeStruct((chunk, width), bf16),
        [smem()] + [vmem()] * 6 + [anywhere()] * 7,
        [
            pltpu.VMEM((X * ff, width), bf16),
            pltpu.VMEM((chunk, width), f32),
            pltpu.SemaphoreType.DMA((7,)),
        ],
        (2 * X * ff * chunk * width, X * ff * width * 4),
    )(
        jnp.stack([core] + spots),
        own,
        square,
        *received,
        proj,
        down_weight,
        *with_other_core(down_near),
    )
    result = lax.all_to_all(result.reshape(LINE, rows, width), ("y", "z"), 0, 0, tiled=True)
    result = jnp.sum(result.astype(f32), axis=0) + hidden_in.astype(f32)
    return result.astype(bf16)


def solution(mesh):
    fine = Mesh(mesh.devices.reshape(2, 2, X, Z, Y), ("role", "pair", "x", "z", "y"))
    dev = ("x", "z", "y")
    every = ("role", "pair") + dev
    return jax.shard_map(
        per_device,
        mesh=fine,
        in_specs=(
            P(every, None),
            P(every, None),
            P(every, None),
            P(every, None, None),
            P(every, None),
            P(every),
            P(every, None),
            P(None, dev),
            P(dev),
            P(None, dev),
            P(None, dev),
            P(dev, None),
        ),
        out_specs=P(every, None),
        check_vma=False,
    )
```

time: 270 us -> 275 us (1.019)
  waiting for transfers between devices: 88.7 us -> 128 us
  matrix products: 24.7 us -> 0 us
  Pallas kernels: 0 us -> 24.1 us
  local copies, waits for them, and re-layouts: 45.6 us -> 24.9 us
  other arithmetic: 15.2 us -> 5.3 us
    ppermute x24, waiting for transfers between devices: 59.6 us -> 124 us  [shifted(): lax.ppermute(value, axis, [(i, (i + step) % size) for i in range(size)])]
    all_to_all x2, waiting for transfers between devices: 29.1 us -> 3.58 us  [the longest x1 3.58 us: per_device(): first = lax.all_to_all(first, ('y', 'z'), 0, 0, tiled=True)]
    dot_general x8 -> x0, matrix products: 24.7 us -> none  [the longest x4 9.83 us: per_device(): halved = [jnp.dot(w, scaled, preferred_element_type=f32) for w in gate_up]]
    pallas_call x0 -> x4, Pallas kernels: none -> 24.1 us  [the longest x1 7.96 us: per_device(): call(down_kernel, jax.ShapeDtypeStruct((chunk, width), bf16), [smem()] +...]
    unnamed x47 -> x57, local copies, waits for them, and re-layouts: 28.4 us -> 20.1 us
    slice x13 -> x0, local copies, waits for them, and re-layouts: 8.02 us -> none  [the longest x1 3.93 us: attend(): kv_cache[:, :, :head_size].reshape(pool_size * block_len, head_size)]
    concatenate x5 -> x4, other arithmetic: 9.22 us -> 4.05 us  [the longest x3 2.51 us: per_device(): jnp.concatenate([lanes(gate_t, begin, slab // 2), lanes(up_t, begin, slab...]
    all_to_all x2, starting transfers between devices: 18.6 us -> 15.3 us  [the longest x1 9.47 us: per_device(): first = lax.all_to_all(first, ('y', 'z'), 0, 0, tiled=True)]
  transfers between devices with their start and end apart: 26 -> 26, of which waited for: 8 -> 15; matrix products, arithmetic and copies ran while one was open for 26% -> 2% of each run, Pallas kernels for 0% -> 3%
where the time goes in v2:
time: 275 us; the launch traced here: 274 us
  waiting for transfers between devices  128 us (47%)
  blocking collectives  51 us (19%)
  starting transfers between devices  40.1 us (15%)
  local copies, waits for them, and re-layouts  24.9 us (9%)
  Pallas kernels  24.1 us (9%)
  other arithmetic  5.3 us (2%)
    ppermute x24, waiting for transfers between devices, shifted(): lax.ppermute(value, axis, [(i, (i + step) % size) for i in range(size)])  124 us
    all_to_all x1, blocking collectives, per_device(): lax.all_to_all(result.reshape(LINE, rows, width), ('y', 'z'), 0, 0, tiled...  51 us
    ppermute x24, starting transfers between devices, shifted(): lax.ppermute(value, axis, [(i, (i + step) % size) for i in range(size)])  24.8 us
    unnamed x57, local copies, waits for them, and re-layouts  20.1 us
    all_to_all x1, starting transfers between devices, per_device(): first = lax.all_to_all(first, ('y', 'z'), 0, 0, tiled=True)  9.47 us
    pallas_call x1, Pallas kernels, per_device(): call(down_kernel, jax.ShapeDtypeStruct((chunk, width), bf16), [smem()] +...  7.96 us
    pallas_call x1, Pallas kernels, per_device(): call(gate_up_kernel, [jax.ShapeDtypeStruct((X * 2 * ff, chunk), f32), jax...  7.63 us
    pallas_call x1, Pallas kernels, per_device(): call(project_kernel, [jax.ShapeDtypeStruct((X, cols, chunk), bf16), jax.S...  6.55 us
  transfers between devices with their start and end apart: 26, of which 15 were waited for; matrix products, arithmetic and copies ran while one was open for 2% of the time, Pallas kernels for 3%

profile of v2, /device:TPU:16, one launch (start us, length us, event | category | flops | bytes accessed | tf_op | source)
XLA Modules:
  0.0 273.8 jit_solution(439342773671820601)
XLA Ops:
  2.6 2.2 copy-done
  4.7 2.0 shard_map.118
  8.6 9.5 %all-to-all-start = ((bf16[16,8,8704]{2,1,0:T(8,128)(2,1)}), bf16[16,8,8704]{2,1,0:T(8,128)(2,1)}, u32[]{:S(2)}, u32[]{:S(2)}) async-start(bf16[16,8,8704]{2,1,0:T(8,128)(2,1)} %pad_maximum_fusion), calls=%async_computation | async-start | bytes 4456448 | tf_op jit(solution)/shard_map/all_to_all | solution.py:313
  19.7 2.7 collective-permute-start.2
  23.9 17.8 %collective-permute-done.w1 = bf16[112,4096]{1,0:T(8,128)(2,1)S(1)} collective-permute-done((bf16[112,4096]{1,0:T(8,128)(2,1)S(1)}, bf16[112,4096]{1,0:T(8,128)(2,1)S(1)}, u32[]{:S(2)}, u32[]{:S(2)}) %collective-permute-start) | collective-permute-done | bytes 917536 | tf_op jit(solution)/shard_map/ppermute | solution.py:256
  41.7 20.2 %collective-permute-done.2.w3 = bf16[112,4096]{1,0:T(8,128)(2,1)S(1)} collective-permute-done((bf16[112,4096]{1,0:T(8,128)(2,1)S(1)}, bf16[112,4096]{1,0:T(8,128)(2,1)S(1)}, u32[]{:S(2)}, u32[]{:S(2)}) %collective-permute-start.2) | collective-permute-done | bytes 917536 | tf_op jit(solution)/shard_map/ppermute | solution.py:256
  66.6 3.6 %all-to-all-done = bf16[16,8,8704]{2,1,0:T(8,128)(2,1)} async-done(((bf16[16,8,8704]{2,1,0:T(8,128)(2,1)}), bf16[16,8,8704]{2,1,0:T(8,128)(2,1)}, u32[]{:S(2)}, u32[]{:S(2)}) %all-to-all-start) | async-done | bytes 2228256 | tf_op jit(solution)/shard_map/all_to_all | solution.py:313
  73.7 6.6 %shard_map.119 = (bf16[4,112,128]{2,1,0:T(8,128)(2,1)S(1)}, f32[4,112,128]{2,1,0:T(8,128)S(1)}) custom-call(s32[1]{0:T(128)} %bitcast.core, bf16[128,8704]{1,0:T(8,128)(2,1)} %bitcast.12.first, bf16[112,8192]{1,0:T(8,128)(2,1)} %bitcast.52, bf16[112,4096]{1,0:T(8,128)(2,1)S(1)} %collective-permute-done.w1, bf16[112,4096]{1,0:T(8,128)(2,1)S(1)} %copy-done.2, ...), custom_call_target="tpu_custom_call" | custom-call | flops 939524096 | bytes 14680064 | tf_op jit(solution)/shard_map/pallas_call | solution.py:330
  81.9 2.5 collective-permute-start.7
  84.4 1.6 collective-permute-start.6
  90.2 5.8 %all-to-all-start.1 = ((bf16[16,120,512]{2,1,0:T(8,128)(2,1)}), bf16[16,120,512]{2,1,0:T(8,128)(2,1)}, u32[]{:S(2)}, u32[]{:S(2)}) async-start(bf16[16,120,512]{2,1,0:T(8,128)(2,1)} %broadcast_in_dim.22), calls=%async_computation.1 | async-start | bytes 3932160 | tf_op jit(solution)/shard_map/all_to_all | solution.py:351
  96.1 1.6 constant_dynamic-slice_fusion.1
  100.1 3.6 %collective-permute-start.11 = (bf16[288,896]{1,0:T(8,128)(2,1)}, bf16[288,896]{1,0:T(8,128)(2,1)S(1)}, u32[]{:S(2)}, u32[]{:S(2)}) collective-permute-start(bf16[288,896]{1,0:T(8,128)(2,1)} %pad_maximum_fusion.2), channel_id=1, source_target_pairs={{0,32},{16,48},{32,0},{48,16},{1,33},{17,49},{33,1},{49,17},{2,34}... | collective-permute-start | bytes 1548296 | tf_op jit(solution)/shard_map/ppermute | solution.py:256
  104.6 9.9 %collective-permute-done.9.w1 = bf16[288,896]{1,0:T(8,128)(2,1)} collective-permute-done((bf16[288,896]{1,0:T(8,128)(2,1)}, bf16[288,896]{1,0:T(8,128)(2,1)}, u32[]{:S(2)}, u32[]{:S(2)}) %collective-permute-start.9) | collective-permute-done | bytes 516128 | tf_op jit(solution)/shard_map/ppermute | solution.py:256
  114.4 9.5 %collective-permute-done.11.w3 = bf16[288,896]{1,0:T(8,128)(2,1)S(1)} collective-permute-done((bf16[288,896]{1,0:T(8,128)(2,1)}, bf16[288,896]{1,0:T(8,128)(2,1)S(1)}, u32[]{:S(2)}, u32[]{:S(2)}) %collective-permute-start.11) | collective-permute-done | bytes 516128 | tf_op jit(solution)/shard_map/ppermute | solution.py:256
  126.7 3.3 %collective-permute-start.20 = (bf16[144,3584]{1,0:T(8,128)(2,1)S(1)}, bf16[144,3584]{1,0:T(8,128)(2,1)S(1)}, u32[]{:S(2)}, u32[]{:S(2)}) collective-permute-start(bf16[144,3584]{1,0:T(8,128)(2,1)S(1)} %constant_dynamic-slice_fusion), channel_id=1, source_target_pairs={{0,32},{16,48},{32,0},{48,16},{1,33},{17,49},{33,1},{49,17},{2,34}... | collective-permute-start | bytes 3096584 | tf_op jit(solution)/shard_map/ppermute | solution.py:256
  130.0 21.6 %collective-permute-done.18.w1 = bf16[144,3584]{1,0:T(8,128)(2,1)S(1)} collective-permute-done((bf16[144,3584]{1,0:T(8,128)(2,1)S(1)}, bf16[144,3584]{1,0:T(8,128)(2,1)S(1)}, u32[]{:S(2)}, u32[]{:S(2)}) %collective-permute-start.18) | collective-permute-done | bytes 1032224 | tf_op jit(solution)/shard_map/ppermute | solution.py:256
  151.6 23.3 %collective-permute-done.20.w3 = bf16[144,3584]{1,0:T(8,128)(2,1)S(1)} collective-permute-done((bf16[144,3584]{1,0:T(8,128)(2,1)S(1)}, bf16[144,3584]{1,0:T(8,128)(2,1)S(1)}, u32[]{:S(2)}, u32[]{:S(2)}) %collective-permute-start.20) | collective-permute-done | bytes 1032224 | tf_op jit(solution)/shard_map/ppermute | solution.py:256
  176.8 3.2 %collective-permute-done.12.w4 = bf16[288,896]{1,0:T(8,128)(2,1)S(1)} collective-permute-done((bf16[288,896]{1,0:T(8,128)(2,1)}, bf16[288,896]{1,0:T(8,128)(2,1)S(1)}, u32[]{:S(2)}, u32[]{:S(2)}) %collective-permute-start.12) | collective-permute-done | bytes 516128 | tf_op jit(solution)/shard_map/ppermute | solution.py:256
  186.7 7.6 %shard_map.120 = (f32[1152,128]{1,0:T(8,128)S(1)}, f32[1,128]{1,0:T(1,128)S(1)}, bf16[1160,128]{1,0:T(8,128)(2,1)}, bf16[1160,128]{1,0:T(8,128)(2,1)}, bf16[1160,128]{1,0:T(8,128)(2,1)}) custom-call(s32[2]{0:T(128)S(1)} %pad_add_fusion.place, bf16[16,120,512]{2,1,0:T(8,128)(2,1)} %all-to-all-done.1.second, bf16[144,7168]{1,0:T(8,128)(2,1)} %bitcast.54, ...), custom_call_target="tpu_custom_call" | custom-call | flops 2113929216 | bytes 8257536 | tf_op jit(solution)/shard_map/pallas_call | solution.py:356
  195.2 2.2 collective-permute-start.16
  198.5 13.5 %collective-permute-done.15.r1 = bf16[1160,128]{1,0:T(8,128)(2,1)S(1)} collective-permute-done((bf16[1160,128]{1,0:T(8,128)(2,1)}, bf16[1160,128]{1,0:T(8,128)(2,1)S(1)}, u32[]{:S(2)}, u32[]{:S(2)}) %collective-permute-start.15) | collective-permute-done | bytes 296992 | tf_op jit(solution)/shard_map/ppermute | solution.py:256
  213.8 8.0 %shard_map.121 = bf16[128,7168]{1,0:T(8,128)(2,1)} custom-call(s32[5]{0:T(128)S(1)} %stack.57.place, f32[1152,128]{1,0:T(8,128)S(1)} %copy-done.8, f32[1,128]{1,0:T(1,128)S(1)} %get-tuple-element.19.square, bf16[1160,128]{1,0:T(8,128)(2,1)S(1)} %collective-permute-done.15.r1, bf16[1160,128]{1,0:T(8,128)(2,1)} %collective-permute-done.16.r2, ...), custom_call_target="tpu_custom_call" | custom-call | flops 1056964608 | bytes 16515072 | tf_op jit(solution)/shard_map/pallas_call | solution.py:376
  221.8 51.0 %all_to_all.15 = bf16[16,8,7168]{2,1,0:T(8,128)(2,1)S(1)} all-to-all(bf16[16,8,7168]{2,1,0:T(8,128)(2,1)} %bitcast.51), channel_id=1, replica_groups=mesh['role'=2,'pair'=2,'x'=4,'z'=8,'y'=2] {'y','z'}, dimensions={0} | all-to-all | bytes 3670016 | tf_op jit(solution)/shard_map/all_to_all | solution.py:395
  (117 shorter events, 40.6 us)
Async XLA Ops:
  8.6 61.6 %all-to-all-start = ((bf16[16,8,8704]{2,1,0:T(8,128)(2,1)}), bf16[16,8,8704]{2,1,0:T(8,128)(2,1)}, u32[]{:S(2)}, u32[]{:S(2)}) async-start(bf16[16,8,8704]{2,1,0:T(8,128)(2,1)} %pad_maximum_fusion), calls=%async_computation | async-start | bytes 4456448 | tf_op jit(solution)/shard_map/all_to_all | solution.py:313
  18.1 23.6 %collective-permute-start = (bf16[112,4096]{1,0:T(8,128)(2,1)S(1)}, bf16[112,4096]{1,0:T(8,128)(2,1)S(1)}, u32[]{:S(2)}, u32[]{:S(2)}) collective-permute-start(bf16[112,4096]{1,0:T(8,128)(2,1)S(1)} %dynamic-slice_bitcast_fusion), channel_id=1, source_target_pairs={{0,16},{16,32},{32,48},{48,0},{1,17},{17,33},{33,49},{49,1},{2,18}... | collective-permute-start | bytes 2752520 | tf_op jit(solution)/shard_map/ppermute | solution.py:256
  19.7 42.2 %collective-permute-start.2 = (bf16[112,4096]{1,0:T(8,128)(2,1)S(1)}, bf16[112,4096]{1,0:T(8,128)(2,1)S(1)}, u32[]{:S(2)}, u32[]{:S(2)}) collective-permute-start(bf16[112,4096]{1,0:T(8,128)(2,1)S(1)} %dynamic-slice_bitcast_fusion), channel_id=1, source_target_pairs={{0,32},{16,48},{32,0},{48,16},{1,33},{17,49},{33,1},{49,17},{2,34}... | collective-permute-start | bytes 2752520 | tf_op jit(solution)/shard_map/ppermute | solution.py:256
  22.4 39.5 %collective-permute-start.4 = (bf16[112,4096]{1,0:T(8,128)(2,1)S(1)}, bf16[112,4096]{1,0:T(8,128)(2,1)S(1)}, u32[]{:S(2)}, u32[]{:S(2)}) collective-permute-start(bf16[112,4096]{1,0:T(8,128)(2,1)S(1)} %dynamic-slice_bitcast_fusion), channel_id=1, source_target_pairs={{0,48},{16,0},{32,16},{48,32},{1,49},{17,1},{33,17},{49,33},{2,50}... | collective-permute-start | bytes 2752520 | tf_op jit(solution)/shard_map/ppermute | solution.py:256
  41.7 20.7 %collective-permute-start.1 = (bf16[112,4096]{1,0:T(8,128)(2,1)S(1)}, bf16[112,4096]{1,0:T(8,128)(2,1)S(1)}, u32[]{:S(2)}, u32[]{:S(2)}) collective-permute-start(bf16[112,4096]{1,0:T(8,128)(2,1)S(1)} %collective-permute-done.w1), channel_id=1, source_target_pairs={{0,64},{64,0},{1,65},{65,1},{2,66},{66,2},{3,67},{67,3},{4,68},{68... | collective-permute-start | bytes 2752520 | tf_op jit(solution)/shard_map/ppermute | solution.py:256
  80.3 5.8 %collective-permute-start.8 = (f32[112,128]{1,0:T(8,128)S(1)}, f32[112,128]{1,0:T(8,128)S(1)}, u32[]{:S(2)}, u32[]{:S(2)}) collective-permute-start(f32[112,128]{1,0:T(8,128)S(1)} %get-tuple-element.34), channel_id=1, source_target_pairs={{0,16},{16,32},{32,48},{48,0},{1,17},{17,33},{33,49},{49,1},{2,18}... | collective-permute-start | bytes 172040 | tf_op jit(solution)/shard_map/ppermute | solution.py:256
  81.9 5.7 %collective-permute-start.7 = (f32[112,128]{1,0:T(8,128)S(1)}, f32[112,128]{1,0:T(8,128)S(1)}, u32[]{:S(2)}, u32[]{:S(2)}) collective-permute-start(f32[112,128]{1,0:T(8,128)S(1)} %get-tuple-element.35), channel_id=1, source_target_pairs={{0,32},{16,48},{32,0},{48,16},{1,33},{17,49},{33,1},{49,17},{2,34}... | collective-permute-start | bytes 172040 | tf_op jit(solution)/shard_map/ppermute | solution.py:256
  84.4 4.2 %collective-permute-start.6 = (f32[112,128]{1,0:T(8,128)S(1)}, f32[112,128]{1,0:T(8,128)S(1)}, u32[]{:S(2)}, u32[]{:S(2)}) collective-permute-start(f32[112,128]{1,0:T(8,128)S(1)} %get-tuple-element.36), channel_id=1, source_target_pairs={{0,48},{16,0},{32,16},{48,32},{1,49},{17,1},{33,17},{49,33},{2,50}... | collective-permute-start | bytes 172040 | tf_op jit(solution)/shard_map/ppermute | solution.py:256
  90.2 91.3 %all-to-all-start.1 = ((bf16[16,120,512]{2,1,0:T(8,128)(2,1)}), bf16[16,120,512]{2,1,0:T(8,128)(2,1)}, u32[]{:S(2)}, u32[]{:S(2)}) async-start(bf16[16,120,512]{2,1,0:T(8,128)(2,1)} %broadcast_in_dim.22), calls=%async_computation.1 | async-start | bytes 3932160 | tf_op jit(solution)/shard_map/all_to_all | solution.py:351
  98.6 15.8 %collective-permute-start.9 = (bf16[288,896]{1,0:T(8,128)(2,1)}, bf16[288,896]{1,0:T(8,128)(2,1)}, u32[]{:S(2)}, u32[]{:S(2)}) collective-permute-start(bf16[288,896]{1,0:T(8,128)(2,1)} %pad_maximum_fusion.1), channel_id=1, source_target_pairs={{0,16},{16,32},{32,48},{48,0},{1,17},{17,33},{33,49},{49,1},{2,18}... | collective-permute-start | bytes 1548296 | tf_op jit(solution)/shard_map/ppermute | solution.py:256
  100.1 23.8 %collective-permute-start.11 = (bf16[288,896]{1,0:T(8,128)(2,1)}, bf16[288,896]{1,0:T(8,128)(2,1)S(1)}, u32[]{:S(2)}, u32[]{:S(2)}) collective-permute-start(bf16[288,896]{1,0:T(8,128)(2,1)} %pad_maximum_fusion.2), channel_id=1, source_target_pairs={{0,32},{16,48},{32,0},{48,16},{1,33},{17,49},{33,1},{49,17},{2,34}... | collective-permute-start | bytes 1548296 | tf_op jit(solution)/shard_map/ppermute | solution.py:256
  104.6 20.1 %collective-permute-start.13 = (bf16[288,896]{1,0:T(8,128)(2,1)}, bf16[288,896]{1,0:T(8,128)(2,1)S(1)}, u32[]{:S(2)}, u32[]{:S(2)}) collective-permute-start(bf16[288,896]{1,0:T(8,128)(2,1)} %pad_maximum_fusion.3), channel_id=1, source_target_pairs={{0,48},{16,0},{32,16},{48,32},{1,49},{17,1},{33,17},{49,33},{2,50}... | collective-permute-start | bytes 1548296 | tf_op jit(solution)/shard_map/ppermute | solution.py:256
  125.7 25.9 %collective-permute-start.18 = (bf16[144,3584]{1,0:T(8,128)(2,1)S(1)}, bf16[144,3584]{1,0:T(8,128)(2,1)S(1)}, u32[]{:S(2)}, u32[]{:S(2)}) collective-permute-start(bf16[144,3584]{1,0:T(8,128)(2,1)S(1)} %constant_dynamic-slice_fusion), channel_id=1, source_target_pairs={{0,16},{16,32},{32,48},{48,0},{1,17},{17,33},{33,49},{49,1},{2,18}... | collective-permute-start | bytes 3096584 | tf_op jit(solution)/shard_map/ppermute | solution.py:256
  126.7 48.2 %collective-permute-start.20 = (bf16[144,3584]{1,0:T(8,128)(2,1)S(1)}, bf16[144,3584]{1,0:T(8,128)(2,1)S(1)}, u32[]{:S(2)}, u32[]{:S(2)}) collective-permute-start(bf16[144,3584]{1,0:T(8,128)(2,1)S(1)} %constant_dynamic-slice_fusion), channel_id=1, source_target_pairs={{0,32},{16,48},{32,0},{48,16},{1,33},{17,49},{33,1},{49,17},{2,34}... | collective-permute-start | bytes 3096584 | tf_op jit(solution)/shard_map/ppermute | solution.py:256
  129.9 44.9 %collective-permute-start.22 = (bf16[144,3584]{1,0:T(8,128)(2,1)S(1)}, bf16[144,3584]{1,0:T(8,128)(2,1)}, u32[]{:S(2)}, u32[]{:S(2)}) collective-permute-start(bf16[144,3584]{1,0:T(8,128)(2,1)S(1)} %constant_dynamic-slice_fusion), channel_id=1, source_target_pairs={{0,48},{16,0},{32,16},{48,32},{1,49},{17,1},{33,17},{49,33},{2,50}... | collective-permute-start | bytes 3096584 | tf_op jit(solution)/shard_map/ppermute | solution.py:256
  130.0 45.4 %collective-permute-start.10 = (bf16[288,896]{1,0:T(8,128)(2,1)}, bf16[288,896]{1,0:T(8,128)(2,1)S(1)}, u32[]{:S(2)}, u32[]{:S(2)}) collective-permute-start(bf16[288,896]{1,0:T(8,128)(2,1)} %collective-permute-done.9.w1), channel_id=1, source_target_pairs={{0,64},{64,0},{1,65},{65,1},{2,66},{66,2},{3,67},{67,3},{4,68},{68... | collective-permute-start | bytes 1548296 | tf_op jit(solution)/shard_map/ppermute | solution.py:256
  151.6 45.8 %collective-permute-start.19 = (bf16[144,3584]{1,0:T(8,128)(2,1)S(1)}, bf16[144,3584]{1,0:T(8,128)(2,1)S(1)}, u32[]{:S(2)}, u32[]{:S(2)}) collective-permute-start(bf16[144,3584]{1,0:T(8,128)(2,1)S(1)} %collective-permute-done.18.w1), channel_id=1, source_target_pairs={{0,64},{64,0},{1,65},{65,1},{2,66},{66,2},{3,67},{67,3},{4,68},{68... | collective-permute-start | bytes 3096584 | tf_op jit(solution)/shard_map/ppermute | solution.py:256
  174.9 23.6 %collective-permute-start.21 = (bf16[144,3584]{1,0:T(8,128)(2,1)S(1)}, bf16[144,3584]{1,0:T(8,128)(2,1)}, u32[]{:S(2)}, u32[]{:S(2)}) collective-permute-start(bf16[144,3584]{1,0:T(8,128)(2,1)S(1)} %collective-permute-done.20.w3), channel_id=1, source_target_pairs={{0,64},{64,0},{1,65},{65,1},{2,66},{66,2},{3,67},{67,3},{4,68},{68... | collective-permute-start | bytes 3096584 | tf_op jit(solution)/shard_map/ppermute | solution.py:256
  174.9 23.6 %collective-permute-start.23 = (bf16[144,3584]{1,0:T(8,128)(2,1)}, bf16[144,3584]{1,0:T(8,128)(2,1)}, u32[]{:S(2)}, u32[]{:S(2)}) collective-permute-start(bf16[144,3584]{1,0:T(8,128)(2,1)} %collective-permute-done.22.w5), channel_id=1, source_target_pairs={{0,64},{64,0},{1,65},{65,1},{2,66},{66,2},{3,67},{67,3},{4,68},{68... | collective-permute-start | bytes 3096584 | tf_op jit(solution)/shard_map/ppermute | solution.py:256
  175.4 4.5 %collective-permute-start.12 = (bf16[288,896]{1,0:T(8,128)(2,1)}, bf16[288,896]{1,0:T(8,128)(2,1)S(1)}, u32[]{:S(2)}, u32[]{:S(2)}) collective-permute-start(bf16[288,896]{1,0:T(8,128)(2,1)} %copy-done.9), channel_id=1, source_target_pairs={{0,64},{64,0},{1,65},{65,1},{2,66},{66,2},{3,67},{67,3},{4,68},{68... | collective-permute-start | bytes 1548296 | tf_op jit(solution)/shard_map/ppermute | solution.py:256
  176.2 4.5 %collective-permute-start.14 = (bf16[288,896]{1,0:T(8,128)(2,1)}, bf16[288,896]{1,0:T(8,128)(2,1)S(1)}, u32[]{:S(2)}, u32[]{:S(2)}) collective-permute-start(bf16[288,896]{1,0:T(8,128)(2,1)} %copy-done.11), channel_id=1, source_target_pairs={{0,64},{64,0},{1,65},{65,1},{2,66},{66,2},{3,67},{67,3},{4,68},{68... | collective-permute-start | bytes 1548296 | tf_op jit(solution)/shard_map/ppermute | solution.py:256
  195.2 16.9 %collective-permute-start.15 = (bf16[1160,128]{1,0:T(8,128)(2,1)}, bf16[1160,128]{1,0:T(8,128)(2,1)S(1)}, u32[]{:S(2)}, u32[]{:S(2)}) collective-permute-start(bf16[1160,128]{1,0:T(8,128)(2,1)} %get-tuple-element.20), channel_id=1, source_target_pairs={{0,16},{16,32},{32,48},{48,0},{1,17},{17,33},{33,49},{49,1},{2,18}... | collective-permute-start | bytes 890888 | tf_op jit(solution)/shard_map/ppermute | solution.py:256
  195.2 16.9 %collective-permute-start.16 = (bf16[1160,128]{1,0:T(8,128)(2,1)}, bf16[1160,128]{1,0:T(8,128)(2,1)}, u32[]{:S(2)}, u32[]{:S(2)}) collective-permute-start(bf16[1160,128]{1,0:T(8,128)(2,1)} %get-tuple-element.21), channel_id=1, source_target_pairs={{0,32},{16,48},{32,0},{48,16},{1,33},{17,49},{33,1},{49,17},{2,34}... | collective-permute-start | bytes 890888 | tf_op jit(solution)/shard_map/ppermute | solution.py:256
  197.4 15.4 %collective-permute-start.17 = (bf16[1160,128]{1,0:T(8,128)(2,1)}, bf16[1160,128]{1,0:T(8,128)(2,1)}, u32[]{:S(2)}, u32[]{:S(2)}) collective-permute-start(bf16[1160,128]{1,0:T(8,128)(2,1)} %get-tuple-element.22), channel_id=1, source_target_pairs={{0,48},{16,0},{32,16},{48,32},{1,49},{17,1},{33,17},{49,33},{2,50}... | collective-permute-start | bytes 890888 | tf_op jit(solution)/shard_map/ppermute | solution.py:256
  (29 other events, 139.6 us)

commit v3 on v0

v3 whole, which is shorter than its diff:
```python
import jax
import jax.numpy as jnp
from jax import lax
from jax.experimental import pallas as pl
from jax.experimental.pallas import tpu as pltpu
from jax.sharding import Mesh, PartitionSpec as P

norm_eps = 1e-05
X, Z, Y = 4, 8, 2
LINE = Z * Y
f32, bf16 = jnp.float32, jnp.bfloat16
NT = (((1,), (1,)), ((), ()))
VMEM_LIMIT = 58 * 1024 * 1024


def smem():
    return pl.BlockSpec(memory_space=pltpu.SMEM)


def vmem():
    return pl.BlockSpec(memory_space=pltpu.VMEM)


def anywhere():
    return pl.BlockSpec(memory_space=pl.ANY)


def call(kernel, outs, ins, scratch, cost):
    single = not isinstance(outs, (list, tuple))
    return pl.pallas_call(
        kernel,
        out_shape=outs,
        in_specs=ins,
        out_specs=vmem() if single else [vmem()] * len(outs),
        scratch_shapes=scratch,
        compiler_params=pltpu.CompilerParams(vmem_limit_bytes=VMEM_LIMIT),
        cost_estimate=pl.CostEstimate(flops=cost[0], bytes_accessed=cost[1], transcendentals=0),
    )


def attend_kernel(counts, tails, order, q_ref, new_ref, kv_ref, out_ref, score, top, total, mixed):
    rows, heads, size = q_ref.shape
    pool, block, _ = kv_ref.shape
    scale = size ** (-0.5)
    owner, limit = [], []
    row, rank = jnp.int32(0), jnp.int32(0)
    for p in range(pool):
        last = rank + 1 == counts[0, row]
        owner.append(row)
        limit.append(jnp.where(last, tails[row], block))
        row = jnp.minimum(jnp.where(last, row + 1, row), rows - 1)
        rank = jnp.where(last, 0, rank + 1)
    own = []
    for r in range(rows):
        key = new_ref[r : r + 1, :size].astype(f32)
        own.append(jnp.sum(q_ref[r].astype(f32) * key, axis=1, keepdims=True) * scale)
        top[r] = jnp.broadcast_to(own[r], (heads, 128))
    lane = lax.broadcasted_iota(jnp.int32, (heads, block), 1)
    for p in range(pool):
        s = lax.dot_general(
            q_ref[owner[p]], kv_ref[order[0, p], :, :size], NT, preferred_element_type=f32
        )
        s = jnp.where(lane < limit[p], s * scale, -jnp.inf)
        score[p] = s
        top[owner[p]] = jnp.maximum(top[owner[p]], jnp.max(s, axis=1, keepdims=True))
    for r in range(rows):
        weight = jnp.exp(own[r] - top[r][:, :1])
        total[r] = jnp.broadcast_to(weight, (heads, 128))
        mixed[r] = weight * new_ref[r : r + 1, size:].astype(f32)
    for p in range(pool):
        weight = jnp.exp(score[p] - top[owner[p]][:, :1])
        total[owner[p]] += jnp.sum(weight, axis=1, keepdims=True)
        mixed[owner[p]] += jnp.dot(
            weight.astype(bf16), kv_ref[order[0, p], :, size:], preferred_element_type=f32
        )
    for r in range(rows):
        out_ref[r] = (mixed[r] / total[r][:, :1]).astype(bf16)


def attend(queries, new_kv, kv_cache, block_counts, tail_lens, block_order):
    rows = queries.shape[0]
    pool, block, twice = kv_cache.shape
    size = twice // 2
    heads = queries.shape[1] // size
    mixed = call(
        attend_kernel,
        jax.ShapeDtypeStruct((rows, heads, size), bf16),
        [smem()] * 3 + [vmem()] * 3,
        [
            pltpu.VMEM((pool, heads, block), f32),
            pltpu.VMEM((rows, heads, 128), f32),
            pltpu.VMEM((rows, heads, 128), f32),
            pltpu.VMEM((rows, heads, size), f32),
        ],
        (4 * pool * heads * block * size, pool * block * twice * 2),
    )(block_counts, tail_lens, block_order, queries.reshape(rows, heads, size), new_kv, kv_cache)
    return mixed.reshape(rows, heads * size)


def gather_pieces(pieces, sems):
    copies = [
        pltpu.make_async_copy(source, target, sems.at[i]) for i, (source, target) in enumerate(pieces)
    ]
    for copy in copies:
        copy.start()
    return copies


def wait_all(copies):
    for copy in copies:
        copy.wait()


def offset(value, unit):
    return pl.multiple_of(value, unit)


def project_kernel(at, first, near, near_far, side, side_far, own_out, o1, o2, o3, weight, sems):
    core, at_y = at[0], at[3]
    cols, half = near.shape[0] // X, near.shape[1]
    width = 2 * half
    pieces = []
    for which, y in ((near, at_y), (side, 1 - at_y)):
        rows = pl.ds(offset(y * X * cols, 16), X * cols)
        pieces.append((which, weight.at[rows, pl.ds(offset(core * half, 128), half)]))
    for which, y in ((near_far, at_y), (side_far, 1 - at_y)):
        rows = pl.ds(offset(y * X * cols, 16), X * cols)
        pieces.append((which, weight.at[rows, pl.ds(offset((1 - core) * half, 128), half)]))
    wait_all(gather_pieces(pieces, sems))
    for y in range(Y):
        for d, out in enumerate((own_out, o1, o2, o3)):
            rows = slice((y * X + d) * cols, (y * X + d + 1) * cols)
            got = lax.dot_general(
                weight[rows], first[:, :width], NT, preferred_element_type=f32
            )
            out[y * cols : (y + 1) * cols] = got.astype(out.dtype)


def norm_kernel(first, own, r1, r2, r3, gain, second, proj_out):
    cols = own.shape[0]
    width = first.shape[1] - 256
    proj = own[...] + r1[...].astype(f32) + r2[...].astype(f32) + r3[...].astype(f32)
    resid = first[:, width:].astype(f32).T
    stream = proj + resid[:cols]
    squares = jnp.sum(stream * stream, axis=0, keepdims=True)
    high = squares.astype(bf16).astype(f32)
    line = lax.broadcasted_iota(jnp.int32, (8, stream.shape[1]), 0)
    tail = jnp.where(line == 0, high, jnp.where(line == 1, squares - high, 0.0)).astype(bf16)
    scaled = (stream * gain[...]).astype(bf16)
    for z in range(Z):
        second[z, :cols] = scaled
        second[z, cols:] = tail
    proj_out[...] = jnp.concatenate(
        [proj, jnp.zeros((256 - cols, proj.shape[1]), f32)], axis=0
    ).T


def gate_up_kernel(
    at, second, proj, near, near_far, side, side_far, own_out, o1, o2, o3, weight, normed, total, sems
):
    core, at_x, at_y = at[0], at[1], at[3]
    ff2, half = near.shape[0] // X, near.shape[1]
    ff = ff2 // 2
    span = X * Y * ff
    cols = normed.shape[0] // Z
    pieces = []
    for which, c, y in (
        (near, core, at_y),
        (side, core, 1 - at_y),
        (near_far, 1 - core, at_y),
        (side_far, 1 - core, 1 - at_y),
    ):
        lanes = pl.ds(offset(c * half, 128), half)
        for d in range(X):
            block = (y * X + (at_x + X - d) % X) * ff
            for part in range(2):
                pieces.append(
                    (
                        which.at[pl.ds(d * ff2 + part * ff, ff)],
                        weight.at[pl.ds(offset(part * span + block, 16), ff), lanes],
                    )
                )
    for z in range(Z):
        pieces.append((second.at[z, pl.ds(0, cols)], normed.at[pl.ds(z * cols, cols)]))
    copies = gather_pieces(pieces, sems)
    squares = jnp.sum(second[:, cols : cols + 8].astype(f32), axis=0).T
    squares = squares[:, 0:1] + squares[:, 1:2]
    high = squares.astype(bf16).astype(f32)
    lane = lax.broadcasted_iota(jnp.int32, proj.shape, 1)
    total[:, 2 * span :] = jnp.where(
        lane == cols, high, jnp.where(lane == cols + 1, squares - high, proj[...])
    )
    wait_all(copies)
    step = 384

    def body(i, _):
        rows = pl.ds(offset(i * step, 128), step)
        total[:, rows] = jnp.dot(weight[rows], normed[...], preferred_element_type=f32).T
        return 0

    lax.fori_loop(0, 2 * span // step, body, 0)
    for e, out in enumerate((own_out, o1, o2, o3)):
        to = (at_x + e) % X
        for z in range(0, Z, 2):
            pair = [total[pl.ds(offset(((z + i) * X + to) * 8, 8), 8)] for i in range(2)]
            out[z * 8 : (z + 2) * 8] = jnp.concatenate(pair, axis=0).astype(out.dtype)


def act_kernel(at, width, own, r1, r2, r3, keep, send, shares):
    at_x, at_y = at[1], at[3]
    span = keep.shape[1] - 512
    summed = own[...] + r1[...].astype(f32) + r2[...].astype(f32) + r3[...].astype(f32)
    for e, r in enumerate((own, r1, r2, r3)):
        shares[e] = r[:, 2 * span :].astype(bf16)
    cols = 2 * span + 224
    squares = summed[:, cols : cols + 1] + summed[:, cols + 1 : cols + 2]
    scale = lax.rsqrt(squares / width + norm_eps)
    gate, up = summed[:, :span] * scale, summed[:, span : 2 * span] * scale
    hidden = (gate / (1.0 + jnp.exp(-gate)) * up).astype(bf16)
    for out, y in ((keep, at_y), (send, 1 - at_y)):
        out[:, :span] = hidden
        for j in range(2):
            e = (at_x + X - (2 * y + j)) % X
            out[:, span + j * 256 : span + (j + 1) * 256] = shares[e]


def down_kernel(at, keep, other, near, far, out, weight, act, total, sems):
    core, at_x, at_z, at_y = at[0], at[1], at[2], at[3]
    rows = keep.shape[0]
    half = near.shape[1]
    width = 2 * half
    ff = near.shape[0] // (X * Y)
    span = X * Y * ff
    pieces = []
    for which, c in ((near, core), (far, 1 - core)):
        lanes = pl.ds(offset(c * half, 128), half)
        for d in range(X):
            for side in range(Y):
                y = at_y if side == 0 else 1 - at_y
                block = (y * X + (at_x + X - d) % X) * ff
                pieces.append(
                    (
                        which.at[pl.ds((d * Y + side) * ff, ff)],
                        weight.at[pl.ds(offset(block, 16), ff), lanes],
                    )
                )
    copies = gather_pieces(pieces, sems)
    act[pl.ds(offset(at_y * rows, 16), rows)] = keep[...]
    act[pl.ds(offset((1 - at_y) * rows, 16), rows)] = other[...]
    wait_all(copies)
    step = 512

    def body(i, _):
        lanes = pl.ds(offset(i * step, 128), step)
        total[:, lanes] = jnp.dot(act[:, :span], weight[:, lanes], preferred_element_type=f32)
        return 0

    lax.fori_loop(0, width // step, body, 0)
    row = lax.broadcasted_iota(jnp.int32, (256, 384), 0)
    lane = lax.broadcasted_iota(jnp.int32, (256, 384), 1)
    for j in range(2):
        spot = j * half + at_z * 224
        base = jnp.minimum(spot // 128 * 128, width - 384)
        pick = jnp.where(row < 224, (row + (spot - base) == lane).astype(f32), 0.0).astype(bf16)
        lanes = pl.ds(offset(base, 128), 384)
        total[:, lanes] += jnp.dot(
            act[:, span + j * 256 : span + (j + 1) * 256], pick, preferred_element_type=f32
        )
    for z in range(Z):
        both = [total[y * rows + z * 8 : y * rows + (z + 1) * 8] for y in range(Y)]
        out[z] = jnp.concatenate(both, axis=0).astype(bf16)


def shifted(value, axis, step):
    size = lax.axis_size(axis)
    return lax.ppermute(value, axis, [(i, (i + step) % size) for i in range(size)])


def after(values, *others):
    return lax.optimization_barrier((values, others))[0]


def lanes(weight, begin, size):
    return lax.dynamic_slice_in_dim(weight, begin, size, 1)


def per_device(
    hidden_in,
    queries,
    new_kv,
    kv_cache,
    block_counts,
    tail_lens,
    block_order,
    out_weight,
    norm_gain,
    gate_weight,
    up_weight,
    down_weight,
):
    core, at_x, at_z, at_y = (lax.axis_index(a) for a in ("pair", "x", "z", "y"))
    at = jnp.stack([core, at_x, at_z, at_y])
    rows, width = hidden_in.shape
    slab = width // X
    block = width // (X * Z * Y)
    cols = Y * block
    chunk = X * Z * rows
    ff = gate_weight.shape[1]
    span = X * Y * ff
    heads = queries.shape[1] // X
    out_t, gate_t, up_t = out_weight.T, gate_weight.T, up_weight.T

    half = heads // 2
    pieces = [lanes(out_t, (at_x + d) % X * heads + core * half, half) for d in range(X)]
    out_near = jnp.concatenate(
        [pieces[0]] + [shifted(pieces[d], "x", d) for d in range(1, X)], axis=0
    )
    gain = shifted(norm_gain, "y", 1)
    gain = jnp.where(
        at_y == 0, jnp.concatenate([norm_gain, gain]), jnp.concatenate([gain, norm_gain])
    )[:, None]

    attended = attend(queries, new_kv, kv_cache, block_counts, tail_lens, block_order)
    first = jnp.concatenate(
        [attended.reshape(rows, X, heads), hidden_in.reshape(rows, X, slab)], axis=2
    ).transpose(1, 0, 2)
    first = after(first, out_near)
    first = lax.all_to_all(first, "x", 0, 0, tiled=True).reshape(X * rows, heads + slab)
    resid = first[:, heads:].reshape(X * rows, Z, cols).transpose(1, 0, 2)
    resid = jnp.pad(resid, ((0, 0), (0, 0), (0, 256 - cols)))
    first = jnp.concatenate(
        [jnp.broadcast_to(first[None, :, :heads], (Z, X * rows, heads)), resid], axis=2
    )
    first = lax.all_to_all(first, "z", 0, 0, tiled=True).reshape(chunk, heads + 256)

    out_side = shifted(out_near, "y", 1)
    out_near_far, out_side_far = shifted(out_near, "pair", 1), shifted(out_side, "pair", 1)

    gate_t, up_t = after((gate_t, up_t), out_near)
    half = slab // 2
    pieces = []
    for d in range(X):
        begin = (at_x + d) % X * slab + core * half
        pieces.append(
            jnp.concatenate([lanes(gate_t, begin, half), lanes(up_t, begin, half)], axis=0)
        )
    gate_up_near = jnp.concatenate(
        [pieces[0]] + [shifted(pieces[d], "x", d) for d in range(1, X)], axis=0
    )
    gate_up_side = shifted(after(gate_up_near, out_side), "y", 1)
    gate_up_near_far = shifted(gate_up_near, "pair", 1)
    gate_up_side_far = shifted(gate_up_side, "pair", 1)

    down_weight = after(down_weight, out_side)
    half = width // (2 * Y)
    down_side = shifted(
        lanes(down_weight, (1 - at_y) * (width // Y) + core * half, half), "y", 1
    )
    square = jnp.concatenate(
        [lanes(down_weight, at_y * (width // Y) + core * half, half), down_side], axis=0
    )
    square = after(square, gate_up_near)
    down_near = [square] + [shifted(square, "x", d) for d in range(1, X)]

    own, *sends = call(
        project_kernel,
        [jax.ShapeDtypeStruct((cols, chunk), t) for t in (f32, bf16, bf16, bf16)],
        [smem(), vmem()] + [anywhere()] * 4,
        [pltpu.VMEM((X * cols, heads), bf16), pltpu.SemaphoreType.DMA((4,))],
        (2 * X * cols * chunk * heads, X * cols * heads * 4),
    )(at, first, out_near, out_near_far, out_side, out_side_far)
    received = [shifted(send, "x", -d) for d, send in enumerate(sends, 1)]
    second, proj = call(
        norm_kernel,
        [
            jax.ShapeDtypeStruct((Z, cols + 8, chunk), bf16),
            jax.ShapeDtypeStruct((chunk, 256), f32),
        ],
        [vmem()] * 6,
        [],
        (10 * cols * chunk, 20 * cols * chunk),
    )(first, own, *received, gain)
    second = lax.all_to_all(second, "z", 0, 0, tiled=True)

    message = (Z * rows, 2 * span + 256)
    own, *sends = call(
        gate_up_kernel,
        [jax.ShapeDtypeStruct(message, t) for t in (f32, bf16, bf16, bf16)],
        [smem(), vmem(), vmem()] + [anywhere()] * 4,
        [
            pltpu.VMEM((2 * span, slab), bf16),
            pltpu.VMEM((slab, chunk), bf16),
            pltpu.VMEM((chunk, message[1]), f32),
            pltpu.SemaphoreType.DMA((8 * X + Z,)),
        ],
        (4 * span * slab * chunk, 2 * span * slab * 4),
    )(at, second, proj, gate_up_near, gate_up_near_far, gate_up_side, gate_up_side_far)
    received = [shifted(send, "x", e) for e, send in enumerate(sends, 1)]
    down_near = jnp.concatenate(after(down_near, own), axis=0)
    down_far = shifted(down_near, "pair", 1)
    keep, send = call(
        lambda *refs: act_kernel(refs[0], width, *refs[1:]),
        [jax.ShapeDtypeStruct((Z * rows, span + 512), bf16)] * 2,
        [smem()] + [vmem()] * 4,
        [pltpu.VMEM((X, Z * rows, 256), bf16)],
        (20 * span * Z * rows, 20 * span * Z * rows),
    )(at, own, *received)
    other = shifted(send, "y", 1)
    result = call(
        down_kernel,
        jax.ShapeDtypeStruct((Z, Y * rows, width // Y), bf16),
        [smem(), vmem(), vmem()] + [anywhere()] * 2,
        [
            pltpu.VMEM((span, width // Y), bf16),
            pltpu.VMEM((Y * Z * rows, span + 512), bf16),
            pltpu.VMEM((Y * Z * rows, width // Y), f32),
            pltpu.SemaphoreType.DMA((4 * X,)),
        ],
        (2 * span * Y * Z * rows * width // Y, span * width // Y * 4),
    )(at, keep, other, down_near, down_far)
    result = lax.all_to_all(result, "z", 0, 0, tiled=True)
    result = jnp.sum(result.astype(f32), axis=0).reshape(Y, rows, width // Y)
    mine = lax.dynamic_index_in_dim(result, at_y, 0, keepdims=False)
    theirs = lax.dynamic_index_in_dim(result, 1 - at_y, 0, keepdims=False)
    theirs = shifted(theirs, "y", 1)
    result = jnp.where(
        at_y == 0,
        jnp.concatenate([mine, theirs], axis=1),
        jnp.concatenate([theirs, mine], axis=1),
    )
    return (result + hidden_in.astype(f32)).astype(bf16)


def solution(mesh):
    fine = Mesh(mesh.devices.reshape(2, 2, X, Z, Y), ("role", "pair", "x", "z", "y"))
    dev = ("x", "z", "y")
    every = ("role", "pair") + dev
    return jax.shard_map(
        per_device,
        mesh=fine,
        in_specs=(
            P(every, None),
            P(every, None),
            P(every, None),
            P(every, None, None),
            P(every, None),
            P(every),
            P(every, None),
            P(None, dev),
            P(dev),
            P(None, dev),
            P(None, dev),
            P(dev, None),
        ),
        out_specs=P(every, None),
        check_vma=False,
    )
```

time: 1180 us -> 277 us (0.23)
  waiting for transfers between devices: 946 us -> 157 us
  blocking collectives: 181 us -> 0 us
  starting transfers between devices: 0.09 us -> 58.1 us
  Pallas kernels: 0 us -> 34.6 us
  matrix products: 25.8 us -> 0 us
  between operations: 13.3 us -> 0.37 us
  local copies, waits for them, and re-layouts: 7.33 us -> 19.2 us
    all_gather x2 -> x0, waiting for transfers between devices: 596 us -> none  [the longest x1 306 us: per_device(): shard_part = lax.all_gather(normed, 'dev', axis=1, tiled=True)]
    reduce_scatter x1 -> x0, waiting for transfers between devices: 350 us -> none  [per_device(): lax.psum_scatter(jnp.dot(hidden_act, down_weight, preferred_element_type=...]
    psum x1 -> x0, blocking collectives: 157 us -> none  [per_device(): square_sums = lax.psum(jnp.sum(stream * stream, axis=1), 'dev')]
    ppermute x0 -> x26, waiting for transfers between devices: none -> 123 us  [shifted(): lax.ppermute(value, axis, [(i, (i + step) % size) for i in range(size)])]
    pallas_call x0 -> x6, Pallas kernels: none -> 34.6 us  [the longest x1 10.1 us: per_device(): call(gate_up_kernel, [jax.ShapeDtypeStruct(message, t) for t in (f32, bf1...]
    all_to_all x0 -> x4, waiting for transfers between devices: none -> 33.5 us  [the longest x1 24.8 us: per_device(): result = lax.all_to_all(result, 'z', 0, 0, tiled=True)]
    ppermute x0 -> x26, starting transfers between devices: none -> 31 us  [shifted(): lax.ppermute(value, axis, [(i, (i + step) % size) for i in range(size)])]
    all_to_all x0 -> x4, starting transfers between devices: none -> 27.1 us  [the longest x1 8.47 us: per_device(): second = lax.all_to_all(second, 'z', 0, 0, tiled=True)]
  transfers between devices with their start and end apart: 3 -> 30, of which waited for: 3 -> 17; matrix products, arithmetic and copies ran while one was open for 0% -> 6% of each run, Pallas kernels for 0% -> 10%
where the time goes in v3:
time: 277 us; the launch traced here: 276 us
  waiting for transfers between devices  157 us (57%)
  starting transfers between devices  58.1 us (21%)
  Pallas kernels  34.6 us (12%)
  local copies, waits for them, and re-layouts  19.2 us (7%)
  other arithmetic  6.73 us (2%)
    ppermute x26, waiting for transfers between devices, shifted(): lax.ppermute(value, axis, [(i, (i + step) % size) for i in range(size)])  123 us
    ppermute x26, starting transfers between devices, shifted(): lax.ppermute(value, axis, [(i, (i + step) % size) for i in range(size)])  31 us
    all_to_all x1, waiting for transfers between devices, per_device(): result = lax.all_to_all(result, 'z', 0, 0, tiled=True)  24.8 us
    pallas_call x1, Pallas kernels, per_device(): call(gate_up_kernel, [jax.ShapeDtypeStruct(message, t) for t in (f32, bf1...  10.1 us
    unnamed x49, local copies, waits for them, and re-layouts  9.72 us
    all_to_all x1, waiting for transfers between devices, per_device(): second = lax.all_to_all(second, 'z', 0, 0, tiled=True)  8.65 us
    all_to_all x1, starting transfers between devices, per_device(): second = lax.all_to_all(second, 'z', 0, 0, tiled=True)  8.47 us
    all_to_all x1, starting transfers between devices, per_device(): lax.all_to_all(first, 'z', 0, 0, tiled=True).reshape(chunk, heads + 256)  8.47 us
  transfers between devices with their start and end apart: 30, of which 17 were waited for; matrix products, arithmetic and copies ran while one was open for 6% of the time, Pallas kernels for 10%

profile of v3, /device:TPU:16, one launch (start us, length us, event | category | flops | bytes accessed | tf_op | source)
XLA Modules:
  0.0 275.6 jit_solution(18043032433752603782)
XLA Ops:
  1.4 2.8 %collective-permute-start.2 = (bf16[112,1024]{1,0:T(8,128)(2,1)S(1)}, bf16[112,1024]{1,0:T(8,128)(2,1)S(1)}, u32[]{:S(2)}, u32[]{:S(2)}) collective-permute-start(bf16[112,1024]{1,0:T(8,128)(2,1)S(1)} %get-tuple-element.61), channel_id=1, source_target_pairs={{0,48},{16,0},{32,16},{48,32},{1,49},{17,1},{33,17},{49,33},{2,50}... | collective-permute-start | bytes 688136 | tf_op jit(solution)/shard_map/ppermute | solution.py:276
  6.6 4.4 %shard_map.118 = bf16[8,32,256]{2,1,0:T(8,128)(2,1)} custom-call(s32[1,8]{1,0:T(1,128)} %counts.1, s32[8]{0:T(128)} %tails.1, s32[1,16]{1,0:T(1,128)} %order.1, bf16[8,32,256]{2,1,0:T(8,128)(2,1)} %bitcast.37, bf16[8,512]{1,0:T(8,128)(2,1)} %new_ref.1, bf16[16,256,512]{2,1,0:T(8,128)(2,1)} %kv_ref.1), custom_call_target="tpu_custom_call" | custom-call | flops 134217728 | bytes 4194304 | tf_op jit(solution)/shard_map/pallas_call | solution.py:85
  14.3 3.4 %collective-permute-done = bf16[112,1024]{1,0:T(8,128)(2,1)S(1)} collective-permute-done((bf16[112,1024]{1,0:T(8,128)(2,1)S(1)}, bf16[112,1024]{1,0:T(8,128)(2,1)S(1)}, u32[]{:S(2)}, u32[]{:S(2)}) %collective-permute-start) | collective-permute-done | bytes 229408 | tf_op jit(solution)/shard_map/ppermute | solution.py:276
  19.1 3.4 %all-to-all-start = ((bf16[4,8,3840]{2,1,0:T(8,128)(2,1)}), bf16[4,8,3840]{2,1,0:T(8,128)(2,1)S(1)}, u32[]{:S(2)}, u32[]{:S(2)}) async-start(bf16[4,8,3840]{2,1,0:T(8,128)(2,1)} %maximum_bitcast_fusion), calls=%async_computation | async-start | bytes 491520 | tf_op jit(solution)/shard_map/all_to_all | solution.py:328
  35.9 8.5 %all-to-all-start.1 = ((bf16[8,32,2304]{2,1,0:T(8,128)(2,1)}), bf16[8,32,2304]{2,1,0:T(8,128)(2,1)S(1)}, u32[]{:S(2)}, u32[]{:S(2)}) async-start(bf16[8,32,2304]{2,1,0:T(8,128)(2,1)} %fusion.1), calls=%async_computation.1 | async-start | bytes 2359296 | tf_op jit(solution)/shard_map/all_to_all | solution.py:334
  45.2 8.5 %collective-permute-done.11 = bf16[288,896]{1,0:T(8,128)(2,1)} collective-permute-done((bf16[288,896]{1,0:T(8,128)(2,1)}, bf16[288,896]{1,0:T(8,128)(2,1)}, u32[]{:S(2)}, u32[]{:S(2)}) %collective-permute-start.11) | collective-permute-done | bytes 516128 | tf_op jit(solution)/shard_map/ppermute | solution.py:276
  60.7 42.5 %collective-permute-done.9 = f32[112]{0:T(128)S(1)} collective-permute-done((f32[112]{0:T(128)S(1)}, f32[112]{0:T(128)S(1)}, u32[]{:S(2)}, u32[]{:S(2)}) %collective-permute-start.9) | collective-permute-done | bytes 480 | tf_op jit(solution)/shard_map/ppermute | solution.py:276
  104.7 6.7 %shard_map.119 = (f32[224,256]{1,0:T(8,128)}, bf16[224,256]{1,0:T(8,128)(2,1)}, bf16[224,256]{1,0:T(8,128)(2,1)}, bf16[224,256]{1,0:T(8,128)(2,1)}) custom-call(s32[4]{0:T(128)} %pad_add_fusion.at.refs_0_, bf16[256,2304]{1,0:T(8,128)(2,1)} %bitcast.31, bf16[448,1024]{1,0:T(8,128)(2,1)} %copy-done.3, bf16[448,1024]{1,0:T(8,128)(2,1)} %collective-permute-done.3.near_far, ...), custom_call_target="tpu_custom_call" | custom-call | flops 939524096 | bytes 7340032 | tf_op jit(solution)/shard_map/pallas_call | solution.py:365
  111.4 2.8 %collective-permute-start.6 = (bf16[224,256]{1,0:T(8,128)(2,1)}, bf16[224,256]{1,0:T(8,128)(2,1)S(1)}, u32[]{:S(2)}, u32[]{:S(2)}) collective-permute-start(bf16[224,256]{1,0:T(8,128)(2,1)} %get-tuple-element.29), channel_id=1, source_target_pairs={{0,48},{16,0},{32,16},{48,32},{1,49},{17,1},{33,17},{49,33},{2,50}... | collective-permute-start | bytes 344072 | tf_op jit(solution)/shard_map/ppermute | solution.py:276
  116.9 3.2 %collective-permute-done.6.r1 = bf16[224,256]{1,0:T(8,128)(2,1)S(1)} collective-permute-done((bf16[224,256]{1,0:T(8,128)(2,1)}, bf16[224,256]{1,0:T(8,128)(2,1)S(1)}, u32[]{:S(2)}, u32[]{:S(2)}) %collective-permute-start.6) | collective-permute-done | bytes 114720 | tf_op jit(solution)/shard_map/ppermute | solution.py:276
  124.3 2.7 shard_map.120
  127.0 8.5 %all-to-all-start.2 = ((bf16[8,232,256]{2,1,0:T(8,128)(2,1)}), bf16[8,232,256]{2,1,0:T(8,128)(2,1)S(1)}, u32[]{:S(2)}, u32[]{:S(2)}) async-start(bf16[8,232,256]{2,1,0:T(8,128)(2,1)} %get-tuple-element.32), calls=%async_computation.2 | async-start | bytes 1900544 | tf_op jit(solution)/shard_map/all_to_all | solution.py:383
  136.4 12.4 %collective-permute-done.20 = bf16[144,1792]{1,0:T(8,128)(2,1)S(1)} collective-permute-done((bf16[144,1792]{1,0:T(8,128)(2,1)S(1)}, bf16[144,1792]{1,0:T(8,128)(2,1)S(1)}, u32[]{:S(2)}, u32[]{:S(2)}) %collective-permute-start.20) | collective-permute-done | bytes 516128 | tf_op jit(solution)/shard_map/ppermute | solution.py:276
  153.3 8.6 %all-to-all-done.2.second = bf16[8,232,256]{2,1,0:T(8,128)(2,1)S(1)} async-done(((bf16[8,232,256]{2,1,0:T(8,128)(2,1)}), bf16[8,232,256]{2,1,0:T(8,128)(2,1)S(1)}, u32[]{:S(2)}, u32[]{:S(2)}) %all-to-all-start.2) | async-done | bytes 950304 | tf_op jit(solution)/shard_map/all_to_all | solution.py:383
  162.9 10.1 %shard_map.121 = (f32[64,2560]{1,0:T(8,128)}, bf16[64,2560]{1,0:T(8,128)(2,1)}, bf16[64,2560]{1,0:T(8,128)(2,1)}, bf16[64,2560]{1,0:T(8,128)(2,1)}) custom-call(s32[4]{0:T(128)} %pad_add_fusion.at.refs_0_, bf16[8,232,256]{2,1,0:T(8,128)(2,1)} %copy-done.2, f32[256,256]{1,0:T(8,128)} %get-tuple-element.33.proj, ...), custom_call_target="tpu_custom_call" | custom-call | flops 2113929216 | bytes 16515072 | tf_op jit(solution)/shard_map/pallas_call | solution.py:386
  173.0 22.5 %collective-permute-done.21 = bf16[288,1792]{1,0:T(8,128)(2,1)S(1)} collective-permute-done((bf16[288,1792]{1,0:T(8,128)(2,1)S(1)}, bf16[288,1792]{1,0:T(8,128)(2,1)S(1)}, u32[]{:S(2)}, u32[]{:S(2)}) %collective-permute-start.21) | collective-permute-done | bytes 1032224 | tf_op jit(solution)/shard_map/ppermute | solution.py:276
  200.5 2.9 %collective-permute-start.17 = (bf16[64,2560]{1,0:T(8,128)(2,1)S(1)}, bf16[64,2560]{1,0:T(8,128)(2,1)S(1)}, u32[]{:S(2)}, u32[]{:S(2)}) collective-permute-start(bf16[64,2560]{1,0:T(8,128)(2,1)S(1)} %copy-done.19), channel_id=1, source_target_pairs={{0,32},{16,48},{32,0},{48,16},{1,33},{17,49},{33,1},{49,17},{2,34}... | collective-permute-start | bytes 983048 | tf_op jit(solution)/shard_map/ppermute | solution.py:276
  203.7 6.8 %collective-permute-done.16.refs_2_ = bf16[64,2560]{1,0:T(8,128)(2,1)S(1)} collective-permute-done((bf16[64,2560]{1,0:T(8,128)(2,1)S(1)}, bf16[64,2560]{1,0:T(8,128)(2,1)S(1)}, u32[]{:S(2)}, u32[]{:S(2)}) %collective-permute-start.16) | collective-permute-done | bytes 327712 | tf_op jit(solution)/shard_map/ppermute | solution.py:276
  210.5 7.9 %collective-permute-done.17.refs_3_ = bf16[64,2560]{1,0:T(8,128)(2,1)S(1)} collective-permute-done((bf16[64,2560]{1,0:T(8,128)(2,1)S(1)}, bf16[64,2560]{1,0:T(8,128)(2,1)S(1)}, u32[]{:S(2)}, u32[]{:S(2)}) %collective-permute-start.17) | collective-permute-done | bytes 327712 | tf_op jit(solution)/shard_map/ppermute | solution.py:276
  223.1 6.3 %collective-permute-done.19.other = bf16[64,1664]{1,0:T(8,128)(2,1)S(1)} collective-permute-done((bf16[64,1664]{1,0:T(8,128)(2,1)}, bf16[64,1664]{1,0:T(8,128)(2,1)S(1)}, u32[]{:S(2)}, u32[]{:S(2)}) %collective-permute-start.19) | collective-permute-done | bytes 213024 | tf_op jit(solution)/shard_map/ppermute | solution.py:276
  230.1 8.2 %shard_map.123 = bf16[8,16,3584]{2,1,0:T(8,128)(2,1)} custom-call(s32[4]{0:T(128)} %pad_add_fusion.at.refs_0_, bf16[64,1664]{1,0:T(8,128)(2,1)} %get-tuple-element.41.keep, bf16[64,1664]{1,0:T(8,128)(2,1)} %copy-done.12, bf16[1152,1792]{1,0:T(8,128)(2,1)} %copy-done.1, bf16[1152,1792]{1,0:T(8,128)(2,1)} %collective-permute-done.24.far), custom_call_target="tpu_custom_call" | custom-call | flops 1056964608 | bytes 16515072 | tf_op jit(solution)/shard_map/pallas_call | solution.py:409
  238.3 6.8 %all-to-all-start.3 = ((bf16[8,16,3584]{2,1,0:T(8,128)(2,1)}), bf16[8,16,3584]{2,1,0:T(8,128)(2,1)S(1)}, u32[]{:S(2)}, u32[]{:S(2)}) async-start(bf16[8,16,3584]{2,1,0:T(8,128)(2,1)} %shard_map.123), calls=%async_computation.3 | async-start | bytes 1835008 | tf_op jit(solution)/shard_map/all_to_all | solution.py:421
  245.1 24.8 %all-to-all-done.3 = bf16[8,16,3584]{2,1,0:T(8,128)(2,1)S(1)} async-done(((bf16[8,16,3584]{2,1,0:T(8,128)(2,1)}), bf16[8,16,3584]{2,1,0:T(8,128)(2,1)S(1)}, u32[]{:S(2)}, u32[]{:S(2)}) %all-to-all-start.3) | async-done | bytes 917536 | tf_op jit(solution)/shard_map/all_to_all | solution.py:421
  270.9 4.0 %collective-permute-done.25 = f32[8,3584]{1,0:T(8,128)S(1)} collective-permute-done((f32[8,3584]{1,0:T(8,128)S(1)}, f32[8,3584]{1,0:T(8,128)S(1)}, u32[]{:S(2)}, u32[]{:S(2)}) %collective-permute-start.25) | collective-permute-done | bytes 114720 | tf_op jit(solution)/shard_map/ppermute | solution.py:276
  (118 shorter events, 56.7 us)
Async XLA Ops:
  1.4 12.6 %collective-permute-start.2 = (bf16[112,1024]{1,0:T(8,128)(2,1)S(1)}, bf16[112,1024]{1,0:T(8,128)(2,1)S(1)}, u32[]{:S(2)}, u32[]{:S(2)}) collective-permute-start(bf16[112,1024]{1,0:T(8,128)(2,1)S(1)} %get-tuple-element.61), channel_id=1, source_target_pairs={{0,48},{16,0},{32,16},{48,32},{1,49},{17,1},{33,17},{49,33},{2,50}... | collective-permute-start | bytes 688136 | tf_op jit(solution)/shard_map/ppermute | solution.py:276
  5.0 12.7 %collective-permute-start = (bf16[112,1024]{1,0:T(8,128)(2,1)S(1)}, bf16[112,1024]{1,0:T(8,128)(2,1)S(1)}, u32[]{:S(2)}, u32[]{:S(2)}) collective-permute-start(bf16[112,1024]{1,0:T(8,128)(2,1)S(1)} %get-tuple-element.60), channel_id=1, source_target_pairs={{0,16},{16,32},{32,48},{48,0},{1,17},{17,33},{33,49},{49,1},{2,18}... | collective-permute-start | bytes 688136 | tf_op jit(solution)/shard_map/ppermute | solution.py:276
  17.8 39.7 %collective-permute-start.4 = (bf16[448,1024]{1,0:T(8,128)(2,1)S(1)}, bf16[448,1024]{1,0:T(8,128)(2,1)S(1)}, u32[]{:S(2)}, u32[]{:S(2)}) collective-permute-start(bf16[448,1024]{1,0:T(8,128)(2,1)S(1)} %pad_maximum_fusion.1.near), channel_id=1, source_target_pairs={{0,1},{1,0},{2,3},{3,2},{4,5},{5,4},{6,7},{7,6},{8,9},{9,8},{10,11... | collective-permute-start | bytes 2752520 | tf_op jit(solution)/shard_map/ppermute | solution.py:276
  19.1 15.2 %all-to-all-start = ((bf16[4,8,3840]{2,1,0:T(8,128)(2,1)}), bf16[4,8,3840]{2,1,0:T(8,128)(2,1)S(1)}, u32[]{:S(2)}, u32[]{:S(2)}) async-start(bf16[4,8,3840]{2,1,0:T(8,128)(2,1)} %maximum_bitcast_fusion), calls=%async_computation | async-start | bytes 491520 | tf_op jit(solution)/shard_map/all_to_all | solution.py:328
  26.5 17.8 %collective-permute-start.10 = (bf16[288,896]{1,0:T(8,128)(2,1)}, bf16[288,896]{1,0:T(8,128)(2,1)S(1)}, u32[]{:S(2)}, u32[]{:S(2)}) collective-permute-start(bf16[288,896]{1,0:T(8,128)(2,1)} %pad_maximum_fusion.2), channel_id=1, source_target_pairs={{0,16},{16,32},{32,48},{48,0},{1,17},{17,33},{33,49},{49,1},{2,18}... | collective-permute-start | bytes 1548296 | tf_op jit(solution)/shard_map/ppermute | solution.py:276
  29.3 24.3 %collective-permute-start.11 = (bf16[288,896]{1,0:T(8,128)(2,1)}, bf16[288,896]{1,0:T(8,128)(2,1)}, u32[]{:S(2)}, u32[]{:S(2)}) collective-permute-start(bf16[288,896]{1,0:T(8,128)(2,1)} %pad_maximum_fusion.3), channel_id=1, source_target_pairs={{0,32},{16,48},{32,0},{48,16},{1,33},{17,49},{33,1},{49,17},{2,34}... | collective-permute-start | bytes 1548296 | tf_op jit(solution)/shard_map/ppermute | solution.py:276
  32.9 22.7 %collective-permute-start.12 = (bf16[288,896]{1,0:T(8,128)(2,1)}, bf16[288,896]{1,0:T(8,128)(2,1)}, u32[]{:S(2)}, u32[]{:S(2)}) collective-permute-start(bf16[288,896]{1,0:T(8,128)(2,1)} %pad_maximum_fusion.4), channel_id=1, source_target_pairs={{0,48},{16,0},{32,16},{48,32},{1,49},{17,1},{33,17},{49,33},{2,50}... | collective-permute-start | bytes 1548296 | tf_op jit(solution)/shard_map/ppermute | solution.py:276
  35.9 67.8 %all-to-all-start.1 = ((bf16[8,32,2304]{2,1,0:T(8,128)(2,1)}), bf16[8,32,2304]{2,1,0:T(8,128)(2,1)S(1)}, u32[]{:S(2)}, u32[]{:S(2)}) async-start(bf16[8,32,2304]{2,1,0:T(8,128)(2,1)} %fusion.1), calls=%async_computation.1 | async-start | bytes 2359296 | tf_op jit(solution)/shard_map/all_to_all | solution.py:334
  57.5 58.7 %collective-permute-start.14 = (bf16[1152,896]{1,0:T(8,128)(2,1)}, bf16[1152,896]{1,0:T(8,128)(2,1)}, u32[]{:S(2)}, u32[]{:S(2)}) collective-permute-start(bf16[1152,896]{1,0:T(8,128)(2,1)} %constant_dynamic-update-slice_fusion.near), channel_id=1, source_target_pairs={{0,1},{1,0},{2,3},{3,2},{4,5},{5,4},{6,7},{7,6},{8,9},{9,8},{10,11... | collective-permute-start | bytes 6193160 | tf_op jit(solution)/shard_map/ppermute | solution.py:276
  58.2 45.4 %collective-permute-start.3 = (bf16[448,1024]{1,0:T(8,128)(2,1)S(1)}, bf16[448,1024]{1,0:T(8,128)(2,1)}, u32[]{:S(2)}, u32[]{:S(2)}) collective-permute-start(bf16[448,1024]{1,0:T(8,128)(2,1)S(1)} %pad_maximum_fusion.1.near), channel_id=1, source_target_pairs={{0,64},{64,0},{1,65},{65,1},{2,66},{66,2},{3,67},{67,3},{4,68},{68... | collective-permute-start | bytes 2752520 | tf_op jit(solution)/shard_map/ppermute | solution.py:276
  58.2 45.4 %collective-permute-start.5 = (bf16[448,1024]{1,0:T(8,128)(2,1)S(1)}, bf16[448,1024]{1,0:T(8,128)(2,1)}, u32[]{:S(2)}, u32[]{:S(2)}) collective-permute-start(bf16[448,1024]{1,0:T(8,128)(2,1)S(1)} %collective-permute-done.4.side), channel_id=1, source_target_pairs={{0,64},{64,0},{1,65},{65,1},{2,66},{66,2},{3,67},{67,3},{4,68},{68... | collective-permute-start | bytes 2752520 | tf_op jit(solution)/shard_map/ppermute | solution.py:276
  58.7 44.4 %collective-permute-start.9 = (f32[112]{0:T(128)S(1)}, f32[112]{0:T(128)S(1)}, u32[]{:S(2)}, u32[]{:S(2)}) collective-permute-start(f32[112]{0:T(128)S(1)} %copy-done.17), channel_id=1, source_target_pairs={{0,1},{1,0},{2,3},{3,2},{4,5},{5,4},{6,7},{7,6},{8,9},{9,8},{10,11... | collective-permute-start | bytes 1352 | tf_op jit(solution)/shard_map/ppermute | solution.py:276
  103.5 49.8 %collective-permute-start.13 = (bf16[1152,896]{1,0:T(8,128)(2,1)}, bf16[1152,896]{1,0:T(8,128)(2,1)}, u32[]{:S(2)}, u32[]{:S(2)}) collective-permute-start(bf16[1152,896]{1,0:T(8,128)(2,1)} %constant_dynamic-update-slice_fusion.near), channel_id=1, source_target_pairs={{0,64},{64,0},{1,65},{65,1},{2,66},{66,2},{3,67},{67,3},{4,68},{68... | collective-permute-start | bytes 6193160 | tf_op jit(solution)/shard_map/ppermute | solution.py:276
  116.2 45.8 %collective-permute-start.15 = (bf16[1152,896]{1,0:T(8,128)(2,1)}, bf16[1152,896]{1,0:T(8,128)(2,1)}, u32[]{:S(2)}, u32[]{:S(2)}) collective-permute-start(bf16[1152,896]{1,0:T(8,128)(2,1)} %collective-permute-done.14.side), channel_id=1, source_target_pairs={{0,64},{64,0},{1,65},{65,1},{2,66},{66,2},{3,67},{67,3},{4,68},{68... | collective-permute-start | bytes 6193160 | tf_op jit(solution)/shard_map/ppermute | solution.py:276
  127.0 35.0 %all-to-all-start.2 = ((bf16[8,232,256]{2,1,0:T(8,128)(2,1)}), bf16[8,232,256]{2,1,0:T(8,128)(2,1)S(1)}, u32[]{:S(2)}, u32[]{:S(2)}) async-start(bf16[8,232,256]{2,1,0:T(8,128)(2,1)} %get-tuple-element.32), calls=%async_computation.2 | async-start | bytes 1900544 | tf_op jit(solution)/shard_map/all_to_all | solution.py:383
  135.6 13.2 %collective-permute-start.20 = (bf16[144,1792]{1,0:T(8,128)(2,1)S(1)}, bf16[144,1792]{1,0:T(8,128)(2,1)S(1)}, u32[]{:S(2)}, u32[]{:S(2)}) collective-permute-start(bf16[144,1792]{1,0:T(8,128)(2,1)S(1)} %get-tuple-element.50), channel_id=1, source_target_pairs={{0,1},{1,0},{2,3},{3,2},{4,5},{5,4},{6,7},{7,6},{8,9},{9,8},{10,11... | collective-permute-start | bytes 1548296 | tf_op jit(solution)/shard_map/ppermute | solution.py:276
  148.8 46.7 %collective-permute-start.21 = (bf16[288,1792]{1,0:T(8,128)(2,1)S(1)}, bf16[288,1792]{1,0:T(8,128)(2,1)S(1)}, u32[]{:S(2)}, u32[]{:S(2)}) collective-permute-start(bf16[288,1792]{1,0:T(8,128)(2,1)S(1)} %pad_maximum_fusion), channel_id=1, source_target_pairs={{0,16},{16,32},{32,48},{48,0},{1,17},{17,33},{33,49},{49,1},{2,18}... | collective-permute-start | bytes 3096584 | tf_op jit(solution)/shard_map/ppermute | solution.py:276
  149.1 46.4 %collective-permute-start.22 = (bf16[288,1792]{1,0:T(8,128)(2,1)S(1)}, bf16[288,1792]{1,0:T(8,128)(2,1)}, u32[]{:S(2)}, u32[]{:S(2)}) collective-permute-start(bf16[288,1792]{1,0:T(8,128)(2,1)S(1)} %pad_maximum_fusion), channel_id=1, source_target_pairs={{0,32},{16,48},{32,0},{48,16},{1,33},{17,49},{33,1},{49,17},{2,34}... | collective-permute-start | bytes 3096584 | tf_op jit(solution)/shard_map/ppermute | solution.py:276
  150.8 45.4 %collective-permute-start.23 = (bf16[288,1792]{1,0:T(8,128)(2,1)S(1)}, bf16[288,1792]{1,0:T(8,128)(2,1)}, u32[]{:S(2)}, u32[]{:S(2)}) collective-permute-start(bf16[288,1792]{1,0:T(8,128)(2,1)S(1)} %pad_maximum_fusion), channel_id=1, source_target_pairs={{0,48},{16,0},{32,16},{48,32},{1,49},{17,1},{33,17},{49,33},{2,50}... | collective-permute-start | bytes 3096584 | tf_op jit(solution)/shard_map/ppermute | solution.py:276
  199.1 30.3 %collective-permute-start.24 = (bf16[1152,1792]{1,0:T(8,128)(2,1)S(1)}, bf16[1152,1792]{1,0:T(8,128)(2,1)}, u32[]{:S(2)}, u32[]{:S(2)}) collective-permute-start(bf16[1152,1792]{1,0:T(8,128)(2,1)S(1)} %constant_dynamic-update-slice_fusion.3.near), channel_id=1, source_target_pairs={{0,64},{64,0},{1,65},{65,1},{2,66},{66,2},{3,67},{67,3},{4,68},{68... | collective-permute-start | bytes 12386312 | tf_op jit(solution)/shard_map/ppermute | solution.py:276
  199.2 11.3 %collective-permute-start.16 = (bf16[64,2560]{1,0:T(8,128)(2,1)S(1)}, bf16[64,2560]{1,0:T(8,128)(2,1)S(1)}, u32[]{:S(2)}, u32[]{:S(2)}) collective-permute-start(bf16[64,2560]{1,0:T(8,128)(2,1)S(1)} %copy-done.20), channel_id=1, source_target_pairs={{0,16},{16,32},{32,48},{48,0},{1,17},{17,33},{33,49},{49,1},{2,18}... | collective-permute-start | bytes 983048 | tf_op jit(solution)/shard_map/ppermute | solution.py:276
  200.5 17.9 %collective-permute-start.17 = (bf16[64,2560]{1,0:T(8,128)(2,1)S(1)}, bf16[64,2560]{1,0:T(8,128)(2,1)S(1)}, u32[]{:S(2)}, u32[]{:S(2)}) collective-permute-start(bf16[64,2560]{1,0:T(8,128)(2,1)S(1)} %copy-done.19), channel_id=1, source_target_pairs={{0,32},{16,48},{32,0},{48,16},{1,33},{17,49},{33,1},{49,17},{2,34}... | collective-permute-start | bytes 983048 | tf_op jit(solution)/shard_map/ppermute | solution.py:276
  203.4 15.0 %collective-permute-start.18 = (bf16[64,2560]{1,0:T(8,128)(2,1)S(1)}, bf16[64,2560]{1,0:T(8,128)(2,1)S(1)}, u32[]{:S(2)}, u32[]{:S(2)}) collective-permute-start(bf16[64,2560]{1,0:T(8,128)(2,1)S(1)} %copy-done.18), channel_id=1, source_target_pairs={{0,48},{16,0},{32,16},{48,32},{1,49},{17,1},{33,17},{49,33},{2,50}... | collective-permute-start | bytes 983048 | tf_op jit(solution)/shard_map/ppermute | solution.py:276
  238.3 31.6 %all-to-all-start.3 = ((bf16[8,16,3584]{2,1,0:T(8,128)(2,1)}), bf16[8,16,3584]{2,1,0:T(8,128)(2,1)S(1)}, u32[]{:S(2)}, u32[]{:S(2)}) async-start(bf16[8,16,3584]{2,1,0:T(8,128)(2,1)} %shard_map.123), calls=%async_computation.3 | async-start | bytes 1835008 | tf_op jit(solution)/shard_map/all_to_all | solution.py:421
  (27 other events, 283.4 us)

commit v4 on v3

--- a/solution.py
+++ b/solution.py
@@ -25,22 +25,60 @@
     return pl.BlockSpec(memory_space=pl.ANY)
 
 
-def call(kernel, outs, ins, scratch, cost):
-    single = not isinstance(outs, (list, tuple))
+def call(kernel, outs, ins, scratch, cost, out_specs=None):
+    if out_specs is None:
+        out_specs = [vmem()] * len(outs) if isinstance(outs, (list, tuple)) else vmem()
     return pl.pallas_call(
         kernel,
         out_shape=outs,
         in_specs=ins,
-        out_specs=vmem() if single else [vmem()] * len(outs),
+        out_specs=out_specs,
         scratch_shapes=scratch,
         compiler_params=pltpu.CompilerParams(vmem_limit_bytes=VMEM_LIMIT),
         cost_estimate=pl.CostEstimate(flops=cost[0], bytes_accessed=cost[1], transcendentals=0),
     )
 
 
-def attend_kernel(counts, tails, order, q_ref, new_ref, kv_ref, out_ref, score, top, total, mixed):
+def gather_pieces(pieces, sems):
+    copies = [
+        pltpu.make_async_copy(source, target, sems.at[i]) for i, (source, target) in enumerate(pieces)
+    ]
+    for copy in copies:
+        copy.start()
+    return copies
+
+
+def wait_all(copies):
+    for copy in copies:
+        copy.wait()
+
+
+def offset(value, unit):
+    return pl.multiple_of(value, unit)
+
+
+def attend_kernel(
+    at, counts, tails, order, q_ref, new_ref, kv_any, gate, up, down,
+    out_ref, g0, g1, g2, g3, down_keep, down_send,
+    kv_ref, score, top, total, mixed, kv_sems, sems,
+):
+    core, at_x, at_y = at[0], at[1], at[3]
     rows, heads, size = q_ref.shape
     pool, block, _ = kv_ref.shape
+    loads = gather_pieces([(kv_any.at[order[0, p]], kv_ref.at[p]) for p in range(pool)], kv_sems)
+    ff, half = gate.shape[0], g0.shape[1]
+    pieces = []
+    for d, out in ((1, g1), (2, g2), (3, g3), (0, g0)):
+        begin = (at_x + d) % X * (2 * half) + core * half
+        for part, source in enumerate((gate, up)):
+            pieces.append(
+                (source.at[:, pl.ds(offset(begin, 128), half)], out.at[pl.ds(part * ff, ff)])
+            )
+    half = down_keep.shape[1]
+    for y, out in ((1 - at_y, down_send), (at_y, down_keep)):
+        begin = offset(y * (2 * half) + core * half, 128)
+        pieces.append((down.at[:, pl.ds(begin, half)], out))
+    slices = gather_pieces(pieces, sems)
     scale = size ** (-0.5)
     owner, limit = [], []
     row, rank = jnp.int32(0), jnp.int32(0)
@@ -57,9 +95,8 @@
         top[r] = jnp.broadcast_to(own[r], (heads, 128))
     lane = lax.broadcasted_iota(jnp.int32, (heads, block), 1)
     for p in range(pool):
-        s = lax.dot_general(
-            q_ref[owner[p]], kv_ref[order[0, p], :, :size], NT, preferred_element_type=f32
-        )
+        loads[p].wait()
+        s = lax.dot_general(q_ref[owner[p]], kv_ref[p, :, :size], NT, preferred_element_type=f32)
         s = jnp.where(lane < limit[p], s * scale, -jnp.inf)
         score[p] = s
         top[owner[p]] = jnp.maximum(top[owner[p]], jnp.max(s, axis=1, keepdims=True))
@@ -71,69 +108,85 @@
         weight = jnp.exp(score[p] - top[owner[p]][:, :1])
         total[owner[p]] += jnp.sum(weight, axis=1, keepdims=True)
         mixed[owner[p]] += jnp.dot(
-            weight.astype(bf16), kv_ref[order[0, p], :, size:], preferred_element_type=f32
+            weight.astype(bf16), kv_ref[p, :, size:], preferred_element_type=f32
         )
     for r in range(rows):
         out_ref[r] = (mixed[r] / total[r][:, :1]).astype(bf16)
-
-
-def attend(queries, new_kv, kv_cache, block_counts, tail_lens, block_order):
+    wait_all(slices)
+
+
+def attend(at, queries, new_kv, kv_cache, block_counts, tail_lens, block_order, gate_t, up_t, down):
     rows = queries.shape[0]
     pool, block, twice = kv_cache.shape
     size = twice // 2
     heads = queries.shape[1] // size
-    mixed = call(
+    ff, width = gate_t.shape
+    piece = jax.ShapeDtypeStruct((2 * ff, width // X // 2), bf16)
+    down_piece = jax.ShapeDtypeStruct((ff, width // Y // 2), bf16)
+    mixed, *pieces = call(
         attend_kernel,
-        jax.ShapeDtypeStruct((rows, heads, size), bf16),
-        [smem()] * 3 + [vmem()] * 3,
+        [jax.ShapeDtypeStruct((rows, heads, size), bf16)] + [piece] * X + [down_piece] * 2,
+        [smem()] * 4 + [vmem()] * 2 + [anywhere()] * 4,
         [
+            pltpu.VMEM(kv_cache.shape, bf16),
             pltpu.VMEM((pool, heads, block), f32),
             pltpu.VMEM((rows, heads, 128), f32),
             pltpu.VMEM((rows, heads, 128), f32),
             pltpu.VMEM((rows, heads, size), f32),
+            pltpu.SemaphoreType.DMA((pool,)),
+            pltpu.SemaphoreType.DMA((2 * X + 2,)),
         ],
         (4 * pool * heads * block * size, pool * block * twice * 2),
-    )(block_counts, tail_lens, block_order, queries.reshape(rows, heads, size), new_kv, kv_cache)
-    return mixed.reshape(rows, heads * size)
-
-
-def gather_pieces(pieces, sems):
-    copies = [
-        pltpu.make_async_copy(source, target, sems.at[i]) for i, (source, target) in enumerate(pieces)
-    ]
-    for copy in copies:
-        copy.start()
-    return copies
-
-
-def wait_all(copies):
-    for copy in copies:
-        copy.wait()
-
-
-def offset(value, unit):
-    return pl.multiple_of(value, unit)
-
-
-def project_kernel(at, first, near, near_far, side, side_far, own_out, o1, o2, o3, weight, sems):
+        None,
+    )(
+        at, block_counts, tail_lens, block_order, queries.reshape(rows, heads, size), new_kv,
+        kv_cache, gate_t, up_t, down,
+    )
+    return mixed.reshape(rows, heads * size), pieces[:X], pieces[X:]
+
+
+def join_kernel(*refs):
+    sources, out, sems = refs[:-2], refs[-2], refs[-1]
+    pieces, at = [], 0
+    for source in sources:
+        pieces.append((source, out.at[pl.ds(at, source.shape[0])]))
+        at += source.shape[0]
+    wait_all(gather_pieces(pieces, sems))
+
+
+def join(pieces):
+    shape = (sum(piece.shape[0] for piece in pieces), pieces[0].shape[1])
+    return call(
+        join_kernel,
+        jax.ShapeDtypeStruct(shape, bf16),
+        [anywhere()] * len(pieces),
+        [pltpu.SemaphoreType.DMA((len(pieces),))],
+        (0, shape[0] * shape[1] * 4),
+    )(*pieces)
+
+
+def project_kernel(
+    at, first, near, near_far, side, side_far, own_out, o1, o2, o3, weight, heads, sems
+):
     core, at_y = at[0], at[3]
     cols, half = near.shape[0] // X, near.shape[1]
     width = 2 * half
-    pieces = []
-    for which, y in ((near, at_y), (side, 1 - at_y)):
+    pieces = [(first.at[:, pl.ds(0, width)], heads)]
+    for which, c, y in (
+        (near, core, at_y),
+        (near_far, 1 - core, at_y),
+        (side, core, 1 - at_y),
+        (side_far, 1 - core, 1 - at_y),
+    ):
         rows = pl.ds(offset(y * X * cols, 16), X * cols)
-        pieces.append((which, weight.at[rows, pl.ds(offset(core * half, 128), half)]))
-    for which, y in ((near_far, at_y), (side_far, 1 - at_y)):
-        rows = pl.ds(offset(y * X * cols, 16), X * cols)
-        pieces.append((which, weight.at[rows, pl.ds(offset((1 - core) * half, 128), half)]))
+        pieces.append((which, weight.at[rows, pl.ds(offset(c * half, 128), half)]))
     wait_all(gather_pieces(pieces, sems))
     for y in range(Y):
+        got = lax.dot_general(
+            weight[y * X * cols : (y + 1) * X * cols], heads[...], NT, preferred_element_type=f32
+        )
         for d, out in enumerate((own_out, o1, o2, o3)):
-            rows = slice((y * X + d) * cols, (y * X + d + 1) * cols)
-            got = lax.dot_general(
-                weight[rows], first[:, :width], NT, preferred_element_type=f32
-            )
-            out[y * cols : (y + 1) * cols] = got.astype(out.dtype)
+            out[y * cols : (y + 1) * cols] = got[d * cols : (d + 1) * cols].astype(out.dtype)
 
 
 def norm_kernel(first, own, r1, r2, r3, gain, second, proj_out):
@@ -156,32 +209,28 @@
 
 
 def gate_up_kernel(
-    at, second, proj, near, near_far, side, side_far, own_out, o1, o2, o3, weight, normed, total, sems
+    at, second, proj, near, near_far, side, side_far,
+    own_out, o1, o2, o3,
+    weight, normed, columns, total, sems,
 ):
     core, at_x, at_y = at[0], at[1], at[3]
     ff2, half = near.shape[0] // X, near.shape[1]
     ff = ff2 // 2
     span = X * Y * ff
     cols = normed.shape[0] // Z
-    pieces = []
-    for which, c, y in (
-        (near, core, at_y),
-        (side, core, 1 - at_y),
-        (near_far, 1 - core, at_y),
-        (side_far, 1 - core, 1 - at_y),
-    ):
-        lanes = pl.ds(offset(c * half, 128), half)
+    pieces = [
+        (second.at[z, pl.ds(0, cols)], normed.at[pl.ds(z * cols, cols)]) for z in range(Z)
+    ]
+    for s, sources in enumerate(((near, near_far), (side, side_far))):
         for d in range(X):
-            block = (y * X + (at_x + X - d) % X) * ff
-            for part in range(2):
+            for which, c in zip(sources, (core, 1 - core)):
+                rows = pl.ds((s * X + d) * ff2, ff2)
                 pieces.append(
                     (
-                        which.at[pl.ds(d * ff2 + part * ff, ff)],
-                        weight.at[pl.ds(offset(part * span + block, 16), ff), lanes],
+                        which.at[pl.ds(d * ff2, ff2)],
+                        weight.at[rows, pl.ds(offset(c * half, 128), half)],
                     )
                 )
-    for z in range(Z):
-        pieces.append((second.at[z, pl.ds(0, cols)], normed.at[pl.ds(z * cols, cols)]))
     copies = gather_pieces(pieces, sems)
     squares = jnp.sum(second[:, cols : cols + 8].astype(f32), axis=0).T
     squares = squares[:, 0:1] + squares[:, 1:2]
@@ -190,15 +239,22 @@
     total[:, 2 * span :] = jnp.where(
         lane == cols, high, jnp.where(lane == cols + 1, squares - high, proj[...])
     )
-    wait_all(copies)
+    wait_all(copies[:Z])
+    for s in range(Y):
+        y = at_y if s == 0 else 1 - at_y
+        for d in range(X):
+            i = s * X + d
+            wait_all(copies[Z + 2 * i : Z + 2 * i + 2])
+            got = jnp.dot(
+                weight[i * ff2 : (i + 1) * ff2], normed[...], preferred_element_type=f32
+            )
+            block = (y * X + (at_x + X - d) % X) * ff
+            columns[pl.ds(offset(block, 16), ff)] = got[:ff]
+            columns[pl.ds(offset(span + block, 16), ff)] = got[ff:]
     step = 384
-
-    def body(i, _):
-        rows = pl.ds(offset(i * step, 128), step)
-        total[:, rows] = jnp.dot(weight[rows], normed[...], preferred_element_type=f32).T
-        return 0
-
-    lax.fori_loop(0, 2 * span // step, body, 0)
+    for i in range(2 * span // step):
+        rows = slice(i * step, (i + 1) * step)
+        total[:, rows] = columns[rows].T
     for e, out in enumerate((own_out, o1, o2, o3)):
         to = (at_x + e) % X
         for z in range(0, Z, 2):
@@ -247,15 +303,10 @@
     copies = gather_pieces(pieces, sems)
     act[pl.ds(offset(at_y * rows, 16), rows)] = keep[...]
     act[pl.ds(offset((1 - at_y) * rows, 16), rows)] = other[...]
-    wait_all(copies)
-    step = 512
-
-    def body(i, _):
-        lanes = pl.ds(offset(i * step, 128), step)
-        total[:, lanes] = jnp.dot(act[:, :span], weight[:, lanes], preferred_element_type=f32)
-        return 0
-
-    lax.fori_loop(0, width // step, body, 0)
+    for i, c in enumerate((core, 1 - core)):
+        wait_all(copies[i * X * Y : (i + 1) * X * Y])
+        here = pl.ds(offset(c * half, 128), half)
+        total[:, here] = jnp.dot(act[:, :span], weight[:, here], preferred_element_type=f32)
     row = lax.broadcasted_iota(jnp.int32, (256, 384), 0)
     lane = lax.broadcasted_iota(jnp.int32, (256, 384), 1)
     for j in range(2):
@@ -312,64 +363,53 @@
 
     half = heads // 2
     pieces = [lanes(out_t, (at_x + d) % X * heads + core * half, half) for d in range(X)]
-    out_near = jnp.concatenate(
-        [pieces[0]] + [shifted(pieces[d], "x", d) for d in range(1, X)], axis=0
-    )
+    out_near = join([pieces[0]] + [shifted(pieces[d], "x", d) for d in range(1, X)])
     gain = shifted(norm_gain, "y", 1)
     gain = jnp.where(
         at_y == 0, jnp.concatenate([norm_gain, gain]), jnp.concatenate([gain, norm_gain])
     )[:, None]
 
-    attended = attend(queries, new_kv, kv_cache, block_counts, tail_lens, block_order)
+    attended, gate_up_pieces, down_pieces = attend(
+        at, queries, new_kv, kv_cache, block_counts, tail_lens, block_order, gate_t, up_t, down_weight
+    )
     first = jnp.concatenate(
         [attended.reshape(rows, X, heads), hidden_in.reshape(rows, X, slab)], axis=2
     ).transpose(1, 0, 2)
-    first = after(first, out_near)
+    first = after(first, (out_near, gain))
     first = lax.all_to_all(first, "x", 0, 0, tiled=True).reshape(X * rows, heads + slab)
     resid = first[:, heads:].reshape(X * rows, Z, cols).transpose(1, 0, 2)
     resid = jnp.pad(resid, ((0, 0), (0, 0), (0, 256 - cols)))
     first = jnp.concatenate(
         [jnp.broadcast_to(first[None, :, :heads], (Z, X * rows, heads)), resid], axis=2
     )
+    ready = first
     first = lax.all_to_all(first, "z", 0, 0, tiled=True).reshape(chunk, heads + 256)
 
     out_side = shifted(out_near, "y", 1)
     out_near_far, out_side_far = shifted(out_near, "pair", 1), shifted(out_side, "pair", 1)
 
-    gate_t, up_t = after((gate_t, up_t), out_near)
-    half = slab // 2
-    pieces = []
-    for d in range(X):
-        begin = (at_x + d) % X * slab + core * half
-        pieces.append(
-            jnp.concatenate([lanes(gate_t, begin, half), lanes(up_t, begin, half)], axis=0)
-        )
-    gate_up_near = jnp.concatenate(
-        [pieces[0]] + [shifted(pieces[d], "x", d) for d in range(1, X)], axis=0
-    )
-    gate_up_side = shifted(after(gate_up_near, out_side), "y", 1)
-    gate_up_near_far = shifted(gate_up_near, "pair", 1)
-    gate_up_side_far = shifted(gate_up_side, "pair", 1)
-
-    down_weight = after(down_weight, out_side)
-    half = width // (2 * Y)
-    down_side = shifted(
-        lanes(down_weight, (1 - at_y) * (width // Y) + core * half, half), "y", 1
-    )
-    square = jnp.concatenate(
-        [lanes(down_weight, at_y * (width // Y) + core * half, half), down_side], axis=0
-    )
-    square = after(square, gate_up_near)
-    down_near = [square] + [shifted(square, "x", d) for d in range(1, X)]
+    down_side = shifted(after(down_pieces[1], out_near), "y", 1)
+
+    pieces = after(gate_up_pieces, out_near)
+    gate_up_near = after([shifted(pieces[d], "x", d) for d in range(1, X)], ready)
+    gate_up_near = join([pieces[0]] + gate_up_near)
+    gate_up_side = shifted(after(gate_up_near, (out_side, down_side)), "y", 1)
+    square = join([after(down_pieces[0], gate_up_near), down_side])
+    down_near = [square, shifted(square, "x", 1), shifted(square, "x", -1)]
 
     own, *sends = call(
         project_kernel,
         [jax.ShapeDtypeStruct((cols, chunk), t) for t in (f32, bf16, bf16, bf16)],
-        [smem(), vmem()] + [anywhere()] * 4,
-        [pltpu.VMEM((X * cols, heads), bf16), pltpu.SemaphoreType.DMA((4,))],
+        [smem()] + [anywhere()] * 5,
+        [
+            pltpu.VMEM((X * cols, heads), bf16),
+            pltpu.VMEM((chunk, heads), bf16),
+            pltpu.SemaphoreType.DMA((5,)),
+        ],
         (2 * X * cols * chunk * heads, X * cols * heads * 4),
     )(at, first, out_near, out_near_far, out_side, out_side_far)
     received = [shifted(send, "x", -d) for d, send in enumerate(sends, 1)]
+    received = after(received, down_near)
     second, proj = call(
         norm_kernel,
         [
@@ -380,6 +420,10 @@
         [],
         (10 * cols * chunk, 20 * cols * chunk),
     )(first, own, *received, gain)
+    gate_up_near, gate_up_side, square = after((gate_up_near, gate_up_side, square), second)
+    gate_up_near_far = shifted(gate_up_near, "pair", 1)
+    gate_up_side_far = shifted(gate_up_side, "pair", 1)
+    down_across = shifted(square, "x", 2)
     second = lax.all_to_all(second, "z", 0, 0, tiled=True)
 
     message = (Z * rows, 2 * span + 256)
@@ -390,13 +434,15 @@
         [
             pltpu.VMEM((2 * span, slab), bf16),
             pltpu.VMEM((slab, chunk), bf16),
+            pltpu.VMEM((2 * span, chunk), f32),
             pltpu.VMEM((chunk, message[1]), f32),
-            pltpu.SemaphoreType.DMA((8 * X + Z,)),
+            pltpu.SemaphoreType.DMA((4 * X + Z,)),
         ],
         (4 * span * slab * chunk, 2 * span * slab * 4),
     )(at, second, proj, gate_up_near, gate_up_near_far, gate_up_side, gate_up_side_far)
     received = [shifted(send, "x", e) for e, send in enumerate(sends, 1)]
-    down_near = jnp.concatenate(after(down_near, own), axis=0)
+    down_across = after(down_across, received)
+    down_near = join([down_near[0], down_near[1], down_across, down_near[2]])
     down_far = shifted(down_near, "pair", 1)
     keep, send = call(
         lambda *refs: act_kernel(refs[0], width, *refs[1:]),

time: 277 us -> 232 us (0.84)
  waiting for transfers between devices: 157 us -> 109 us
  Pallas kernels: 34.6 us -> 48.2 us
  local copies, waits for them, and re-layouts: 19.2 us -> 10.1 us
    ppermute x26, waiting for transfers between devices: 123 us -> 51.5 us  [shifted(): lax.ppermute(value, axis, [(i, (i + step) % size) for i in range(size)])]
    pallas_call x1 -> x5, Pallas kernels: 4.39 us -> 20.3 us  [the longest x4 11.5 us: join(): call(join_kernel, jax.ShapeDtypeStruct(shape, bf16), [anywhere()] * len(p...]
    all_to_all x1, waiting for transfers between devices: 8.65 us -> 24.4 us  [per_device(): second = lax.all_to_all(second, 'z', 0, 0, tiled=True)]
    all_to_all x1, waiting for transfers between devices: 0.01 us -> 6.52 us  [per_device(): lax.all_to_all(first, 'z', 0, 0, tiled=True).reshape(chunk, heads + 256)]
    ppermute x26, starting transfers between devices: 31 us -> 35.4 us  [shifted(): lax.ppermute(value, axis, [(i, (i + step) % size) for i in range(size)])]
    unnamed x49 -> x40, local copies, waits for them, and re-layouts: 9.72 us -> 6.33 us
    all_to_all x1, starting transfers between devices: 6.79 us -> 3.56 us  [per_device(): result = lax.all_to_all(result, 'z', 0, 0, tiled=True)]
    concatenate x2 -> x0, local copies, waits for them, and re-layouts: 3.22 us -> none  [the longest x1 1.93 us: per_device(): jnp.concatenate([pieces[0]] + [shifted(pieces[d], 'x', d) for d in range(...]
  transfers between devices with their start and end apart: 30 -> 30, of which waited for: 17 -> 15; matrix products, arithmetic and copies ran while one was open for 6% -> 2% of each run, Pallas kernels for 10% -> 15%
where the time goes in v4:
time: 232 us; the launch traced here: 231 us
  waiting for transfers between devices  109 us (47%)
  starting transfers between devices  59.3 us (26%)
  Pallas kernels  48.2 us (21%)
  local copies, waits for them, and re-layouts  10.1 us (4%)
  other arithmetic  3.98 us (2%)
    ppermute x26, waiting for transfers between devices, shifted(): lax.ppermute(value, axis, [(i, (i + step) % size) for i in range(size)])  51.5 us
    ppermute x26, starting transfers between devices, shifted(): lax.ppermute(value, axis, [(i, (i + step) % size) for i in range(size)])  35.4 us
    all_to_all x1, waiting for transfers between devices, per_device(): result = lax.all_to_all(result, 'z', 0, 0, tiled=True)  26 us
    all_to_all x1, waiting for transfers between devices, per_device(): second = lax.all_to_all(second, 'z', 0, 0, tiled=True)  24.4 us
    pallas_call x4, Pallas kernels, join(): call(join_kernel, jax.ShapeDtypeStruct(shape, bf16), [anywhere()] * len(p...  11.5 us
    pallas_call x1, Pallas kernels, per_device(): call(gate_up_kernel, [jax.ShapeDtypeStruct(message, t) for t in (f32, bf1...  11.2 us
    pallas_call x1, Pallas kernels, attend(): call(attend_kernel, [jax.ShapeDtypeStruct((rows, heads, size), bf16)] + [...  8.84 us
    all_to_all x1, starting transfers between devices, per_device(): second = lax.all_to_all(second, 'z', 0, 0, tiled=True)  8.47 us
  transfers between devices with their start and end apart: 30, of which 15 were waited for; matrix products, arithmetic and copies ran while one was open for 2% of the time, Pallas kernels for 15%

profile of v4, /device:TPU:16, one launch (start us, length us, event | category | flops | bytes accessed | tf_op | source)
XLA Modules:
  0.0 230.9 jit_solution(1291158631415702014)
XLA Ops:
  3.6 2.7 %collective-permute-start.1 = (bf16[112,1024]{1,0:T(8,128)(2,1)S(1)}, bf16[112,1024]{1,0:T(8,128)(2,1)S(1)}, u32[]{:S(2)}, u32[]{:S(2)}) collective-permute-start(bf16[112,1024]{1,0:T(8,128)(2,1)S(1)} %get-tuple-element.82), channel_id=1, source_target_pairs={{0,32},{16,48},{32,0},{48,16},{1,33},{17,49},{33,1},{49,17},{2,34}... | collective-permute-start | bytes 688136 | tf_op jit(solution)/shard_map/ppermute | solution.py:327
  10.3 8.8 %shard_map.118 = (bf16[8,32,256]{2,1,0:T(8,128)(2,1)}, bf16[288,896]{1,0:T(8,128)(2,1)}, bf16[288,896]{1,0:T(8,128)(2,1)}, bf16[288,896]{1,0:T(8,128)(2,1)}, bf1...) custom-call(s32[4]{0:T(128)} %pad_add_fusion.at.refs_0_, s32[1,8]{1,0:T(1,128)} %counts.1, ...), custom_call_target="tpu_custom_call" | custom-call | flops 134217728 | bytes 4194304 | tf_op jit(solution)/shard_map/pallas_call | solution.py:126
  25.9 3.4 %all-to-all-start = ((bf16[4,8,3840]{2,1,0:T(8,128)(2,1)}), bf16[4,8,3840]{2,1,0:T(8,128)(2,1)S(1)}, u32[]{:S(2)}, u32[]{:S(2)}) async-start(bf16[4,8,3840]{2,1,0:T(8,128)(2,1)} %maximum_bitcast_fusion), calls=%async_computation | async-start | bytes 491520 | tf_op jit(solution)/shard_map/all_to_all | solution.py:379
  38.8 8.5 %all-to-all-start.1 = ((bf16[8,32,2304]{2,1,0:T(8,128)(2,1)}), bf16[8,32,2304]{2,1,0:T(8,128)(2,1)S(1)}, u32[]{:S(2)}, u32[]{:S(2)}) async-start(bf16[8,32,2304]{2,1,0:T(8,128)(2,1)} %fusion.1), calls=%async_computation.1 | async-start | bytes 2359296 | tf_op jit(solution)/shard_map/all_to_all | solution.py:386
  47.8 9.1 %collective-permute-done.11.refs_2_ = bf16[288,896]{1,0:T(8,128)(2,1)} collective-permute-done((bf16[288,896]{1,0:T(8,128)(2,1)}, bf16[288,896]{1,0:T(8,128)(2,1)}, u32[]{:S(2)}, u32[]{:S(2)}) %collective-permute-start.11) | collective-permute-done | bytes 516128 | tf_op jit(solution)/shard_map/ppermute | solution.py:327
  56.9 2.9 %shard_map.121.near = bf16[1152,896]{1,0:T(8,128)(2,1)} custom-call(bf16[288,896]{1,0:T(8,128)(2,1)} %get-tuple-element.53.refs_0_, bf16[288,896]{1,0:T(8,128)(2,1)} %collective-permute-done.10.refs_1_, bf16[288,896]{1,0:T(8,128)(2,1)} %collective-permute-done.11.refs_2_, bf16[288,896]{1,0:T(8,128)(2,1)} %collective-permute-done.12.refs_3_), custom_call_target="tpu_custom_call" | custom-call | bytes 4128768 | tf_op jit(solution)/shard_map/pallas_call | solution.py:159
  69.0 6.5 %all-to-all-done.1 = bf16[8,32,2304]{2,1,0:T(8,128)(2,1)S(1)} async-done(((bf16[8,32,2304]{2,1,0:T(8,128)(2,1)}), bf16[8,32,2304]{2,1,0:T(8,128)(2,1)S(1)}, u32[]{:S(2)}, u32[]{:S(2)}) %all-to-all-start.1) | async-done | bytes 1179680 | tf_op jit(solution)/shard_map/all_to_all | solution.py:386
  76.6 5.0 %shard_map.120 = (f32[224,256]{1,0:T(8,128)}, bf16[224,256]{1,0:T(8,128)(2,1)}, bf16[224,256]{1,0:T(8,128)(2,1)}, bf16[224,256]{1,0:T(8,128)(2,1)}) custom-call(s32[4]{0:T(128)} %pad_add_fusion.at.refs_0_, bf16[256,2304]{1,0:T(8,128)(2,1)} %bitcast.31, bf16[448,1024]{1,0:T(8,128)(2,1)} %shard_map.119.near, bf16[448,1024]{1,0:T(8,128)(2,1)} %copy-done.6, ...), custom_call_target="tpu_custom_call" | custom-call | flops 939524096 | bytes 7340032 | tf_op jit(solution)/shard_map/pallas_call | solution.py:400
  84.4 3.8 %collective-permute-done.14.refs_1_ = bf16[288,1792]{1,0:T(8,128)(2,1)} collective-permute-done((bf16[288,1792]{1,0:T(8,128)(2,1)}, bf16[288,1792]{1,0:T(8,128)(2,1)}, u32[]{:S(2)}, u32[]{:S(2)}) %collective-permute-start.14) | collective-permute-done | bytes 1032224 | tf_op jit(solution)/shard_map/ppermute | solution.py:327
  90.8 3.9 %collective-permute-done.7.r1 = bf16[224,256]{1,0:T(8,128)(2,1)S(1)} collective-permute-done((bf16[224,256]{1,0:T(8,128)(2,1)}, bf16[224,256]{1,0:T(8,128)(2,1)S(1)}, u32[]{:S(2)}, u32[]{:S(2)}) %collective-permute-start.7) | collective-permute-done | bytes 114720 | tf_op jit(solution)/shard_map/ppermute | solution.py:327
  95.4 2.7 %shard_map.123 = (bf16[8,232,256]{2,1,0:T(8,128)(2,1)}, f32[256,256]{1,0:T(8,128)}) custom-call(bf16[256,2304]{1,0:T(8,128)(2,1)} %bitcast.32, f32[224,256]{1,0:T(8,128)} %get-tuple-element.44.own, bf16[224,256]{1,0:T(8,128)(2,1)} %copy-done.15, bf16[224,256]{1,0:T(8,128)(2,1)} %copy-done.16, bf16[224,256]{1,0:T(8,128)(2,1)} %copy-done.17, ...), custom_call_target="tpu_custom_call" | custom-call | flops 573440 | bytes 1146880 | tf_op jit(solution)/shard_map/pallas_call | solution.py:413
  98.1 7.0 %collective-permute-done.16.side = bf16[1152,896]{1,0:T(8,128)(2,1)} collective-permute-done((bf16[1152,896]{1,0:T(8,128)(2,1)}, bf16[1152,896]{1,0:T(8,128)(2,1)}, u32[]{:S(2)}, u32[]{:S(2)}) %collective-permute-start.16) | collective-permute-done | bytes 2064416 | tf_op jit(solution)/shard_map/ppermute | solution.py:327
  105.7 8.5 %all-to-all-start.2 = ((bf16[8,232,256]{2,1,0:T(8,128)(2,1)}), bf16[8,232,256]{2,1,0:T(8,128)(2,1)}, u32[]{:S(2)}, u32[]{:S(2)}) async-start(bf16[8,232,256]{2,1,0:T(8,128)(2,1)} %get-tuple-element.66), calls=%async_computation.2 | async-start | bytes 1900544 | tf_op jit(solution)/shard_map/all_to_all | solution.py:427
  116.6 24.4 %all-to-all-done.2.second = bf16[8,232,256]{2,1,0:T(8,128)(2,1)} async-done(((bf16[8,232,256]{2,1,0:T(8,128)(2,1)}), bf16[8,232,256]{2,1,0:T(8,128)(2,1)}, u32[]{:S(2)}, u32[]{:S(2)}) %all-to-all-start.2) | async-done | bytes 950304 | tf_op jit(solution)/shard_map/all_to_all | solution.py:427
  141.0 11.2 %shard_map.124 = (f32[64,2560]{1,0:T(8,128)}, bf16[64,2560]{1,0:T(8,128)(2,1)}, bf16[64,2560]{1,0:T(8,128)(2,1)}, bf16[64,2560]{1,0:T(8,128)(2,1)}) custom-call(s32[4]{0:T(128)} %pad_add_fusion.at.refs_0_, bf16[8,232,256]{2,1,0:T(8,128)(2,1)} %all-to-all-done.2.second, f32[256,256]{1,0:T(8,128)} %get-tuple-element.67.proj, ...), custom_call_target="tpu_custom_call" | custom-call | flops 2113929216 | bytes 16515072 | tf_op jit(solution)/shard_map/pallas_call | solution.py:430
  154.1 3.3 %collective-permute-start.20 = (bf16[64,2560]{1,0:T(8,128)(2,1)}, bf16[64,2560]{1,0:T(8,128)(2,1)}, u32[]{:S(2)}, u32[]{:S(2)}) collective-permute-start(bf16[64,2560]{1,0:T(8,128)(2,1)} %get-tuple-element.73), channel_id=1, source_target_pairs={{0,32},{16,48},{32,0},{48,16},{1,33},{17,49},{33,1},{49,17},{2,34}... | collective-permute-start | bytes 983048 | tf_op jit(solution)/shard_map/ppermute | solution.py:327
  157.4 6.6 %collective-permute-done.19.refs_2_ = bf16[64,2560]{1,0:T(8,128)(2,1)S(1)} collective-permute-done((bf16[64,2560]{1,0:T(8,128)(2,1)}, bf16[64,2560]{1,0:T(8,128)(2,1)S(1)}, u32[]{:S(2)}, u32[]{:S(2)}) %collective-permute-start.19) | collective-permute-done | bytes 327712 | tf_op jit(solution)/shard_map/ppermute | solution.py:327
  164.1 8.3 %collective-permute-done.20.refs_3_ = bf16[64,2560]{1,0:T(8,128)(2,1)} collective-permute-done((bf16[64,2560]{1,0:T(8,128)(2,1)}, bf16[64,2560]{1,0:T(8,128)(2,1)}, u32[]{:S(2)}, u32[]{:S(2)}) %collective-permute-start.20) | collective-permute-done | bytes 327712 | tf_op jit(solution)/shard_map/ppermute | solution.py:327
  172.4 4.2 %shard_map.126.near = bf16[1152,1792]{1,0:T(8,128)(2,1)} custom-call(bf16[288,1792]{1,0:T(8,128)(2,1)} %shard_map.122.refs_0_, bf16[288,1792]{1,0:T(8,128)(2,1)} %collective-permute-done.14.refs_1_, bf16[288,1792]{1,0:T(8,128)(2,1)} %collective-permute-done.23.refs_2_, bf16[288,1792]{1,0:T(8,128)(2,1)} %collective-permute-done.15.refs_3_), custom_call_target="tpu_custom_call" | custom-call | bytes 8257536 | tf_op jit(solution)/shard_map/pallas_call | solution.py:159
  180.5 6.6 %collective-permute-done.22.other = bf16[64,1664]{1,0:T(8,128)(2,1)S(1)} collective-permute-done((bf16[64,1664]{1,0:T(8,128)(2,1)}, bf16[64,1664]{1,0:T(8,128)(2,1)S(1)}, u32[]{:S(2)}, u32[]{:S(2)}) %collective-permute-start.22) | collective-permute-done | bytes 213024 | tf_op jit(solution)/shard_map/ppermute | solution.py:327
  189.1 6.5 %shard_map.127 = bf16[8,16,3584]{2,1,0:T(8,128)(2,1)} custom-call(s32[4]{0:T(128)} %pad_add_fusion.at.refs_0_, bf16[64,1664]{1,0:T(8,128)(2,1)} %get-tuple-element.75.keep, bf16[64,1664]{1,0:T(8,128)(2,1)} %copy-done.13, bf16[1152,1792]{1,0:T(8,128)(2,1)} %shard_map.126.near, bf16[1152,1792]{1,0:T(8,128)(2,1)} %copy-done.2), custom_call_target="tpu_custom_call" | custom-call | flops 1056964608 | bytes 16515072 | tf_op jit(solution)/shard_map/pallas_call | solution.py:455
  195.6 3.6 %all-to-all-start.3 = ((bf16[8,16,3584]{2,1,0:T(8,128)(2,1)}), bf16[8,16,3584]{2,1,0:T(8,128)(2,1)S(1)}, u32[]{:S(2)}, u32[]{:S(2)}) async-start(bf16[8,16,3584]{2,1,0:T(8,128)(2,1)} %shard_map.127), calls=%async_computation.3 | async-start | bytes 1835008 | tf_op jit(solution)/shard_map/all_to_all | solution.py:467
  199.2 26.0 %all-to-all-done.3 = bf16[8,16,3584]{2,1,0:T(8,128)(2,1)S(1)} async-done(((bf16[8,16,3584]{2,1,0:T(8,128)(2,1)}), bf16[8,16,3584]{2,1,0:T(8,128)(2,1)S(1)}, u32[]{:S(2)}, u32[]{:S(2)}) %all-to-all-start.3) | async-done | bytes 917536 | tf_op jit(solution)/shard_map/all_to_all | solution.py:467
  226.7 3.5 %collective-permute-done.25 = f32[8,3584]{1,0:T(8,128)S(1)} collective-permute-done((f32[8,3584]{1,0:T(8,128)S(1)}, f32[8,3584]{1,0:T(8,128)S(1)}, u32[]{:S(2)}, u32[]{:S(2)}) %collective-permute-start.25) | collective-permute-done | bytes 114720 | tf_op jit(solution)/shard_map/ppermute | solution.py:327
  (103 shorter events, 53.5 us)
Async XLA Ops:
  2.1 19.2 %collective-permute-start = (bf16[112,1024]{1,0:T(8,128)(2,1)S(1)}, bf16[112,1024]{1,0:T(8,128)(2,1)S(1)}, u32[]{:S(2)}, u32[]{:S(2)}) collective-permute-start(bf16[112,1024]{1,0:T(8,128)(2,1)S(1)} %get-tuple-element.80), channel_id=1, source_target_pairs={{0,16},{16,32},{32,48},{48,0},{1,17},{17,33},{33,49},{49,1},{2,18}... | collective-permute-start | bytes 688136 | tf_op jit(solution)/shard_map/ppermute | solution.py:327
  3.6 17.7 %collective-permute-start.1 = (bf16[112,1024]{1,0:T(8,128)(2,1)S(1)}, bf16[112,1024]{1,0:T(8,128)(2,1)S(1)}, u32[]{:S(2)}, u32[]{:S(2)}) collective-permute-start(bf16[112,1024]{1,0:T(8,128)(2,1)S(1)} %get-tuple-element.82), channel_id=1, source_target_pairs={{0,32},{16,48},{32,0},{48,16},{1,33},{17,49},{33,1},{49,17},{2,34}... | collective-permute-start | bytes 688136 | tf_op jit(solution)/shard_map/ppermute | solution.py:327
  6.3 15.0 %collective-permute-start.2 = (bf16[112,1024]{1,0:T(8,128)(2,1)S(1)}, bf16[112,1024]{1,0:T(8,128)(2,1)S(1)}, u32[]{:S(2)}, u32[]{:S(2)}) collective-permute-start(bf16[112,1024]{1,0:T(8,128)(2,1)S(1)} %get-tuple-element.79), channel_id=1, source_target_pairs={{0,48},{16,0},{32,16},{48,32},{1,49},{17,1},{33,17},{49,33},{2,50}... | collective-permute-start | bytes 688136 | tf_op jit(solution)/shard_map/ppermute | solution.py:327
  7.7 13.2 %collective-permute-start.3 = (f32[112]{0:T(128)}, f32[112]{0:T(128)S(1)}, u32[]{:S(2)}, u32[]{:S(2)}) collective-permute-start(f32[112]{0:T(128)} %param.20), channel_id=1, source_target_pairs={{0,1},{1,0},{2,3},{3,2},{4,5},{5,4},{6,7},{7,6},{8,9},{9,8},{10,11... | collective-permute-start | bytes 1352 | tf_op jit(solution)/shard_map/ppermute | solution.py:327
  24.4 35.4 %collective-permute-start.5 = (bf16[448,1024]{1,0:T(8,128)(2,1)}, bf16[448,1024]{1,0:T(8,128)(2,1)S(1)}, u32[]{:S(2)}, u32[]{:S(2)}) collective-permute-start(bf16[448,1024]{1,0:T(8,128)(2,1)} %shard_map.119.near), channel_id=1, source_target_pairs={{0,1},{1,0},{2,3},{3,2},{4,5},{5,4},{6,7},{7,6},{8,9},{9,8},{10,11... | collective-permute-start | bytes 2752520 | tf_op jit(solution)/shard_map/ppermute | solution.py:327
  25.9 11.3 %all-to-all-start = ((bf16[4,8,3840]{2,1,0:T(8,128)(2,1)}), bf16[4,8,3840]{2,1,0:T(8,128)(2,1)S(1)}, u32[]{:S(2)}, u32[]{:S(2)}) async-start(bf16[4,8,3840]{2,1,0:T(8,128)(2,1)} %maximum_bitcast_fusion), calls=%async_computation | async-start | bytes 491520 | tf_op jit(solution)/shard_map/all_to_all | solution.py:379
  29.3 18.5 %collective-permute-start.10 = (bf16[288,896]{1,0:T(8,128)(2,1)}, bf16[288,896]{1,0:T(8,128)(2,1)}, u32[]{:S(2)}, u32[]{:S(2)}) collective-permute-start(bf16[288,896]{1,0:T(8,128)(2,1)} %get-tuple-element.54), channel_id=1, source_target_pairs={{0,16},{16,32},{32,48},{48,0},{1,17},{17,33},{33,49},{49,1},{2,18}... | collective-permute-start | bytes 1548296 | tf_op jit(solution)/shard_map/ppermute | solution.py:327
  31.3 25.6 %collective-permute-start.11 = (bf16[288,896]{1,0:T(8,128)(2,1)}, bf16[288,896]{1,0:T(8,128)(2,1)}, u32[]{:S(2)}, u32[]{:S(2)}) collective-permute-start(bf16[288,896]{1,0:T(8,128)(2,1)} %get-tuple-element.55), channel_id=1, source_target_pairs={{0,32},{16,48},{32,0},{48,16},{1,33},{17,49},{33,1},{49,17},{2,34}... | collective-permute-start | bytes 1548296 | tf_op jit(solution)/shard_map/ppermute | solution.py:327
  34.0 22.9 %collective-permute-start.12 = (bf16[288,896]{1,0:T(8,128)(2,1)}, bf16[288,896]{1,0:T(8,128)(2,1)}, u32[]{:S(2)}, u32[]{:S(2)}) collective-permute-start(bf16[288,896]{1,0:T(8,128)(2,1)} %get-tuple-element.56), channel_id=1, source_target_pairs={{0,48},{16,0},{32,16},{48,32},{1,49},{17,1},{33,17},{49,33},{2,50}... | collective-permute-start | bytes 1548296 | tf_op jit(solution)/shard_map/ppermute | solution.py:327
  35.4 24.3 %collective-permute-start.13 = (bf16[144,1792]{1,0:T(8,128)(2,1)}, bf16[144,1792]{1,0:T(8,128)(2,1)S(1)}, u32[]{:S(2)}, u32[]{:S(2)}) collective-permute-start(bf16[144,1792]{1,0:T(8,128)(2,1)} %get-tuple-element.62), channel_id=1, source_target_pairs={{0,1},{1,0},{2,3},{3,2},{4,5},{5,4},{6,7},{7,6},{8,9},{9,8},{10,11... | collective-permute-start | bytes 1548296 | tf_op jit(solution)/shard_map/ppermute | solution.py:327
  38.8 36.7 %all-to-all-start.1 = ((bf16[8,32,2304]{2,1,0:T(8,128)(2,1)}), bf16[8,32,2304]{2,1,0:T(8,128)(2,1)S(1)}, u32[]{:S(2)}, u32[]{:S(2)}) async-start(bf16[8,32,2304]{2,1,0:T(8,128)(2,1)} %fusion.1), calls=%async_computation.1 | async-start | bytes 2359296 | tf_op jit(solution)/shard_map/all_to_all | solution.py:386
  59.8 45.4 %collective-permute-start.16 = (bf16[1152,896]{1,0:T(8,128)(2,1)}, bf16[1152,896]{1,0:T(8,128)(2,1)}, u32[]{:S(2)}, u32[]{:S(2)}) collective-permute-start(bf16[1152,896]{1,0:T(8,128)(2,1)} %shard_map.121.near), channel_id=1, source_target_pairs={{0,1},{1,0},{2,3},{3,2},{4,5},{5,4},{6,7},{7,6},{8,9},{9,8},{10,11... | collective-permute-start | bytes 6193160 | tf_op jit(solution)/shard_map/ppermute | solution.py:327
  63.3 24.9 %collective-permute-start.14 = (bf16[288,1792]{1,0:T(8,128)(2,1)}, bf16[288,1792]{1,0:T(8,128)(2,1)}, u32[]{:S(2)}, u32[]{:S(2)}) collective-permute-start(bf16[288,1792]{1,0:T(8,128)(2,1)} %shard_map.122.refs_0_), channel_id=1, source_target_pairs={{0,16},{16,32},{32,48},{48,0},{1,17},{17,33},{33,49},{49,1},{2,18}... | collective-permute-start | bytes 3096584 | tf_op jit(solution)/shard_map/ppermute | solution.py:327
  64.8 26.0 %collective-permute-start.15 = (bf16[288,1792]{1,0:T(8,128)(2,1)}, bf16[288,1792]{1,0:T(8,128)(2,1)}, u32[]{:S(2)}, u32[]{:S(2)}) collective-permute-start(bf16[288,1792]{1,0:T(8,128)(2,1)} %shard_map.122.refs_0_), channel_id=1, source_target_pairs={{0,48},{16,0},{32,16},{48,32},{1,49},{17,1},{33,17},{49,33},{2,50}... | collective-permute-start | bytes 3096584 | tf_op jit(solution)/shard_map/ppermute | solution.py:327
  81.6 13.1 %collective-permute-start.7 = (bf16[224,256]{1,0:T(8,128)(2,1)}, bf16[224,256]{1,0:T(8,128)(2,1)S(1)}, u32[]{:S(2)}, u32[]{:S(2)}) collective-permute-start(bf16[224,256]{1,0:T(8,128)(2,1)} %get-tuple-element.45), channel_id=1, source_target_pairs={{0,48},{16,0},{32,16},{48,32},{1,49},{17,1},{33,17},{49,33},{2,50}... | collective-permute-start | bytes 344072 | tf_op jit(solution)/shard_map/ppermute | solution.py:327
  82.2 12.4 %collective-permute-start.8 = (bf16[224,256]{1,0:T(8,128)(2,1)}, bf16[224,256]{1,0:T(8,128)(2,1)S(1)}, u32[]{:S(2)}, u32[]{:S(2)}) collective-permute-start(bf16[224,256]{1,0:T(8,128)(2,1)} %get-tuple-element.46), channel_id=1, source_target_pairs={{0,32},{16,48},{32,0},{48,16},{1,33},{17,49},{33,1},{49,17},{2,34}... | collective-permute-start | bytes 344072 | tf_op jit(solution)/shard_map/ppermute | solution.py:327
  105.2 35.9 %collective-permute-start.17 = (bf16[1152,896]{1,0:T(8,128)(2,1)S(1)}, bf16[1152,896]{1,0:T(8,128)(2,1)}, u32[]{:S(2)}, u32[]{:S(2)}) collective-permute-start(bf16[1152,896]{1,0:T(8,128)(2,1)S(1)} %copy-done.1), channel_id=1, source_target_pairs={{0,64},{64,0},{1,65},{65,1},{2,66},{66,2},{3,67},{67,3},{4,68},{68... | collective-permute-start | bytes 6193160 | tf_op jit(solution)/shard_map/ppermute | solution.py:327
  105.2 35.9 %collective-permute-start.18 = (bf16[1152,896]{1,0:T(8,128)(2,1)}, bf16[1152,896]{1,0:T(8,128)(2,1)}, u32[]{:S(2)}, u32[]{:S(2)}) collective-permute-start(bf16[1152,896]{1,0:T(8,128)(2,1)} %collective-permute-done.16.side), channel_id=1, source_target_pairs={{0,64},{64,0},{1,65},{65,1},{2,66},{66,2},{3,67},{67,3},{4,68},{68... | collective-permute-start | bytes 6193160 | tf_op jit(solution)/shard_map/ppermute | solution.py:327
  105.7 35.4 %all-to-all-start.2 = ((bf16[8,232,256]{2,1,0:T(8,128)(2,1)}), bf16[8,232,256]{2,1,0:T(8,128)(2,1)}, u32[]{:S(2)}, u32[]{:S(2)}) async-start(bf16[8,232,256]{2,1,0:T(8,128)(2,1)} %get-tuple-element.66), calls=%async_computation.2 | async-start | bytes 1900544 | tf_op jit(solution)/shard_map/all_to_all | solution.py:427
  114.1 43.3 %collective-permute-start.23 = (bf16[288,1792]{1,0:T(8,128)(2,1)S(1)}, bf16[288,1792]{1,0:T(8,128)(2,1)}, u32[]{:S(2)}, u32[]{:S(2)}) collective-permute-start(bf16[288,1792]{1,0:T(8,128)(2,1)S(1)} %copy-done.3), channel_id=1, source_target_pairs={{0,32},{16,48},{32,0},{48,16},{1,33},{17,49},{33,1},{49,17},{2,34}... | collective-permute-start | bytes 3096584 | tf_op jit(solution)/shard_map/ppermute | solution.py:327
  152.2 11.9 %collective-permute-start.19 = (bf16[64,2560]{1,0:T(8,128)(2,1)}, bf16[64,2560]{1,0:T(8,128)(2,1)S(1)}, u32[]{:S(2)}, u32[]{:S(2)}) collective-permute-start(bf16[64,2560]{1,0:T(8,128)(2,1)} %get-tuple-element.72), channel_id=1, source_target_pairs={{0,16},{16,32},{32,48},{48,0},{1,17},{17,33},{33,49},{49,1},{2,18}... | collective-permute-start | bytes 983048 | tf_op jit(solution)/shard_map/ppermute | solution.py:327
  154.1 18.3 %collective-permute-start.20 = (bf16[64,2560]{1,0:T(8,128)(2,1)}, bf16[64,2560]{1,0:T(8,128)(2,1)}, u32[]{:S(2)}, u32[]{:S(2)}) collective-permute-start(bf16[64,2560]{1,0:T(8,128)(2,1)} %get-tuple-element.73), channel_id=1, source_target_pairs={{0,32},{16,48},{32,0},{48,16},{1,33},{17,49},{33,1},{49,17},{2,34}... | collective-permute-start | bytes 983048 | tf_op jit(solution)/shard_map/ppermute | solution.py:327
  157.4 15.0 %collective-permute-start.21 = (bf16[64,2560]{1,0:T(8,128)(2,1)}, bf16[64,2560]{1,0:T(8,128)(2,1)}, u32[]{:S(2)}, u32[]{:S(2)}) collective-permute-start(bf16[64,2560]{1,0:T(8,128)(2,1)} %get-tuple-element.74), channel_id=1, source_target_pairs={{0,48},{16,0},{32,16},{48,32},{1,49},{17,1},{33,17},{49,33},{2,50}... | collective-permute-start | bytes 983048 | tf_op jit(solution)/shard_map/ppermute | solution.py:327
  195.6 29.5 %all-to-all-start.3 = ((bf16[8,16,3584]{2,1,0:T(8,128)(2,1)}), bf16[8,16,3584]{2,1,0:T(8,128)(2,1)S(1)}, u32[]{:S(2)}, u32[]{:S(2)}) async-start(bf16[8,16,3584]{2,1,0:T(8,128)(2,1)} %shard_map.127), calls=%async_computation.3 | async-start | bytes 1835008 | tf_op jit(solution)/shard_map/all_to_all | solution.py:467
  (25 other events, 172.0 us)

commit v5 on v4

v5 whole, which is shorter than its diff:
```python
import jax
import jax.numpy as jnp
from jax import lax
from jax.experimental import pallas as pl
from jax.experimental.pallas import tpu as pltpu
from jax.sharding import Mesh, PartitionSpec as P

norm_eps = 1e-05
X, Z, Y = 4, 8, 2
LINE = Z * Y
f32, bf16 = jnp.float32, jnp.bfloat16
NT = (((1,), (1,)), ((), ()))
MIB = 1024 * 1024


def smem():
    return pl.BlockSpec(memory_space=pltpu.SMEM)


def vmem():
    return pl.BlockSpec(memory_space=pltpu.VMEM)


def anywhere():
    return pl.BlockSpec(memory_space=pl.ANY)


def call(kernel, outs, ins, scratch, cost, mib):
    single = not isinstance(outs, (list, tuple))
    return pl.pallas_call(
        kernel,
        out_shape=outs,
        in_specs=ins,
        out_specs=vmem() if single else [vmem()] * len(outs),
        scratch_shapes=scratch,
        compiler_params=pltpu.CompilerParams(vmem_limit_bytes=mib * MIB),
        cost_estimate=pl.CostEstimate(flops=cost[0], bytes_accessed=cost[1], transcendentals=0),
    )


def gather_pieces(pieces, sems):
    copies = [
        pltpu.make_async_copy(source, target, sems.at[i]) for i, (source, target) in enumerate(pieces)
    ]
    for copy in copies:
        copy.start()
    return copies


def wait_all(copies):
    for copy in copies:
        copy.wait()


def offset(value, unit):
    return pl.multiple_of(value, unit)


def cut_kernel(at, gate, up, down, p0, p1, p2, p3, sems):
    core, at_x = at[0], at[1]
    ff, half = gate.shape[0], p0.shape[1]
    pieces = []
    for d, out in ((1, p1), (3, p3), (2, p2), (0, p0)):
        begin = offset((at_x + d) % X * (2 * half) + core * half, 128)
        for part, source in enumerate((gate, up, down)):
            pieces.append((source.at[:, pl.ds(begin, half)], out.at[pl.ds(part * ff, ff)]))
    wait_all(gather_pieces(pieces, sems))


def cut(at, gate_t, up_t, down):
    ff, width = gate_t.shape
    return call(
        cut_kernel,
        [jax.ShapeDtypeStruct((3 * ff, width // X // 2), bf16)] * X,
        [smem()] + [anywhere()] * 3,
        [pltpu.SemaphoreType.DMA((3 * X,))],
        (0, 6 * ff * width),
        58,
    )(at, gate_t, up_t, down)


def attend_kernel(
    counts, tails, order, q_ref, new_ref, kv_ref, out_ref, score, top, total, mixed
):
    rows, heads, size = q_ref.shape
    pool, block, _ = kv_ref.shape
    scale = size ** (-0.5)
    owner, limit = [], []
    row, rank = jnp.int32(0), jnp.int32(0)
    for p in range(pool):
        last = rank + 1 == counts[0, row]
        owner.append(row)
        limit.append(jnp.where(last, tails[row], block))
        row = jnp.minimum(jnp.where(last, row + 1, row), rows - 1)
        rank = jnp.where(last, 0, rank + 1)
    own = []
    for r in range(rows):
        key = new_ref[r : r + 1, :size].astype(f32)
        own.append(jnp.sum(q_ref[r].astype(f32) * key, axis=1, keepdims=True) * scale)
        top[r] = jnp.broadcast_to(own[r], (heads, 128))
    lane = lax.broadcasted_iota(jnp.int32, (heads, block), 1)
    for p in range(pool):
        s = lax.dot_general(
            q_ref[owner[p]], kv_ref[order[0, p], :, :size], NT, preferred_element_type=f32
        )
        s = jnp.where(lane < limit[p], s * scale, -jnp.inf)
        score[p] = s
        top[owner[p]] = jnp.maximum(top[owner[p]], jnp.max(s, axis=1, keepdims=True))
    for r in range(rows):
        weight = jnp.exp(own[r] - top[r][:, :1])
        total[r] = jnp.broadcast_to(weight, (heads, 128))
        mixed[r] = weight * new_ref[r : r + 1, size:].astype(f32)
    for p in range(pool):
        weight = jnp.exp(score[p] - top[owner[p]][:, :1])
        total[owner[p]] += jnp.sum(weight, axis=1, keepdims=True)
        mixed[owner[p]] += jnp.dot(
            weight.astype(bf16), kv_ref[order[0, p], :, size:], preferred_element_type=f32
        )
    for r in range(rows):
        out_ref[r] = (mixed[r] / total[r][:, :1]).astype(bf16)


def attend(queries, new_kv, kv_cache, block_counts, tail_lens, block_order):
    rows = queries.shape[0]
    pool, block, twice = kv_cache.shape
    size = twice // 2
    heads = queries.shape[1] // size
    mixed = call(
        attend_kernel,
        jax.ShapeDtypeStruct((rows, heads, size), bf16),
        [smem()] * 3 + [vmem()] * 3,
        [
            pltpu.VMEM((pool, heads, block), f32),
            pltpu.VMEM((rows, heads, 128), f32),
            pltpu.VMEM((rows, heads, 128), f32),
            pltpu.VMEM((rows, heads, size), f32),
        ],
        (4 * pool * heads * block * size, pool * block * twice * 2),
        58,
    )(block_counts, tail_lens, block_order, queries.reshape(rows, heads, size), new_kv, kv_cache)
    return mixed.reshape(rows, heads * size)


def join_kernel(*refs):
    sources, out, sems = refs[:-2], refs[-2], refs[-1]
    pieces, row = [], 0
    for source in sources:
        pieces.append((source, out.at[pl.ds(row, source.shape[0])]))
        row += source.shape[0]
    wait_all(gather_pieces(pieces, sems))


def join(pieces):
    shape = (sum(piece.shape[0] for piece in pieces), pieces[0].shape[1])
    return call(
        join_kernel,
        jax.ShapeDtypeStruct(shape, bf16),
        [anywhere()] * len(pieces),
        [pltpu.SemaphoreType.DMA((len(pieces),))],
        (0, shape[0] * shape[1] * 4),
        58,
    )(*pieces)


def project_kernel(
    at, first, near, near_far, side, side_far, own_out, o1, o2, o3, weight, heads, sems
):
    core, at_y = at[0], at[3]
    cols, half = near.shape[0] // X, near.shape[1]
    width = 2 * half
    pieces = [(first.at[:, pl.ds(0, width)], heads)]
    for which, c, y in (
        (near, core, at_y),
        (side, core, 1 - at_y),
        (near_far, 1 - core, at_y),
        (side_far, 1 - core, 1 - at_y),
    ):
        rows = pl.ds(offset(y * X * cols, 16), X * cols)
        pieces.append((which, weight.at[rows, pl.ds(offset(c * half, 128), half)]))
    wait_all(gather_pieces(pieces, sems))
    for y in range(Y):
        got = lax.dot_general(
            weight[y * X * cols : (y + 1) * X * cols], heads[...], NT, preferred_element_type=f32
        )
        for d, out in enumerate((own_out, o1, o2, o3)):
            out[y * cols : (y + 1) * cols] = got[d * cols : (d + 1) * cols].astype(out.dtype)


def norm_kernel(first, own, r1, r2, r3, gain, second, proj_out):
    cols = own.shape[0]
    width = first.shape[1] - 256
    proj = own[...] + r1[...].astype(f32) + r2[...].astype(f32) + r3[...].astype(f32)
    resid = first[:, width:].astype(f32).T
    stream = proj + resid[:cols]
    squares = jnp.sum(stream * stream, axis=0, keepdims=True)
    high = squares.astype(bf16).astype(f32)
    line = lax.broadcasted_iota(jnp.int32, (8, stream.shape[1]), 0)
    tail = jnp.where(line == 0, high, jnp.where(line == 1, squares - high, 0.0)).astype(bf16)
    scaled = (stream * gain[...]).astype(bf16)
    for z in range(Z):
        second[z, :cols] = scaled
        second[z, cols:] = tail
    proj_out[...] = jnp.concatenate(
        [proj, jnp.zeros((256 - cols, proj.shape[1]), f32)], axis=0
    ).T


def sources_of(at, own, far):
    return [(which, c) for a, b in zip(own, far) for which, c in ((a, at[0]), (b, 1 - at[0]))]


def gate_up_kernel(
    at, second, w0, w1, w2, w3, f0, f1, f2, f3,
    own_out, o1, o2, o3, weight, normed, columns, total, sems,
):
    at_x, at_y = at[1], at[3]
    both, half = X // 2, w0.shape[1]
    ff = w0.shape[0] // (3 * both)
    ff2 = 2 * ff
    span = X * Y * ff
    cols = normed.shape[0] // Z
    pieces = [
        (second.at[z, pl.ds(0, cols)], normed.at[pl.ds(z * cols, cols)]) for z in range(Z)
    ]
    for i, (which, c) in enumerate(sources_of(at, (w0, w1, w2, w3), (f0, f1, f2, f3))):
        lanes = pl.ds(offset(c * half, 128), half)
        for j in range(both):
            rows = pl.ds((i // 2 * both + j) * ff2, ff2)
            pieces.append((which.at[pl.ds(j * 3 * ff, ff2)], weight.at[rows, lanes]))
    copies = gather_pieces(pieces, sems)
    squares = jnp.sum(second[:, cols : cols + 8].astype(f32), axis=0).T
    squares = squares[:, 0:1] + squares[:, 1:2]
    high = squares.astype(bf16).astype(f32)
    lane = lax.broadcasted_iota(jnp.int32, (squares.shape[0], 128), 1)
    total[:, 2 * span :] = jnp.where(
        lane == 0, high, jnp.where(lane == 1, squares - high, 0.0)
    )
    wait_all(copies[:Z])
    for s in range(Y):
        y = at_y if s == 0 else 1 - at_y
        for d in range(X):
            i = s * X + d
            if i % both == 0:
                wait_all(copies[Z + 2 * i : Z + 2 * (i + both)])
            got = jnp.dot(
                weight[i * ff2 : (i + 1) * ff2], normed[...], preferred_element_type=f32
            )
            block = (y * X + (at_x + X - d) % X) * ff
            columns[pl.ds(offset(block, 16), ff)] = got[:ff]
            columns[pl.ds(offset(span + block, 16), ff)] = got[ff:]
    step = 384
    for i in range(2 * span // step):
        rows = slice(i * step, (i + 1) * step)
        total[:, rows] = columns[rows].T
    for e, out in enumerate((own_out, o1, o2, o3)):
        to = (at_x + e) % X
        for z in range(0, Z, 2):
            pair = [total[pl.ds(offset(((z + i) * X + to) * 8, 8), 8)] for i in range(2)]
            out[z * 8 : (z + 2) * 8] = jnp.concatenate(pair, axis=0).astype(out.dtype)


def act_kernel(width, own, r1, r2, r3, hidden):
    span = hidden.shape[1]
    summed = own[...] + r1[...].astype(f32) + r2[...].astype(f32) + r3[...].astype(f32)
    squares = summed[:, 2 * span : 2 * span + 1] + summed[:, 2 * span + 1 : 2 * span + 2]
    scale = lax.rsqrt(squares / width + norm_eps)
    gate, up = summed[:, :span] * scale, summed[:, span : 2 * span] * scale
    hidden[...] = (gate / (1.0 + jnp.exp(-gate)) * up).astype(bf16)


def down_kernel(
    at, h0, h1, h2, h3, proj, w0, w1, w2, w3, f0, f1, f2, f3, out, weight, act, total, sems
):
    at_x, at_z, at_y = at[1], at[2], at[3]
    both, half = X // 2, w0.shape[1]
    width = 2 * half
    ff = w0.shape[0] // (3 * both)
    rows = h0.shape[0]
    pieces = []
    for i, (which, c) in enumerate(sources_of(at, (w0, w1, w2, w3), (f0, f1, f2, f3))):
        lanes = pl.ds(offset(c * half, 128), half)
        y = at_y if i // 4 == 0 else 1 - at_y
        for j in range(both):
            d = i // 2 % 2 * both + j
            block = (y * X + (at_x + X - d) % X) * ff
            pieces.append(
                (
                    which.at[pl.ds((3 * j + 2) * ff, ff)],
                    weight.at[pl.ds(offset(block, 16), ff), lanes],
                )
            )
    copies = gather_pieces(pieces, sems)
    for e, h in enumerate((h0, h1, h2, h3)):
        act[pl.ds(offset((at_x + X - e) % X * rows, 16), rows)] = h[...]
    spot = at_z * 224
    base = jnp.minimum(spot // 128 * 128, width - 384)
    row = lax.broadcasted_iota(jnp.int32, (256, 384), 0)
    lane = lax.broadcasted_iota(jnp.int32, (256, 384), 1)
    pick = jnp.where(row < 224, (row + (spot - base) == lane).astype(f32), 0.0).astype(bf16)
    placed = jnp.dot(proj[...].astype(bf16), pick, preferred_element_type=f32)
    wait_all(copies)
    got = jnp.dot(act[...], weight[...], preferred_element_type=f32)
    for z in range(Z):
        for x in range(X):
            at_row = x * rows + z * 8
            total[(z * X + x) * 8 : (z * X + x + 1) * 8] = got[at_row : at_row + 8]
    total[:, pl.ds(offset(base, 128), 384)] += placed
    out[...] = total[...].astype(bf16).reshape(out.shape)


def shifted(value, axis, step):
    size = lax.axis_size(axis)
    return lax.ppermute(value, axis, [(i, (i + step) % size) for i in range(size)])


def around(low, high):
    size = lax.axis_size("role") * Y
    up = [(i, (i + 1) % size) for i in range(size)]
    return (
        lax.ppermute(low, ("role", "y"), up),
        lax.ppermute(high, ("role", "y"), [(b, a) for a, b in up]),
    )


def pair(values):
    return [shifted(value, "pair", 1) for value in values]


def after(values, *others):
    return lax.optimization_barrier((values, others))[0]


def lanes(weight, begin, size):
    return lax.dynamic_slice_in_dim(weight, begin, size, 1)


def per_device(
    hidden_in,
    queries,
    new_kv,
    kv_cache,
    block_counts,
    tail_lens,
    block_order,
    out_weight,
    norm_gain,
    gate_weight,
    up_weight,
    down_weight,
):
    core, at_x, at_z, at_y = (lax.axis_index(a) for a in ("pair", "x", "z", "y"))
    at = jnp.stack([core, at_x, at_z, at_y])
    rows, width = hidden_in.shape
    slab = width // X
    block = width // (X * Z * Y)
    cols = Y * block
    chunk = X * Z * rows
    ff = gate_weight.shape[1]
    span = X * Y * ff
    heads = queries.shape[1] // X
    out_t, gate_t, up_t = out_weight.T, gate_weight.T, up_weight.T

    half = heads // 2
    pieces = [lanes(out_t, (at_x + d) % X * heads + core * half, half) for d in range(X)]
    out_pieces = [pieces[0]] + [shifted(pieces[d], "x", d) for d in range(1, X)]
    gain = shifted(norm_gain, "y", 1)
    gain = jnp.where(
        at_y == 0, jnp.concatenate([norm_gain, gain]), jnp.concatenate([gain, norm_gain])
    )[:, None]

    attended = attend(queries, new_kv, kv_cache, block_counts, tail_lens, block_order)
    first = jnp.concatenate(
        [attended.reshape(rows, X, heads), hidden_in.reshape(rows, X, slab)], axis=2
    ).transpose(1, 0, 2)
    first = after(first, (out_pieces, gain))
    pieces = cut(at, *after((gate_t, up_t, down_weight), first))
    first = lax.all_to_all(first, "x", 0, 0, tiled=True).reshape(X * rows, heads + slab)
    resid = first[:, heads:].reshape(X * rows, Z, cols).transpose(1, 0, 2)
    resid = jnp.pad(resid, ((0, 0), (0, 0), (0, 256 - cols)))
    first = jnp.concatenate(
        [jnp.broadcast_to(first[None, :, :heads], (Z, X * rows, heads)), resid], axis=2
    )
    first = lax.all_to_all(first, "z", 0, 0, tiled=True).reshape(chunk, heads + 256)

    out_near = join(out_pieces)
    out_side = shifted(out_near, "y", 1)
    out_all = [out_near, *pair([out_near]), out_side, *pair([out_side])]
    moved = [shifted(pieces[1], "x", 1), shifted(pieces[3], "x", -1)]
    across = shifted(after(pieces[2], moved), "x", 2)

    own, *sends = call(
        project_kernel,
        [jax.ShapeDtypeStruct((cols, chunk), t) for t in (f32, bf16, bf16, bf16)],
        [smem()] + [anywhere()] * 5,
        [
            pltpu.VMEM((X * cols, heads), bf16),
            pltpu.VMEM((chunk, heads), bf16),
            pltpu.SemaphoreType.DMA((5,)),
        ],
        (2 * X * cols * chunk * heads, X * cols * heads * 4),
        58,
    )(at, first, *out_all)
    received = [shifted(send, "x", -d) for d, send in enumerate(sends, 1)]
    weights = [join([pieces[0], moved[0]]), join([after(across, own), moved[1]])]
    weights += around(*weights)
    second, proj = call(
        norm_kernel,
        [
            jax.ShapeDtypeStruct((Z, cols + 8, chunk), bf16),
            jax.ShapeDtypeStruct((chunk, 256), f32),
        ],
        [vmem()] * 6,
        [],
        (10 * cols * chunk, 20 * cols * chunk),
        58,
    )(first, own, *received, gain)
    weights = after(weights, second)
    weights += pair(weights)
    second = lax.all_to_all(second, "z", 0, 0, tiled=True)

    message = (Z * rows, 2 * span + 128)
    own, *sends = call(
        gate_up_kernel,
        [jax.ShapeDtypeStruct(message, t) for t in (f32, bf16, bf16, bf16)],
        [smem(), vmem()] + [anywhere()] * 8,
        [
            pltpu.VMEM((2 * span, slab), bf16),
            pltpu.VMEM((slab, chunk), bf16),
            pltpu.VMEM((2 * span, chunk), f32),
            pltpu.VMEM((chunk, message[1]), f32),
            pltpu.SemaphoreType.DMA((16 + Z,)),
        ],
        (4 * span * slab * chunk, 2 * span * slab * 4),
        58,
    )(at, second, *weights)
    received = [shifted(send, "x", e) for e, send in enumerate(sends, 1)]
    hidden = call(
        lambda *refs: act_kernel(width, *refs),
        jax.ShapeDtypeStruct((Z * rows, span), bf16),
        [vmem()] * 4,
        [],
        (20 * span * Z * rows, 20 * span * Z * rows),
        8,
    )(own, *received)
    hidden = [hidden] + [shifted(hidden, "x", e) for e in range(1, X)]
    result = call(
        down_kernel,
        jax.ShapeDtypeStruct((Z, X * rows, slab), bf16),
        [smem()] + [vmem()] * 5 + [anywhere()] * 8,
        [
            pltpu.VMEM((span, slab), bf16),
            pltpu.VMEM((chunk, span), bf16),
            pltpu.VMEM((chunk, slab), f32),
            pltpu.SemaphoreType.DMA((16,)),
        ],
        (2 * span * chunk * slab, span * slab * 4),
        58,
    )(at, *hidden, proj, *weights)
    result = lax.all_to_all(result, "z", 0, 0, tiled=True)
    result = jnp.sum(result.astype(f32), axis=0).reshape(X, rows, slab)
    result = lax.all_to_all(result, "x", 0, 0, tiled=True)
    result = result.transpose(1, 0, 2).reshape(rows, width)
    return (result + hidden_in.astype(f32)).astype(bf16)


def solution(mesh):
    fine = Mesh(mesh.devices.reshape(2, 2, X, Z, Y), ("role", "pair", "x", "z", "y"))
    dev = ("x", "z", "y")
    every = ("role", "pair") + dev
    return jax.shard_map(
        per_device,
        mesh=fine,
        in_specs=(
            P(every, None),
            P(every, None),
            P(every, None),
            P(every, None, None),
            P(every, None),
            P(every),
            P(every, None),
            P(None, dev),
            P(dev),
            P(None, dev),
            P(None, dev),
            P(dev, None),
        ),
        out_specs=P(every, None),
        check_vma=False,
    )
```

time: 232 us -> 214 us (0.922)
  blocking collectives: 0 us -> 47.4 us
  waiting for transfers between devices: 109 us -> 72.2 us
  starting transfers between devices: 59.3 us -> 40.9 us
  Pallas kernels: 48.2 us -> 39.5 us
    all_to_all x0 -> x3, blocking collectives: none -> 47.4 us  [the longest x1 29.6 us: per_device(): result = lax.all_to_all(result, 'z', 0, 0, tiled=True)]
    all_to_all x2 -> x0, waiting for transfers between devices: 26.5 us -> none  [the longest x1 26 us: per_device(): result = lax.all_to_all(result, 'z', 0, 0, tiled=True)]
    ppermute x26 -> x23, starting transfers between devices: 35.4 us -> 23.6 us  [shifted(): lax.ppermute(value, axis, [(i, (i + step) % size) for i in range(size)])]
    all_to_all x1, waiting for transfers between devices: 24.4 us -> 16.9 us  [per_device(): second = lax.all_to_all(second, 'z', 0, 0, tiled=True)]
    all_to_all x2 -> x0, starting transfers between devices: 6.96 us -> none  [the longest x1 3.56 us: per_device(): result = lax.all_to_all(result, 'z', 0, 0, tiled=True)]
    all_to_all x1, waiting for transfers between devices: 6.52 us -> 0.01 us  [per_device(): lax.all_to_all(first, 'z', 0, 0, tiled=True).reshape(chunk, heads + 256)]
    pallas_call x4 -> x3, Pallas kernels: 11.5 us -> 7.66 us  [join(): call(join_kernel, jax.ShapeDtypeStruct(shape, bf16), [anywhere()] * len(p...]
    ppermute x26 -> x23, waiting for transfers between devices: 51.5 us -> 55.3 us  [shifted(): lax.ppermute(value, axis, [(i, (i + step) % size) for i in range(size)])]
  transfers between devices with their start and end apart: 30 -> 27, of which waited for: 15 -> 14; matrix products, arithmetic and copies ran while one was open for 2% -> 3% of each run, Pallas kernels for 15% -> 11%
where the time goes in v5:
time: 214 us; the launch traced here: 212 us
  waiting for transfers between devices  72.2 us (34%)
  blocking collectives  47.4 us (22%)
  starting transfers between devices  40.9 us (19%)
  Pallas kernels  39.5 us (18%)
  local copies, waits for them, and re-layouts  8.15 us (4%)
  other arithmetic  3.34 us (2%)
    ppermute x23, waiting for transfers between devices, shifted(): lax.ppermute(value, axis, [(i, (i + step) % size) for i in range(size)])  55.3 us
    all_to_all x1, blocking collectives, per_device(): result = lax.all_to_all(result, 'z', 0, 0, tiled=True)  29.6 us
    ppermute x23, starting transfers between devices, shifted(): lax.ppermute(value, axis, [(i, (i + step) % size) for i in range(size)])  23.6 us
    all_to_all x1, waiting for transfers between devices, per_device(): second = lax.all_to_all(second, 'z', 0, 0, tiled=True)  16.9 us
    all_to_all x1, blocking collectives, per_device(): lax.all_to_all(first, 'x', 0, 0, tiled=True).reshape(X * rows, heads + slab)  8.97 us
    all_to_all x1, blocking collectives, per_device(): result = lax.all_to_all(result, 'x', 0, 0, tiled=True)  8.88 us
    pallas_call x1, Pallas kernels, per_device(): call(gate_up_kernel, [jax.ShapeDtypeStruct(message, t) for t in (f32, bf1...  8.84 us
    all_to_all x1, starting transfers between devices, per_device(): lax.all_to_all(first, 'z', 0, 0, tiled=True).reshape(chunk, heads + 256)  8.47 us
  transfers between devices with their start and end apart: 27, of which 14 were waited for; matrix products, arithmetic and copies ran while one was open for 3% of the time, Pallas kernels for 11%

profile of v5, /device:TPU:16, one launch (start us, length us, event | category | flops | bytes accessed | tf_op | source)
XLA Modules:
  0.0 211.8 jit_solution(16548936852079515105)
XLA Ops:
  3.3 2.8 %collective-permute-start.2 = (bf16[112,1024]{1,0:T(8,128)(2,1)S(1)}, bf16[112,1024]{1,0:T(8,128)(2,1)S(1)}, u32[]{:S(2)}, u32[]{:S(2)}) collective-permute-start(bf16[112,1024]{1,0:T(8,128)(2,1)S(1)} %get-tuple-element.53), channel_id=1, source_target_pairs={{0,48},{16,0},{32,16},{48,32},{1,49},{17,1},{33,17},{49,33},{2,50}... | collective-permute-start | bytes 688136 | tf_op jit(solution)/shard_map/ppermute | solution.py:313
  9.0 4.4 %shard_map.118 = bf16[8,32,256]{2,1,0:T(8,128)(2,1)} custom-call(s32[1,8]{1,0:T(1,128)} %counts.1, s32[8]{0:T(128)} %tails.1, s32[1,16]{1,0:T(1,128)} %order.1, bf16[8,32,256]{2,1,0:T(8,128)(2,1)} %bitcast.39, bf16[8,512]{1,0:T(8,128)(2,1)} %new_ref.1, bf16[16,256,512]{2,1,0:T(8,128)(2,1)} %kv_ref.1), custom_call_target="tpu_custom_call" | custom-call | flops 134217728 | bytes 4194304 | tf_op jit(solution)/shard_map/pallas_call | solution.py:128
  15.6 3.4 %collective-permute-done.refs_1_ = bf16[112,1024]{1,0:T(8,128)(2,1)S(1)} collective-permute-done((bf16[112,1024]{1,0:T(8,128)(2,1)S(1)}, bf16[112,1024]{1,0:T(8,128)(2,1)S(1)}, u32[]{:S(2)}, u32[]{:S(2)}) %collective-permute-start) | collective-permute-done | bytes 229408 | tf_op jit(solution)/shard_map/ppermute | solution.py:313
  19.0 9.0 %all_to_all.25 = bf16[4,8,3840]{2,1,0:T(8,128)(2,1)S(1)} all-to-all(bf16[4,8,3840]{2,1,0:T(8,128)(2,1)S(1)} %maximum_bitcast_fusion), channel_id=1, replica_groups=mesh['role'=2,'pair'=2,'x'=4,'z'=8,'y'=2] {'x'}, dimensions={0} | all-to-all | bytes 491520 | tf_op jit(solution)/shard_map/all_to_all | solution.py:377
  29.5 8.5 %all-to-all-start.1 = ((bf16[8,32,2304]{2,1,0:T(8,128)(2,1)}), bf16[8,32,2304]{2,1,0:T(8,128)(2,1)S(1)}, u32[]{:S(2)}, u32[]{:S(2)}) async-start(bf16[8,32,2304]{2,1,0:T(8,128)(2,1)} %fusion.1), calls=%async_computation.1 | async-start | bytes 2359296 | tf_op jit(solution)/shard_map/all_to_all | solution.py:383
  41.7 4.5 %shard_map.122 = (bf16[432,896]{1,0:T(8,128)(2,1)}, bf16[432,896]{1,0:T(8,128)(2,1)}, bf16[432,896]{1,0:T(8,128)(2,1)}, bf16[432,896]{1,0:T(8,128)(2,1)}) custom-call(s32[4]{0:T(128)} %pad_add_fusion.at, bf16[144,7168]{1,0:T(8,128)(2,1)} %bitcast.32, bf16[144,7168]{1,0:T(8,128)(2,1)} %bitcast.33, bf16[144,7168]{1,0:T(8,128)(2,1)} %down), custom_call_target="tpu_custom_call" | custom-call | bytes 6193152 | tf_op jit(solution)/shard_map/pallas_call | solution.py:72
  49.5 9.4 %collective-permute-done.5.side = bf16[448,1024]{1,0:T(8,128)(2,1)S(1)} collective-permute-done((bf16[448,1024]{1,0:T(8,128)(2,1)}, bf16[448,1024]{1,0:T(8,128)(2,1)S(1)}, u32[]{:S(2)}, u32[]{:S(2)}) %collective-permute-start.5) | collective-permute-done | bytes 917536 | tf_op jit(solution)/shard_map/ppermute | solution.py:313
  59.0 3.8 %collective-permute-done.10.refs_1_ = bf16[432,896]{1,0:T(8,128)(2,1)S(1)} collective-permute-done((bf16[432,896]{1,0:T(8,128)(2,1)}, bf16[432,896]{1,0:T(8,128)(2,1)S(1)}, u32[]{:S(2)}, u32[]{:S(2)}) %collective-permute-start.10) | collective-permute-done | bytes 774176 | tf_op jit(solution)/shard_map/ppermute | solution.py:313
  62.8 7.7 %collective-permute-done.11.refs_1_ = bf16[432,896]{1,0:T(8,128)(2,1)S(1)} collective-permute-done((bf16[432,896]{1,0:T(8,128)(2,1)}, bf16[432,896]{1,0:T(8,128)(2,1)S(1)}, u32[]{:S(2)}, u32[]{:S(2)}) %collective-permute-start.11) | collective-permute-done | bytes 774176 | tf_op jit(solution)/shard_map/ppermute | solution.py:313
  70.5 2.8 %shard_map.123.w0 = bf16[864,896]{1,0:T(8,128)(2,1)} custom-call(bf16[432,896]{1,0:T(8,128)(2,1)} %get-tuple-element.38.refs_0_, bf16[432,896]{1,0:T(8,128)(2,1)} %copy-done.9), custom_call_target="tpu_custom_call" | custom-call | bytes 3096576 | tf_op jit(solution)/shard_map/pallas_call | solution.py:155
  76.1 4.9 %shard_map.120 = (f32[224,256]{1,0:T(8,128)}, bf16[224,256]{1,0:T(8,128)(2,1)}, bf16[224,256]{1,0:T(8,128)(2,1)}, bf16[224,256]{1,0:T(8,128)(2,1)}) custom-call(s32[4]{0:T(128)} %pad_add_fusion.at, bf16[256,2304]{1,0:T(8,128)(2,1)} %bitcast.30, bf16[448,1024]{1,0:T(8,128)(2,1)} %shard_map.119.near, bf16[448,1024]{1,0:T(8,128)(2,1)} %copy-done.7, ...), custom_call_target="tpu_custom_call" | custom-call | flops 939524096 | bytes 7340032 | tf_op jit(solution)/shard_map/pallas_call | solution.py:391
  81.0 5.7 %collective-permute-done.12.refs_0_ = bf16[432,896]{1,0:T(8,128)(2,1)} collective-permute-done((bf16[432,896]{1,0:T(8,128)(2,1)}, bf16[432,896]{1,0:T(8,128)(2,1)}, u32[]{:S(2)}, u32[]{:S(2)}) %collective-permute-start.12) | collective-permute-done | bytes 774176 | tf_op jit(solution)/shard_map/ppermute | solution.py:313
  89.8 3.5 %collective-permute-start.7 = (bf16[224,256]{1,0:T(8,128)(2,1)S(1)}, bf16[224,256]{1,0:T(8,128)(2,1)S(1)}, u32[]{:S(2)}, u32[]{:S(2)}) collective-permute-start(bf16[224,256]{1,0:T(8,128)(2,1)S(1)} %copy-done.24), channel_id=1, source_target_pairs={{0,48},{16,0},{32,16},{48,32},{1,49},{17,1},{33,17},{49,33},{2,50}... | collective-permute-start | bytes 344072 | tf_op jit(solution)/shard_map/ppermute | solution.py:313
  96.9 2.8 %collective-permute-done.8.r2 = bf16[224,256]{1,0:T(8,128)(2,1)S(1)} collective-permute-done((bf16[224,256]{1,0:T(8,128)(2,1)S(1)}, bf16[224,256]{1,0:T(8,128)(2,1)S(1)}, u32[]{:S(2)}, u32[]{:S(2)}) %collective-permute-start.8) | collective-permute-done | bytes 114720 | tf_op jit(solution)/shard_map/ppermute | solution.py:313
  101.3 2.7 %shard_map.121 = (bf16[8,232,256]{2,1,0:T(8,128)(2,1)}, f32[256,256]{1,0:T(8,128)}) custom-call(bf16[256,2304]{1,0:T(8,128)(2,1)} %bitcast.31, f32[224,256]{1,0:T(8,128)} %get-tuple-element.30.own, bf16[224,256]{1,0:T(8,128)(2,1)} %copy-done.18, bf16[224,256]{1,0:T(8,128)(2,1)} %copy-done.19, bf16[224,256]{1,0:T(8,128)(2,1)} %copy-done.20, ...), custom_call_target="tpu_custom_call" | custom-call | flops 573440 | bytes 1146880 | tf_op jit(solution)/shard_map/pallas_call | solution.py:406
  104.0 6.9 %all-to-all-start.2 = ((bf16[8,232,256]{2,1,0:T(8,128)(2,1)}), bf16[8,232,256]{2,1,0:T(8,128)(2,1)}, u32[]{:S(2)}, u32[]{:S(2)}) async-start(bf16[8,232,256]{2,1,0:T(8,128)(2,1)} %get-tuple-element.34), calls=%async_computation.2 | async-start | bytes 1900544 | tf_op jit(solution)/shard_map/all_to_all | solution.py:419
  112.1 16.9 %all-to-all-done.2.second = bf16[8,232,256]{2,1,0:T(8,128)(2,1)} async-done(((bf16[8,232,256]{2,1,0:T(8,128)(2,1)}), bf16[8,232,256]{2,1,0:T(8,128)(2,1)}, u32[]{:S(2)}, u32[]{:S(2)}) %all-to-all-start.2) | async-done | bytes 950304 | tf_op jit(solution)/shard_map/all_to_all | solution.py:419
  129.0 8.8 %shard_map.125 = (f32[64,2432]{1,0:T(8,128)}, bf16[64,2432]{1,0:T(8,128)(2,1)}, bf16[64,2432]{1,0:T(8,128)(2,1)}, bf16[64,2432]{1,0:T(8,128)(2,1)}) custom-call(s32[4]{0:T(128)} %pad_add_fusion.at, bf16[8,232,256]{2,1,0:T(8,128)(2,1)} %all-to-all-done.2.second, bf16[864,896]{1,0:T(8,128)(2,1)} %shard_map.123.w0, bf16[864,896]{1,0:T(8,128)(2,1)} %shard_map.124.w1, ...), custom_call_target="tpu_custom_call" | custom-call | flops 2113929216 | bytes 16515072 | tf_op jit(solution)/shard_map/pallas_call | solution.py:422
  141.5 9.9 %collective-permute-done.19.refs_1_ = bf16[64,2432]{1,0:T(8,128)(2,1)S(1)} collective-permute-done((bf16[64,2432]{1,0:T(8,128)(2,1)}, bf16[64,2432]{1,0:T(8,128)(2,1)S(1)}, u32[]{:S(2)}, u32[]{:S(2)}) %collective-permute-start.19) | collective-permute-done | bytes 311328 | tf_op jit(solution)/shard_map/ppermute | solution.py:313
  155.0 2.7 %collective-permute-start.24 = (bf16[64,1152]{1,0:T(8,128)(2,1)S(1)}, bf16[64,1152]{1,0:T(8,128)(2,1)S(1)}, u32[]{:S(2)}, u32[]{:S(2)}) collective-permute-start(bf16[64,1152]{1,0:T(8,128)(2,1)S(1)} %shard_map.126.h0), channel_id=1, source_target_pairs={{0,48},{16,0},{32,16},{48,32},{1,49},{17,1},{33,17},{49,33},{2,50}... | collective-permute-start | bytes 442376 | tf_op jit(solution)/shard_map/ppermute | solution.py:313
  158.7 3.3 %collective-permute-done.24.h3 = bf16[64,1152]{1,0:T(8,128)(2,1)S(1)} collective-permute-done((bf16[64,1152]{1,0:T(8,128)(2,1)S(1)}, bf16[64,1152]{1,0:T(8,128)(2,1)S(1)}, u32[]{:S(2)}, u32[]{:S(2)}) %collective-permute-start.24) | collective-permute-done | bytes 147488 | tf_op jit(solution)/shard_map/ppermute | solution.py:313
  166.3 6.2 %shard_map.127 = bf16[8,32,1792]{2,1,0:T(8,128)(2,1)} custom-call(s32[4]{0:T(128)} %pad_add_fusion.at, bf16[64,1152]{1,0:T(8,128)(2,1)} %copy-done.1, bf16[64,1152]{1,0:T(8,128)(2,1)} %copy-done.16, bf16[64,1152]{1,0:T(8,128)(2,1)} %copy-done.15, bf16[64,1152]{1,0:T(8,128)(2,1)} %copy-done.14, f32[256,256]{1,0:T(8,128)} %get-tuple-element.52.proj, ...), custom_call_target="tpu_custom_call" | custom-call | flops 1056964608 | bytes 8257536 | tf_op jit(solution)/shard_map/pallas_call | solution.py:446
  172.5 29.6 %all_to_all.26 = bf16[8,32,1792]{2,1,0:T(8,128)(2,1)S(1)} all-to-all(bf16[8,32,1792]{2,1,0:T(8,128)(2,1)} %shard_map.127), channel_id=1, replica_groups=mesh['role'=2,'pair'=2,'x'=4,'z'=8,'y'=2] {'z'}, dimensions={0} | all-to-all | bytes 1835008 | tf_op jit(solution)/shard_map/all_to_all | solution.py:459
  202.2 8.9 %all_to_all.27 = f32[4,8,1792]{2,1,0:T(8,128)S(1)} all-to-all(f32[4,8,1792]{2,1,0:T(8,128)S(1)} %bitcast.37), channel_id=1, replica_groups=mesh['role'=2,'pair'=2,'x'=4,'z'=8,'y'=2] {'x'}, dimensions={0} | all-to-all | bytes 458752 | tf_op jit(solution)/shard_map/all_to_all | solution.py:461
  (111 shorter events, 42.3 us)
Async XLA Ops:
  0.0 14.5 %collective-permute-start.3 = (f32[112]{0:T(128)}, f32[112]{0:T(128)S(1)}, u32[]{:S(2)}, u32[]{:S(2)}) collective-permute-start(f32[112]{0:T(128)} %param.20), channel_id=1, source_target_pairs={{0,1},{1,0},{2,3},{3,2},{4,5},{5,4},{6,7},{7,6},{8,9},{9,8},{10,11... | collective-permute-start | bytes 1352 | tf_op jit(solution)/shard_map/ppermute | solution.py:313
  3.3 12.3 %collective-permute-start.2 = (bf16[112,1024]{1,0:T(8,128)(2,1)S(1)}, bf16[112,1024]{1,0:T(8,128)(2,1)S(1)}, u32[]{:S(2)}, u32[]{:S(2)}) collective-permute-start(bf16[112,1024]{1,0:T(8,128)(2,1)S(1)} %get-tuple-element.53), channel_id=1, source_target_pairs={{0,48},{16,0},{32,16},{48,32},{1,49},{17,1},{33,17},{49,33},{2,50}... | collective-permute-start | bytes 688136 | tf_op jit(solution)/shard_map/ppermute | solution.py:313
  6.1 12.9 %collective-permute-start = (bf16[112,1024]{1,0:T(8,128)(2,1)S(1)}, bf16[112,1024]{1,0:T(8,128)(2,1)S(1)}, u32[]{:S(2)}, u32[]{:S(2)}) collective-permute-start(bf16[112,1024]{1,0:T(8,128)(2,1)S(1)} %get-tuple-element.54), channel_id=1, source_target_pairs={{0,16},{16,32},{32,48},{48,0},{1,17},{17,33},{33,49},{49,1},{2,18}... | collective-permute-start | bytes 688136 | tf_op jit(solution)/shard_map/ppermute | solution.py:313
  6.1 12.9 %collective-permute-start.1 = (bf16[112,1024]{1,0:T(8,128)(2,1)S(1)}, bf16[112,1024]{1,0:T(8,128)(2,1)S(1)}, u32[]{:S(2)}, u32[]{:S(2)}) collective-permute-start(bf16[112,1024]{1,0:T(8,128)(2,1)S(1)} %get-tuple-element.56), channel_id=1, source_target_pairs={{0,32},{16,48},{32,0},{48,16},{1,33},{17,49},{33,1},{49,17},{2,34}... | collective-permute-start | bytes 688136 | tf_op jit(solution)/shard_map/ppermute | solution.py:313
  29.5 45.3 %all-to-all-start.1 = ((bf16[8,32,2304]{2,1,0:T(8,128)(2,1)}), bf16[8,32,2304]{2,1,0:T(8,128)(2,1)S(1)}, u32[]{:S(2)}, u32[]{:S(2)}) async-start(bf16[8,32,2304]{2,1,0:T(8,128)(2,1)} %fusion.1), calls=%async_computation.1 | async-start | bytes 2359296 | tf_op jit(solution)/shard_map/all_to_all | solution.py:383
  40.2 18.7 %collective-permute-start.5 = (bf16[448,1024]{1,0:T(8,128)(2,1)}, bf16[448,1024]{1,0:T(8,128)(2,1)S(1)}, u32[]{:S(2)}, u32[]{:S(2)}) collective-permute-start(bf16[448,1024]{1,0:T(8,128)(2,1)} %shard_map.119.near), channel_id=1, source_target_pairs={{0,1},{1,0},{2,3},{3,2},{4,5},{5,4},{6,7},{7,6},{8,9},{9,8},{10,11... | collective-permute-start | bytes 2752520 | tf_op jit(solution)/shard_map/ppermute | solution.py:313
  46.2 16.6 %collective-permute-start.10 = (bf16[432,896]{1,0:T(8,128)(2,1)}, bf16[432,896]{1,0:T(8,128)(2,1)S(1)}, u32[]{:S(2)}, u32[]{:S(2)}) collective-permute-start(bf16[432,896]{1,0:T(8,128)(2,1)} %get-tuple-element.39), channel_id=1, source_target_pairs={{0,16},{16,32},{32,48},{48,0},{1,17},{17,33},{33,49},{49,1},{2,18}... | collective-permute-start | bytes 2322440 | tf_op jit(solution)/shard_map/ppermute | solution.py:313
  46.9 23.6 %collective-permute-start.11 = (bf16[432,896]{1,0:T(8,128)(2,1)}, bf16[432,896]{1,0:T(8,128)(2,1)S(1)}, u32[]{:S(2)}, u32[]{:S(2)}) collective-permute-start(bf16[432,896]{1,0:T(8,128)(2,1)} %get-tuple-element.41), channel_id=1, source_target_pairs={{0,48},{16,0},{32,16},{48,32},{1,49},{17,1},{33,17},{49,33},{2,50}... | collective-permute-start | bytes 2322440 | tf_op jit(solution)/shard_map/ppermute | solution.py:313
  49.5 25.2 %collective-permute-start.4 = (bf16[448,1024]{1,0:T(8,128)(2,1)S(1)}, bf16[448,1024]{1,0:T(8,128)(2,1)S(1)}, u32[]{:S(2)}, u32[]{:S(2)}) collective-permute-start(bf16[448,1024]{1,0:T(8,128)(2,1)S(1)} %copy-done.5), channel_id=1, source_target_pairs={{0,64},{64,0},{1,65},{65,1},{2,66},{66,2},{3,67},{67,3},{4,68},{68... | collective-permute-start | bytes 2752520 | tf_op jit(solution)/shard_map/ppermute | solution.py:313
  59.0 15.8 %collective-permute-start.6 = (bf16[448,1024]{1,0:T(8,128)(2,1)S(1)}, bf16[448,1024]{1,0:T(8,128)(2,1)}, u32[]{:S(2)}, u32[]{:S(2)}) collective-permute-start(bf16[448,1024]{1,0:T(8,128)(2,1)S(1)} %collective-permute-done.5.side), channel_id=1, source_target_pairs={{0,64},{64,0},{1,65},{65,1},{2,66},{66,2},{3,67},{67,3},{4,68},{68... | collective-permute-start | bytes 2752520 | tf_op jit(solution)/shard_map/ppermute | solution.py:313
  70.5 16.2 %collective-permute-start.12 = (bf16[432,896]{1,0:T(8,128)(2,1)}, bf16[432,896]{1,0:T(8,128)(2,1)}, u32[]{:S(2)}, u32[]{:S(2)}) collective-permute-start(bf16[432,896]{1,0:T(8,128)(2,1)} %get-tuple-element.42), channel_id=1, source_target_pairs={{0,32},{16,48},{32,0},{48,16},{1,33},{17,49},{33,1},{49,17},{2,34}... | collective-permute-start | bytes 2322440 | tf_op jit(solution)/shard_map/ppermute | solution.py:313
  73.4 37.6 %collective-permute-start.13 = (bf16[864,896]{1,0:T(8,128)(2,1)}, bf16[864,896]{1,0:T(8,128)(2,1)}, u32[]{:S(2)}, u32[]{:S(2)}) collective-permute-start(bf16[864,896]{1,0:T(8,128)(2,1)} %shard_map.123.w0), channel_id=1, source_target_pairs={{0,1},{1,128},{128,129},{129,0},{2,3},{3,130},{130,131},{131,2},{4... | collective-permute-start | bytes 4644872 | tf_op jit(solution)/shard_map/ppermute | solution.py:320
  89.2 21.7 %collective-permute-start.14 = (bf16[864,896]{1,0:T(8,128)(2,1)}, bf16[864,896]{1,0:T(8,128)(2,1)}, u32[]{:S(2)}, u32[]{:S(2)}) collective-permute-start(bf16[864,896]{1,0:T(8,128)(2,1)} %shard_map.124.w1), channel_id=1, source_target_pairs={{1,0},{128,1},{129,128},{0,129},{3,2},{130,3},{131,130},{2,131},{5... | collective-permute-start | bytes 4644872 | tf_op jit(solution)/shard_map/ppermute | solution.py:321
  89.8 7.1 %collective-permute-start.7 = (bf16[224,256]{1,0:T(8,128)(2,1)S(1)}, bf16[224,256]{1,0:T(8,128)(2,1)S(1)}, u32[]{:S(2)}, u32[]{:S(2)}) collective-permute-start(bf16[224,256]{1,0:T(8,128)(2,1)S(1)} %copy-done.24), channel_id=1, source_target_pairs={{0,48},{16,0},{32,16},{48,32},{1,49},{17,1},{33,17},{49,33},{2,50}... | collective-permute-start | bytes 344072 | tf_op jit(solution)/shard_map/ppermute | solution.py:313
  93.3 7.3 %collective-permute-start.9 = (bf16[224,256]{1,0:T(8,128)(2,1)S(1)}, bf16[224,256]{1,0:T(8,128)(2,1)S(1)}, u32[]{:S(2)}, u32[]{:S(2)}) collective-permute-start(bf16[224,256]{1,0:T(8,128)(2,1)S(1)} %copy-done.22), channel_id=1, source_target_pairs={{0,16},{16,32},{32,48},{48,0},{1,17},{17,33},{33,49},{49,1},{2,18}... | collective-permute-start | bytes 344072 | tf_op jit(solution)/shard_map/ppermute | solution.py:313
  104.0 24.9 %all-to-all-start.2 = ((bf16[8,232,256]{2,1,0:T(8,128)(2,1)}), bf16[8,232,256]{2,1,0:T(8,128)(2,1)}, u32[]{:S(2)}, u32[]{:S(2)}) async-start(bf16[8,232,256]{2,1,0:T(8,128)(2,1)} %get-tuple-element.34), calls=%async_computation.2 | async-start | bytes 1900544 | tf_op jit(solution)/shard_map/all_to_all | solution.py:419
  111.0 18.0 %collective-permute-start.15 = (bf16[864,896]{1,0:T(8,128)(2,1)S(1)}, bf16[864,896]{1,0:T(8,128)(2,1)}, u32[]{:S(2)}, u32[]{:S(2)}) collective-permute-start(bf16[864,896]{1,0:T(8,128)(2,1)S(1)} %copy-done.2), channel_id=1, source_target_pairs={{0,64},{64,0},{1,65},{65,1},{2,66},{66,2},{3,67},{67,3},{4,68},{68... | collective-permute-start | bytes 4644872 | tf_op jit(solution)/shard_map/ppermute | solution.py:313
  111.1 17.9 %collective-permute-start.16 = (bf16[864,896]{1,0:T(8,128)(2,1)S(1)}, bf16[864,896]{1,0:T(8,128)(2,1)}, u32[]{:S(2)}, u32[]{:S(2)}) collective-permute-start(bf16[864,896]{1,0:T(8,128)(2,1)S(1)} %copy-done.3), channel_id=1, source_target_pairs={{0,64},{64,0},{1,65},{65,1},{2,66},{66,2},{3,67},{67,3},{4,68},{68... | collective-permute-start | bytes 4644872 | tf_op jit(solution)/shard_map/ppermute | solution.py:313
  111.6 17.4 %collective-permute-start.17 = (bf16[864,896]{1,0:T(8,128)(2,1)}, bf16[864,896]{1,0:T(8,128)(2,1)}, u32[]{:S(2)}, u32[]{:S(2)}) collective-permute-start(bf16[864,896]{1,0:T(8,128)(2,1)} %collective-permute-done.13.w2), channel_id=1, source_target_pairs={{0,64},{64,0},{1,65},{65,1},{2,66},{66,2},{3,67},{67,3},{4,68},{68... | collective-permute-start | bytes 4644872 | tf_op jit(solution)/shard_map/ppermute | solution.py:313
  111.7 17.3 %collective-permute-start.18 = (bf16[864,896]{1,0:T(8,128)(2,1)}, bf16[864,896]{1,0:T(8,128)(2,1)}, u32[]{:S(2)}, u32[]{:S(2)}) collective-permute-start(bf16[864,896]{1,0:T(8,128)(2,1)} %collective-permute-done.14.w3), channel_id=1, source_target_pairs={{0,64},{64,0},{1,65},{65,1},{2,66},{66,2},{3,67},{67,3},{4,68},{68... | collective-permute-start | bytes 4644872 | tf_op jit(solution)/shard_map/ppermute | solution.py:313
  137.8 13.6 %collective-permute-start.19 = (bf16[64,2432]{1,0:T(8,128)(2,1)}, bf16[64,2432]{1,0:T(8,128)(2,1)S(1)}, u32[]{:S(2)}, u32[]{:S(2)}) collective-permute-start(bf16[64,2432]{1,0:T(8,128)(2,1)} %get-tuple-element.49), channel_id=1, source_target_pairs={{0,16},{16,32},{32,48},{48,0},{1,17},{17,33},{33,49},{49,1},{2,18}... | collective-permute-start | bytes 933896 | tf_op jit(solution)/shard_map/ppermute | solution.py:313
  137.9 13.5 %collective-permute-start.20 = (bf16[64,2432]{1,0:T(8,128)(2,1)}, bf16[64,2432]{1,0:T(8,128)(2,1)S(1)}, u32[]{:S(2)}, u32[]{:S(2)}) collective-permute-start(bf16[64,2432]{1,0:T(8,128)(2,1)} %get-tuple-element.50), channel_id=1, source_target_pairs={{0,32},{16,48},{32,0},{48,16},{1,33},{17,49},{33,1},{49,17},{2,34}... | collective-permute-start | bytes 933896 | tf_op jit(solution)/shard_map/ppermute | solution.py:313
  140.2 13.4 %collective-permute-start.21 = (bf16[64,2432]{1,0:T(8,128)(2,1)}, bf16[64,2432]{1,0:T(8,128)(2,1)S(1)}, u32[]{:S(2)}, u32[]{:S(2)}) collective-permute-start(bf16[64,2432]{1,0:T(8,128)(2,1)} %get-tuple-element.51), channel_id=1, source_target_pairs={{0,48},{16,0},{32,16},{48,32},{1,49},{17,1},{33,17},{49,33},{2,50}... | collective-permute-start | bytes 933896 | tf_op jit(solution)/shard_map/ppermute | solution.py:313
  157.7 7.9 %collective-permute-start.22 = (bf16[64,1152]{1,0:T(8,128)(2,1)S(1)}, bf16[64,1152]{1,0:T(8,128)(2,1)S(1)}, u32[]{:S(2)}, u32[]{:S(2)}) collective-permute-start(bf16[64,1152]{1,0:T(8,128)(2,1)S(1)} %shard_map.126.h0), channel_id=1, source_target_pairs={{0,16},{16,32},{32,48},{48,0},{1,17},{17,33},{33,49},{49,1},{2,18}... | collective-permute-start | bytes 442376 | tf_op jit(solution)/shard_map/ppermute | solution.py:313
  (28 other events, 183.9 us)

commit v6 on v5

--- a/solution.py
+++ b/solution.py
@@ -299,13 +299,12 @@
     pick = jnp.where(row < 224, (row + (spot - base) == lane).astype(f32), 0.0).astype(bf16)
     placed = jnp.dot(proj[...].astype(bf16), pick, preferred_element_type=f32)
     wait_all(copies)
-    got = jnp.dot(act[...], weight[...], preferred_element_type=f32)
-    for z in range(Z):
-        for x in range(X):
-            at_row = x * rows + z * 8
-            total[(z * X + x) * 8 : (z * X + x + 1) * 8] = got[at_row : at_row + 8]
-    total[:, pl.ds(offset(base, 128), 384)] += placed
-    out[...] = total[...].astype(bf16).reshape(out.shape)
+    total[...] = jnp.dot(act[...], weight[...], preferred_element_type=f32)
+    lanes = pl.ds(offset(base, 128), 384)
+    for x in range(X):
+        mine = [placed[(z * X + x) * 8 : (z * X + x + 1) * 8] for z in range(Z)]
+        total[x * rows : (x + 1) * rows, lanes] += jnp.concatenate(mine, axis=0)
+    out[...] = total[...].astype(bf16)
 
 
 def shifted(value, axis, step):
@@ -445,7 +444,7 @@
     hidden = [hidden] + [shifted(hidden, "x", e) for e in range(1, X)]
     result = call(
         down_kernel,
-        jax.ShapeDtypeStruct((Z, X * rows, slab), bf16),
+        jax.ShapeDtypeStruct((chunk, slab), bf16),
         [smem()] + [vmem()] * 5 + [anywhere()] * 8,
         [
             pltpu.VMEM((span, slab), bf16),
@@ -456,9 +455,9 @@
         (2 * span * chunk * slab, span * slab * 4),
         58,
     )(at, *hidden, proj, *weights)
-    result = lax.all_to_all(result, "z", 0, 0, tiled=True)
-    result = jnp.sum(result.astype(f32), axis=0).reshape(X, rows, slab)
-    result = lax.all_to_all(result, "x", 0, 0, tiled=True)
+    result = result.reshape(X * Z, rows, slab)
+    result = lax.all_to_all(result, ("x", "z"), 0, 0, tiled=True).reshape(X, Z, rows, slab)
+    result = jnp.sum(result.astype(f32), axis=1)
     result = result.transpose(1, 0, 2).reshape(rows, width)
     return (result + hidden_in.astype(f32)).astype(bf16)
 

time: 214 us -> 206 us (0.963)
  blocking collectives: 47.4 us -> 39.1 us
    all_to_all x2 -> x1, blocking collectives: 38.5 us -> 30.2 us  [per_device(): lax.all_to_all(result, ('x', 'z'), 0, 0, tiled=True)]
  transfers between devices with their start and end apart: 27 -> 27, of which waited for: 14 -> 14; matrix products, arithmetic and copies ran while one was open for 3% -> 3% of each run, Pallas kernels for 11% -> 12%
where the time goes in v6:
time: 206 us; the launch traced here: 204 us
  waiting for transfers between devices  72.2 us (35%)
  starting transfers between devices  40.9 us (20%)
  Pallas kernels  39.5 us (19%)
  blocking collectives  39.1 us (19%)
  local copies, waits for them, and re-layouts  8.15 us (4%)
  other arithmetic  3.33 us (2%)
    ppermute x23, waiting for transfers between devices, shifted(): lax.ppermute(value, axis, [(i, (i + step) % size) for i in range(size)])  55.3 us
    all_to_all x1, blocking collectives, per_device(): lax.all_to_all(result, ('x', 'z'), 0, 0, tiled=True)  30.2 us
    ppermute x23, starting transfers between devices, shifted(): lax.ppermute(value, axis, [(i, (i + step) % size) for i in range(size)])  23.6 us
    all_to_all x1, waiting for transfers between devices, per_device(): second = lax.all_to_all(second, 'z', 0, 0, tiled=True)  16.9 us
    all_to_all x1, blocking collectives, per_device(): lax.all_to_all(first, 'x', 0, 0, tiled=True).reshape(X * rows, heads + slab)  8.97 us
    pallas_call x1, Pallas kernels, per_device(): call(gate_up_kernel, [jax.ShapeDtypeStruct(message, t) for t in (f32, bf1...  8.84 us
    all_to_all x1, starting transfers between devices, per_device(): lax.all_to_all(first, 'z', 0, 0, tiled=True).reshape(chunk, heads + 256)  8.47 us
    pallas_call x3, Pallas kernels, join(): call(join_kernel, jax.ShapeDtypeStruct(shape, bf16), [anywhere()] * len(p...  7.66 us
  transfers between devices with their start and end apart: 27, of which 14 were waited for; matrix products, arithmetic and copies ran while one was open for 3% of the time, Pallas kernels for 12%

profile of v6, /device:TPU:16, one launch (start us, length us, event | category | flops | bytes accessed | tf_op | source)
XLA Modules:
  0.0 203.5 jit_solution(3095767415811333149)
XLA Ops:
  3.3 2.8 %collective-permute-start.2 = (bf16[112,1024]{1,0:T(8,128)(2,1)S(1)}, bf16[112,1024]{1,0:T(8,128)(2,1)S(1)}, u32[]{:S(2)}, u32[]{:S(2)}) collective-permute-start(bf16[112,1024]{1,0:T(8,128)(2,1)S(1)} %get-tuple-element.53), channel_id=1, source_target_pairs={{0,48},{16,0},{32,16},{48,32},{1,49},{17,1},{33,17},{49,33},{2,50}... | collective-permute-start | bytes 688136 | tf_op jit(solution)/shard_map/ppermute | solution.py:312
  9.0 4.4 %shard_map.118 = bf16[8,32,256]{2,1,0:T(8,128)(2,1)} custom-call(s32[1,8]{1,0:T(1,128)} %counts.1, s32[8]{0:T(128)} %tails.1, s32[1,16]{1,0:T(1,128)} %order.1, bf16[8,32,256]{2,1,0:T(8,128)(2,1)} %bitcast.42, bf16[8,512]{1,0:T(8,128)(2,1)} %new_ref.1, bf16[16,256,512]{2,1,0:T(8,128)(2,1)} %kv_ref.1), custom_call_target="tpu_custom_call" | custom-call | flops 134217728 | bytes 4194304 | tf_op jit(solution)/shard_map/pallas_call | solution.py:128
  15.6 3.4 %collective-permute-done.refs_1_ = bf16[112,1024]{1,0:T(8,128)(2,1)S(1)} collective-permute-done((bf16[112,1024]{1,0:T(8,128)(2,1)S(1)}, bf16[112,1024]{1,0:T(8,128)(2,1)S(1)}, u32[]{:S(2)}, u32[]{:S(2)}) %collective-permute-start) | collective-permute-done | bytes 229408 | tf_op jit(solution)/shard_map/ppermute | solution.py:312
  19.0 9.0 %all_to_all.20 = bf16[4,8,3840]{2,1,0:T(8,128)(2,1)S(1)} all-to-all(bf16[4,8,3840]{2,1,0:T(8,128)(2,1)S(1)} %maximum_bitcast_fusion), channel_id=1, replica_groups=mesh['role'=2,'pair'=2,'x'=4,'z'=8,'y'=2] {'x'}, dimensions={0} | all-to-all | bytes 491520 | tf_op jit(solution)/shard_map/all_to_all | solution.py:376
  29.5 8.5 %all-to-all-start.1 = ((bf16[8,32,2304]{2,1,0:T(8,128)(2,1)}), bf16[8,32,2304]{2,1,0:T(8,128)(2,1)S(1)}, u32[]{:S(2)}, u32[]{:S(2)}) async-start(bf16[8,32,2304]{2,1,0:T(8,128)(2,1)} %fusion.1), calls=%async_computation.1 | async-start | bytes 2359296 | tf_op jit(solution)/shard_map/all_to_all | solution.py:382
  41.7 4.5 %shard_map.122 = (bf16[432,896]{1,0:T(8,128)(2,1)}, bf16[432,896]{1,0:T(8,128)(2,1)}, bf16[432,896]{1,0:T(8,128)(2,1)}, bf16[432,896]{1,0:T(8,128)(2,1)}) custom-call(s32[4]{0:T(128)} %pad_add_fusion.at, bf16[144,7168]{1,0:T(8,128)(2,1)} %bitcast.36, bf16[144,7168]{1,0:T(8,128)(2,1)} %bitcast.37, bf16[144,7168]{1,0:T(8,128)(2,1)} %down), custom_call_target="tpu_custom_call" | custom-call | bytes 6193152 | tf_op jit(solution)/shard_map/pallas_call | solution.py:72
  46.9 2.7 %collective-permute-start.11 = (bf16[432,896]{1,0:T(8,128)(2,1)}, bf16[432,896]{1,0:T(8,128)(2,1)S(1)}, u32[]{:S(2)}, u32[]{:S(2)}) collective-permute-start(bf16[432,896]{1,0:T(8,128)(2,1)} %get-tuple-element.41), channel_id=1, source_target_pairs={{0,48},{16,0},{32,16},{48,32},{1,49},{17,1},{33,17},{49,33},{2,50}... | collective-permute-start | bytes 2322440 | tf_op jit(solution)/shard_map/ppermute | solution.py:312
  49.5 9.4 %collective-permute-done.5.side = bf16[448,1024]{1,0:T(8,128)(2,1)S(1)} collective-permute-done((bf16[448,1024]{1,0:T(8,128)(2,1)}, bf16[448,1024]{1,0:T(8,128)(2,1)S(1)}, u32[]{:S(2)}, u32[]{:S(2)}) %collective-permute-start.5) | collective-permute-done | bytes 917536 | tf_op jit(solution)/shard_map/ppermute | solution.py:312
  59.0 3.8 %collective-permute-done.10.refs_1_ = bf16[432,896]{1,0:T(8,128)(2,1)S(1)} collective-permute-done((bf16[432,896]{1,0:T(8,128)(2,1)}, bf16[432,896]{1,0:T(8,128)(2,1)S(1)}, u32[]{:S(2)}, u32[]{:S(2)}) %collective-permute-start.10) | collective-permute-done | bytes 774176 | tf_op jit(solution)/shard_map/ppermute | solution.py:312
  62.8 7.7 %collective-permute-done.11.refs_1_ = bf16[432,896]{1,0:T(8,128)(2,1)S(1)} collective-permute-done((bf16[432,896]{1,0:T(8,128)(2,1)}, bf16[432,896]{1,0:T(8,128)(2,1)S(1)}, u32[]{:S(2)}, u32[]{:S(2)}) %collective-permute-start.11) | collective-permute-done | bytes 774176 | tf_op jit(solution)/shard_map/ppermute | solution.py:312
  70.5 2.8 %shard_map.123.w0 = bf16[864,896]{1,0:T(8,128)(2,1)} custom-call(bf16[432,896]{1,0:T(8,128)(2,1)} %get-tuple-element.38.refs_0_, bf16[432,896]{1,0:T(8,128)(2,1)} %copy-done.9), custom_call_target="tpu_custom_call" | custom-call | bytes 3096576 | tf_op jit(solution)/shard_map/pallas_call | solution.py:155
  76.1 4.9 %shard_map.120 = (f32[224,256]{1,0:T(8,128)}, bf16[224,256]{1,0:T(8,128)(2,1)}, bf16[224,256]{1,0:T(8,128)(2,1)}, bf16[224,256]{1,0:T(8,128)(2,1)}) custom-call(s32[4]{0:T(128)} %pad_add_fusion.at, bf16[256,2304]{1,0:T(8,128)(2,1)} %bitcast.33, bf16[448,1024]{1,0:T(8,128)(2,1)} %shard_map.119.near, bf16[448,1024]{1,0:T(8,128)(2,1)} %copy-done.7, ...), custom_call_target="tpu_custom_call" | custom-call | flops 939524096 | bytes 7340032 | tf_op jit(solution)/shard_map/pallas_call | solution.py:390
  81.0 5.7 %collective-permute-done.12.refs_0_ = bf16[432,896]{1,0:T(8,128)(2,1)} collective-permute-done((bf16[432,896]{1,0:T(8,128)(2,1)}, bf16[432,896]{1,0:T(8,128)(2,1)}, u32[]{:S(2)}, u32[]{:S(2)}) %collective-permute-start.12) | collective-permute-done | bytes 774176 | tf_op jit(solution)/shard_map/ppermute | solution.py:312
  89.8 3.5 %collective-permute-start.7 = (bf16[224,256]{1,0:T(8,128)(2,1)S(1)}, bf16[224,256]{1,0:T(8,128)(2,1)S(1)}, u32[]{:S(2)}, u32[]{:S(2)}) collective-permute-start(bf16[224,256]{1,0:T(8,128)(2,1)S(1)} %copy-done.24), channel_id=1, source_target_pairs={{0,48},{16,0},{32,16},{48,32},{1,49},{17,1},{33,17},{49,33},{2,50}... | collective-permute-start | bytes 344072 | tf_op jit(solution)/shard_map/ppermute | solution.py:312
  96.9 2.8 %collective-permute-done.8.r2 = bf16[224,256]{1,0:T(8,128)(2,1)S(1)} collective-permute-done((bf16[224,256]{1,0:T(8,128)(2,1)S(1)}, bf16[224,256]{1,0:T(8,128)(2,1)S(1)}, u32[]{:S(2)}, u32[]{:S(2)}) %collective-permute-start.8) | collective-permute-done | bytes 114720 | tf_op jit(solution)/shard_map/ppermute | solution.py:312
  101.3 2.7 %shard_map.121 = (bf16[8,232,256]{2,1,0:T(8,128)(2,1)}, f32[256,256]{1,0:T(8,128)}) custom-call(bf16[256,2304]{1,0:T(8,128)(2,1)} %bitcast.34, f32[224,256]{1,0:T(8,128)} %get-tuple-element.30.own, bf16[224,256]{1,0:T(8,128)(2,1)} %copy-done.18, bf16[224,256]{1,0:T(8,128)(2,1)} %copy-done.19, bf16[224,256]{1,0:T(8,128)(2,1)} %copy-done.20, ...), custom_call_target="tpu_custom_call" | custom-call | flops 573440 | bytes 1146880 | tf_op jit(solution)/shard_map/pallas_call | solution.py:405
  104.0 6.9 %all-to-all-start.2 = ((bf16[8,232,256]{2,1,0:T(8,128)(2,1)}), bf16[8,232,256]{2,1,0:T(8,128)(2,1)}, u32[]{:S(2)}, u32[]{:S(2)}) async-start(bf16[8,232,256]{2,1,0:T(8,128)(2,1)} %get-tuple-element.34), calls=%async_computation.2 | async-start | bytes 1900544 | tf_op jit(solution)/shard_map/all_to_all | solution.py:418
  112.1 16.9 %all-to-all-done.2.second = bf16[8,232,256]{2,1,0:T(8,128)(2,1)} async-done(((bf16[8,232,256]{2,1,0:T(8,128)(2,1)}), bf16[8,232,256]{2,1,0:T(8,128)(2,1)}, u32[]{:S(2)}, u32[]{:S(2)}) %all-to-all-start.2) | async-done | bytes 950304 | tf_op jit(solution)/shard_map/all_to_all | solution.py:418
  129.0 8.8 %shard_map.125 = (f32[64,2432]{1,0:T(8,128)}, bf16[64,2432]{1,0:T(8,128)(2,1)}, bf16[64,2432]{1,0:T(8,128)(2,1)}, bf16[64,2432]{1,0:T(8,128)(2,1)}) custom-call(s32[4]{0:T(128)} %pad_add_fusion.at, bf16[8,232,256]{2,1,0:T(8,128)(2,1)} %all-to-all-done.2.second, bf16[864,896]{1,0:T(8,128)(2,1)} %shard_map.123.w0, bf16[864,896]{1,0:T(8,128)(2,1)} %shard_map.124.w1, ...), custom_call_target="tpu_custom_call" | custom-call | flops 2113929216 | bytes 16515072 | tf_op jit(solution)/shard_map/pallas_call | solution.py:421
  141.5 9.9 %collective-permute-done.19.refs_1_ = bf16[64,2432]{1,0:T(8,128)(2,1)S(1)} collective-permute-done((bf16[64,2432]{1,0:T(8,128)(2,1)}, bf16[64,2432]{1,0:T(8,128)(2,1)S(1)}, u32[]{:S(2)}, u32[]{:S(2)}) %collective-permute-start.19) | collective-permute-done | bytes 311328 | tf_op jit(solution)/shard_map/ppermute | solution.py:312
  155.0 2.7 %collective-permute-start.24 = (bf16[64,1152]{1,0:T(8,128)(2,1)S(1)}, bf16[64,1152]{1,0:T(8,128)(2,1)S(1)}, u32[]{:S(2)}, u32[]{:S(2)}) collective-permute-start(bf16[64,1152]{1,0:T(8,128)(2,1)S(1)} %shard_map.126.h0), channel_id=1, source_target_pairs={{0,48},{16,0},{32,16},{48,32},{1,49},{17,1},{33,17},{49,33},{2,50}... | collective-permute-start | bytes 442376 | tf_op jit(solution)/shard_map/ppermute | solution.py:312
  158.7 3.3 %collective-permute-done.24.h3 = bf16[64,1152]{1,0:T(8,128)(2,1)S(1)} collective-permute-done((bf16[64,1152]{1,0:T(8,128)(2,1)S(1)}, bf16[64,1152]{1,0:T(8,128)(2,1)S(1)}, u32[]{:S(2)}, u32[]{:S(2)}) %collective-permute-start.24) | collective-permute-done | bytes 147488 | tf_op jit(solution)/shard_map/ppermute | solution.py:312
  166.3 6.2 %shard_map.127 = bf16[256,1792]{1,0:T(8,128)(2,1)} custom-call(s32[4]{0:T(128)} %pad_add_fusion.at, bf16[64,1152]{1,0:T(8,128)(2,1)} %copy-done.1, bf16[64,1152]{1,0:T(8,128)(2,1)} %copy-done.16, bf16[64,1152]{1,0:T(8,128)(2,1)} %copy-done.15, bf16[64,1152]{1,0:T(8,128)(2,1)} %copy-done.14, f32[256,256]{1,0:T(8,128)} %get-tuple-element.52.proj, ...), custom_call_target="tpu_custom_call" | custom-call | flops 1056964608 | bytes 8257536 | tf_op jit(solution)/shard_map/pallas_call | solution.py:445
  172.5 30.2 %all_to_all.21 = bf16[32,8,1792]{2,1,0:T(8,128)(2,1)S(1)} all-to-all(bf16[32,8,1792]{2,1,0:T(8,128)(2,1)} %bitcast.35), channel_id=1, replica_groups=mesh['role'=2,'pair'=2,'x'=4,'z'=8,'y'=2] {'x','z'}, dimensions={0} | all-to-all | bytes 1835008 | tf_op jit(solution)/shard_map/all_to_all | solution.py:459
  (110 shorter events, 39.7 us)
Async XLA Ops:
  0.0 14.5 %collective-permute-start.3 = (f32[112]{0:T(128)}, f32[112]{0:T(128)S(1)}, u32[]{:S(2)}, u32[]{:S(2)}) collective-permute-start(f32[112]{0:T(128)} %param.20), channel_id=1, source_target_pairs={{0,1},{1,0},{2,3},{3,2},{4,5},{5,4},{6,7},{7,6},{8,9},{9,8},{10,11... | collective-permute-start | bytes 1352 | tf_op jit(solution)/shard_map/ppermute | solution.py:312
  3.3 12.3 %collective-permute-start.2 = (bf16[112,1024]{1,0:T(8,128)(2,1)S(1)}, bf16[112,1024]{1,0:T(8,128)(2,1)S(1)}, u32[]{:S(2)}, u32[]{:S(2)}) collective-permute-start(bf16[112,1024]{1,0:T(8,128)(2,1)S(1)} %get-tuple-element.53), channel_id=1, source_target_pairs={{0,48},{16,0},{32,16},{48,32},{1,49},{17,1},{33,17},{49,33},{2,50}... | collective-permute-start | bytes 688136 | tf_op jit(solution)/shard_map/ppermute | solution.py:312
  6.1 12.9 %collective-permute-start = (bf16[112,1024]{1,0:T(8,128)(2,1)S(1)}, bf16[112,1024]{1,0:T(8,128)(2,1)S(1)}, u32[]{:S(2)}, u32[]{:S(2)}) collective-permute-start(bf16[112,1024]{1,0:T(8,128)(2,1)S(1)} %get-tuple-element.54), channel_id=1, source_target_pairs={{0,16},{16,32},{32,48},{48,0},{1,17},{17,33},{33,49},{49,1},{2,18}... | collective-permute-start | bytes 688136 | tf_op jit(solution)/shard_map/ppermute | solution.py:312
  6.1 12.9 %collective-permute-start.1 = (bf16[112,1024]{1,0:T(8,128)(2,1)S(1)}, bf16[112,1024]{1,0:T(8,128)(2,1)S(1)}, u32[]{:S(2)}, u32[]{:S(2)}) collective-permute-start(bf16[112,1024]{1,0:T(8,128)(2,1)S(1)} %get-tuple-element.56), channel_id=1, source_target_pairs={{0,32},{16,48},{32,0},{48,16},{1,33},{17,49},{33,1},{49,17},{2,34}... | collective-permute-start | bytes 688136 | tf_op jit(solution)/shard_map/ppermute | solution.py:312
  29.5 45.3 %all-to-all-start.1 = ((bf16[8,32,2304]{2,1,0:T(8,128)(2,1)}), bf16[8,32,2304]{2,1,0:T(8,128)(2,1)S(1)}, u32[]{:S(2)}, u32[]{:S(2)}) async-start(bf16[8,32,2304]{2,1,0:T(8,128)(2,1)} %fusion.1), calls=%async_computation.1 | async-start | bytes 2359296 | tf_op jit(solution)/shard_map/all_to_all | solution.py:382
  40.2 18.7 %collective-permute-start.5 = (bf16[448,1024]{1,0:T(8,128)(2,1)}, bf16[448,1024]{1,0:T(8,128)(2,1)S(1)}, u32[]{:S(2)}, u32[]{:S(2)}) collective-permute-start(bf16[448,1024]{1,0:T(8,128)(2,1)} %shard_map.119.near), channel_id=1, source_target_pairs={{0,1},{1,0},{2,3},{3,2},{4,5},{5,4},{6,7},{7,6},{8,9},{9,8},{10,11... | collective-permute-start | bytes 2752520 | tf_op jit(solution)/shard_map/ppermute | solution.py:312
  46.2 16.6 %collective-permute-start.10 = (bf16[432,896]{1,0:T(8,128)(2,1)}, bf16[432,896]{1,0:T(8,128)(2,1)S(1)}, u32[]{:S(2)}, u32[]{:S(2)}) collective-permute-start(bf16[432,896]{1,0:T(8,128)(2,1)} %get-tuple-element.39), channel_id=1, source_target_pairs={{0,16},{16,32},{32,48},{48,0},{1,17},{17,33},{33,49},{49,1},{2,18}... | collective-permute-start | bytes 2322440 | tf_op jit(solution)/shard_map/ppermute | solution.py:312
  46.9 23.6 %collective-permute-start.11 = (bf16[432,896]{1,0:T(8,128)(2,1)}, bf16[432,896]{1,0:T(8,128)(2,1)S(1)}, u32[]{:S(2)}, u32[]{:S(2)}) collective-permute-start(bf16[432,896]{1,0:T(8,128)(2,1)} %get-tuple-element.41), channel_id=1, source_target_pairs={{0,48},{16,0},{32,16},{48,32},{1,49},{17,1},{33,17},{49,33},{2,50}... | collective-permute-start | bytes 2322440 | tf_op jit(solution)/shard_map/ppermute | solution.py:312
  49.5 25.2 %collective-permute-start.4 = (bf16[448,1024]{1,0:T(8,128)(2,1)S(1)}, bf16[448,1024]{1,0:T(8,128)(2,1)S(1)}, u32[]{:S(2)}, u32[]{:S(2)}) collective-permute-start(bf16[448,1024]{1,0:T(8,128)(2,1)S(1)} %copy-done.5), channel_id=1, source_target_pairs={{0,64},{64,0},{1,65},{65,1},{2,66},{66,2},{3,67},{67,3},{4,68},{68... | collective-permute-start | bytes 2752520 | tf_op jit(solution)/shard_map/ppermute | solution.py:312
  59.0 15.8 %collective-permute-start.6 = (bf16[448,1024]{1,0:T(8,128)(2,1)S(1)}, bf16[448,1024]{1,0:T(8,128)(2,1)}, u32[]{:S(2)}, u32[]{:S(2)}) collective-permute-start(bf16[448,1024]{1,0:T(8,128)(2,1)S(1)} %collective-permute-done.5.side), channel_id=1, source_target_pairs={{0,64},{64,0},{1,65},{65,1},{2,66},{66,2},{3,67},{67,3},{4,68},{68... | collective-permute-start | bytes 2752520 | tf_op jit(solution)/shard_map/ppermute | solution.py:312
  70.5 16.2 %collective-permute-start.12 = (bf16[432,896]{1,0:T(8,128)(2,1)}, bf16[432,896]{1,0:T(8,128)(2,1)}, u32[]{:S(2)}, u32[]{:S(2)}) collective-permute-start(bf16[432,896]{1,0:T(8,128)(2,1)} %get-tuple-element.42), channel_id=1, source_target_pairs={{0,32},{16,48},{32,0},{48,16},{1,33},{17,49},{33,1},{49,17},{2,34}... | collective-permute-start | bytes 2322440 | tf_op jit(solution)/shard_map/ppermute | solution.py:312
  73.4 37.6 %collective-permute-start.13 = (bf16[864,896]{1,0:T(8,128)(2,1)}, bf16[864,896]{1,0:T(8,128)(2,1)}, u32[]{:S(2)}, u32[]{:S(2)}) collective-permute-start(bf16[864,896]{1,0:T(8,128)(2,1)} %shard_map.123.w0), channel_id=1, source_target_pairs={{0,1},{1,128},{128,129},{129,0},{2,3},{3,130},{130,131},{131,2},{4... | collective-permute-start | bytes 4644872 | tf_op jit(solution)/shard_map/ppermute | solution.py:319
  89.2 21.7 %collective-permute-start.14 = (bf16[864,896]{1,0:T(8,128)(2,1)}, bf16[864,896]{1,0:T(8,128)(2,1)}, u32[]{:S(2)}, u32[]{:S(2)}) collective-permute-start(bf16[864,896]{1,0:T(8,128)(2,1)} %shard_map.124.w1), channel_id=1, source_target_pairs={{1,0},{128,1},{129,128},{0,129},{3,2},{130,3},{131,130},{2,131},{5... | collective-permute-start | bytes 4644872 | tf_op jit(solution)/shard_map/ppermute | solution.py:320
  89.8 7.1 %collective-permute-start.7 = (bf16[224,256]{1,0:T(8,128)(2,1)S(1)}, bf16[224,256]{1,0:T(8,128)(2,1)S(1)}, u32[]{:S(2)}, u32[]{:S(2)}) collective-permute-start(bf16[224,256]{1,0:T(8,128)(2,1)S(1)} %copy-done.24), channel_id=1, source_target_pairs={{0,48},{16,0},{32,16},{48,32},{1,49},{17,1},{33,17},{49,33},{2,50}... | collective-permute-start | bytes 344072 | tf_op jit(solution)/shard_map/ppermute | solution.py:312
  93.3 7.3 %collective-permute-start.9 = (bf16[224,256]{1,0:T(8,128)(2,1)S(1)}, bf16[224,256]{1,0:T(8,128)(2,1)S(1)}, u32[]{:S(2)}, u32[]{:S(2)}) collective-permute-start(bf16[224,256]{1,0:T(8,128)(2,1)S(1)} %copy-done.22), channel_id=1, source_target_pairs={{0,16},{16,32},{32,48},{48,0},{1,17},{17,33},{33,49},{49,1},{2,18}... | collective-permute-start | bytes 344072 | tf_op jit(solution)/shard_map/ppermute | solution.py:312
  104.0 24.9 %all-to-all-start.2 = ((bf16[8,232,256]{2,1,0:T(8,128)(2,1)}), bf16[8,232,256]{2,1,0:T(8,128)(2,1)}, u32[]{:S(2)}, u32[]{:S(2)}) async-start(bf16[8,232,256]{2,1,0:T(8,128)(2,1)} %get-tuple-element.34), calls=%async_computation.2 | async-start | bytes 1900544 | tf_op jit(solution)/shard_map/all_to_all | solution.py:418
  111.0 18.0 %collective-permute-start.15 = (bf16[864,896]{1,0:T(8,128)(2,1)S(1)}, bf16[864,896]{1,0:T(8,128)(2,1)}, u32[]{:S(2)}, u32[]{:S(2)}) collective-permute-start(bf16[864,896]{1,0:T(8,128)(2,1)S(1)} %copy-done.2), channel_id=1, source_target_pairs={{0,64},{64,0},{1,65},{65,1},{2,66},{66,2},{3,67},{67,3},{4,68},{68... | collective-permute-start | bytes 4644872 | tf_op jit(solution)/shard_map/ppermute | solution.py:312
  111.1 17.9 %collective-permute-start.16 = (bf16[864,896]{1,0:T(8,128)(2,1)S(1)}, bf16[864,896]{1,0:T(8,128)(2,1)}, u32[]{:S(2)}, u32[]{:S(2)}) collective-permute-start(bf16[864,896]{1,0:T(8,128)(2,1)S(1)} %copy-done.3), channel_id=1, source_target_pairs={{0,64},{64,0},{1,65},{65,1},{2,66},{66,2},{3,67},{67,3},{4,68},{68... | collective-permute-start | bytes 4644872 | tf_op jit(solution)/shard_map/ppermute | solution.py:312
  111.6 17.4 %collective-permute-start.17 = (bf16[864,896]{1,0:T(8,128)(2,1)}, bf16[864,896]{1,0:T(8,128)(2,1)}, u32[]{:S(2)}, u32[]{:S(2)}) collective-permute-start(bf16[864,896]{1,0:T(8,128)(2,1)} %collective-permute-done.13.w2), channel_id=1, source_target_pairs={{0,64},{64,0},{1,65},{65,1},{2,66},{66,2},{3,67},{67,3},{4,68},{68... | collective-permute-start | bytes 4644872 | tf_op jit(solution)/shard_map/ppermute | solution.py:312
  111.7 17.3 %collective-permute-start.18 = (bf16[864,896]{1,0:T(8,128)(2,1)}, bf16[864,896]{1,0:T(8,128)(2,1)}, u32[]{:S(2)}, u32[]{:S(2)}) collective-permute-start(bf16[864,896]{1,0:T(8,128)(2,1)} %collective-permute-done.14.w3), channel_id=1, source_target_pairs={{0,64},{64,0},{1,65},{65,1},{2,66},{66,2},{3,67},{67,3},{4,68},{68... | collective-permute-start | bytes 4644872 | tf_op jit(solution)/shard_map/ppermute | solution.py:312
  137.8 13.6 %collective-permute-start.19 = (bf16[64,2432]{1,0:T(8,128)(2,1)}, bf16[64,2432]{1,0:T(8,128)(2,1)S(1)}, u32[]{:S(2)}, u32[]{:S(2)}) collective-permute-start(bf16[64,2432]{1,0:T(8,128)(2,1)} %get-tuple-element.49), channel_id=1, source_target_pairs={{0,16},{16,32},{32,48},{48,0},{1,17},{17,33},{33,49},{49,1},{2,18}... | collective-permute-start | bytes 933896 | tf_op jit(solution)/shard_map/ppermute | solution.py:312
  137.9 13.5 %collective-permute-start.20 = (bf16[64,2432]{1,0:T(8,128)(2,1)}, bf16[64,2432]{1,0:T(8,128)(2,1)S(1)}, u32[]{:S(2)}, u32[]{:S(2)}) collective-permute-start(bf16[64,2432]{1,0:T(8,128)(2,1)} %get-tuple-element.50), channel_id=1, source_target_pairs={{0,32},{16,48},{32,0},{48,16},{1,33},{17,49},{33,1},{49,17},{2,34}... | collective-permute-start | bytes 933896 | tf_op jit(solution)/shard_map/ppermute | solution.py:312
  140.2 13.4 %collective-permute-start.21 = (bf16[64,2432]{1,0:T(8,128)(2,1)}, bf16[64,2432]{1,0:T(8,128)(2,1)S(1)}, u32[]{:S(2)}, u32[]{:S(2)}) collective-permute-start(bf16[64,2432]{1,0:T(8,128)(2,1)} %get-tuple-element.51), channel_id=1, source_target_pairs={{0,48},{16,0},{32,16},{48,32},{1,49},{17,1},{33,17},{49,33},{2,50}... | collective-permute-start | bytes 933896 | tf_op jit(solution)/shard_map/ppermute | solution.py:312
  157.7 7.9 %collective-permute-start.22 = (bf16[64,1152]{1,0:T(8,128)(2,1)S(1)}, bf16[64,1152]{1,0:T(8,128)(2,1)S(1)}, u32[]{:S(2)}, u32[]{:S(2)}) collective-permute-start(bf16[64,1152]{1,0:T(8,128)(2,1)S(1)} %shard_map.126.h0), channel_id=1, source_target_pairs={{0,16},{16,32},{32,48},{48,0},{1,17},{17,33},{33,49},{49,1},{2,18}... | collective-permute-start | bytes 442376 | tf_op jit(solution)/shard_map/ppermute | solution.py:312
  (28 other events, 183.9 us)

commit v7 on v6

--- a/solution.py
+++ b/solution.py
@@ -194,7 +194,7 @@
     stream = proj + resid[:cols]
     squares = jnp.sum(stream * stream, axis=0, keepdims=True)
     high = squares.astype(bf16).astype(f32)
-    line = lax.broadcasted_iota(jnp.int32, (8, stream.shape[1]), 0)
+    line = lax.broadcasted_iota(jnp.int32, (16, stream.shape[1]), 0)
     tail = jnp.where(line == 0, high, jnp.where(line == 1, squares - high, 0.0)).astype(bf16)
     scaled = (stream * gain[...]).astype(bf16)
     for z in range(Z):
@@ -228,7 +228,7 @@
             rows = pl.ds((i // 2 * both + j) * ff2, ff2)
             pieces.append((which.at[pl.ds(j * 3 * ff, ff2)], weight.at[rows, lanes]))
     copies = gather_pieces(pieces, sems)
-    squares = jnp.sum(second[:, cols : cols + 8].astype(f32), axis=0).T
+    squares = jnp.sum(second[:, cols : cols + 16].astype(f32), axis=0).T
     squares = squares[:, 0:1] + squares[:, 1:2]
     high = squares.astype(bf16).astype(f32)
     lane = lax.broadcasted_iota(jnp.int32, (squares.shape[0], 128), 1)
@@ -405,13 +405,13 @@
     second, proj = call(
         norm_kernel,
         [
-            jax.ShapeDtypeStruct((Z, cols + 8, chunk), bf16),
+            jax.ShapeDtypeStruct((Z, cols + 16, chunk), bf16),
             jax.ShapeDtypeStruct((chunk, 256), f32),
         ],
         [vmem()] * 6,
         [],
         (10 * cols * chunk, 20 * cols * chunk),
-        58,
+        8,
     )(first, own, *received, gain)
     weights = after(weights, second)
     weights += pair(weights)
@@ -430,7 +430,7 @@
             pltpu.SemaphoreType.DMA((16 + Z,)),
         ],
         (4 * span * slab * chunk, 2 * span * slab * 4),
-        58,
+        26,
     )(at, second, *weights)
     received = [shifted(send, "x", e) for e, send in enumerate(sends, 1)]
     hidden = call(
@@ -453,7 +453,7 @@
             pltpu.SemaphoreType.DMA((16,)),
         ],
         (2 * span * chunk * slab, span * slab * 4),
-        58,
+        20,
     )(at, *hidden, proj, *weights)
     result = result.reshape(X * Z, rows, slab)
     result = lax.all_to_all(result, ("x", "z"), 0, 0, tiled=True).reshape(X, Z, rows, slab)

time: 206 us -> 200 us (0.971)
  Pallas kernels: 39.5 us -> 33.9 us
    pallas_call x1, Pallas kernels: 2.72 us -> 0.22 us  [per_device(): call(norm_kernel, [jax.ShapeDtypeStruct((Z, cols + 16, chunk), bf16), jax...]
    unnamed x52 -> x46, local copies, waits for them, and re-layouts: 4.48 us -> 3.64 us
  transfers between devices with their start and end apart: 27 -> 27, of which waited for: 14 -> 16; matrix products, arithmetic and copies ran while one was open for 3% -> 2% of each run, Pallas kernels for 12% -> 11%
where the time goes in v7:
time: 200 us; the launch traced here: 198 us
  waiting for transfers between devices  72 us (36%)
  blocking collectives  41 us (20%)
  starting transfers between devices  40.9 us (20%)
  Pallas kernels  33.9 us (17%)
  local copies, waits for them, and re-layouts  7.33 us (4%)
  other arithmetic  2.68 us (1%)
    ppermute x23, waiting for transfers between devices, shifted(): lax.ppermute(value, axis, [(i, (i + step) % size) for i in range(size)])  54.7 us
    all_to_all x1, blocking collectives, per_device(): lax.all_to_all(result, ('x', 'z'), 0, 0, tiled=True)  32 us
    ppermute x23, starting transfers between devices, shifted(): lax.ppermute(value, axis, [(i, (i + step) % size) for i in range(size)])  23.6 us
    all_to_all x1, waiting for transfers between devices, per_device(): second = lax.all_to_all(second, 'z', 0, 0, tiled=True)  15.3 us
    all_to_all x1, blocking collectives, per_device(): lax.all_to_all(first, 'x', 0, 0, tiled=True).reshape(X * rows, heads + slab)  8.97 us
    all_to_all x1, starting transfers between devices, per_device(): lax.all_to_all(first, 'z', 0, 0, tiled=True).reshape(chunk, heads + 256)  8.47 us
    pallas_call x3, Pallas kernels, join(): call(join_kernel, jax.ShapeDtypeStruct(shape, bf16), [anywhere()] * len(p...  7.76 us
    pallas_call x1, Pallas kernels, per_device(): call(gate_up_kernel, [jax.ShapeDtypeStruct(message, t) for t in (f32, bf1...  7.58 us
  transfers between devices with their start and end apart: 27, of which 16 were waited for; matrix products, arithmetic and copies ran while one was open for 2% of the time, Pallas kernels for 11%

profile of v7, /device:TPU:16, one launch (start us, length us, event | category | flops | bytes accessed | tf_op | source)
XLA Modules:
  0.0 198.1 jit_solution(18067963960102053217)
XLA Ops:
  3.3 2.8 %collective-permute-start.2 = (bf16[112,1024]{1,0:T(8,128)(2,1)S(1)}, bf16[112,1024]{1,0:T(8,128)(2,1)S(1)}, u32[]{:S(2)}, u32[]{:S(2)}) collective-permute-start(bf16[112,1024]{1,0:T(8,128)(2,1)S(1)} %get-tuple-element.53), channel_id=1, source_target_pairs={{0,48},{16,0},{32,16},{48,32},{1,49},{17,1},{33,17},{49,33},{2,50}... | collective-permute-start | bytes 688136 | tf_op jit(solution)/shard_map/ppermute | solution.py:312
  9.1 4.4 %shard_map.118 = bf16[8,32,256]{2,1,0:T(8,128)(2,1)} custom-call(s32[1,8]{1,0:T(1,128)} %counts.1, s32[8]{0:T(128)} %tails.1, s32[1,16]{1,0:T(1,128)} %order.1, bf16[8,32,256]{2,1,0:T(8,128)(2,1)} %bitcast.42, bf16[8,512]{1,0:T(8,128)(2,1)} %new_ref.1, bf16[16,256,512]{2,1,0:T(8,128)(2,1)} %kv_ref.1), custom_call_target="tpu_custom_call" | custom-call | flops 134217728 | bytes 4194304 | tf_op jit(solution)/shard_map/pallas_call | solution.py:128
  15.6 3.4 %collective-permute-done.refs_1_ = bf16[112,1024]{1,0:T(8,128)(2,1)S(1)} collective-permute-done((bf16[112,1024]{1,0:T(8,128)(2,1)S(1)}, bf16[112,1024]{1,0:T(8,128)(2,1)S(1)}, u32[]{:S(2)}, u32[]{:S(2)}) %collective-permute-start) | collective-permute-done | bytes 229408 | tf_op jit(solution)/shard_map/ppermute | solution.py:312
  19.0 9.0 %all_to_all.20 = bf16[4,8,3840]{2,1,0:T(8,128)(2,1)S(1)} all-to-all(bf16[4,8,3840]{2,1,0:T(8,128)(2,1)S(1)} %maximum_bitcast_fusion), channel_id=1, replica_groups=mesh['role'=2,'pair'=2,'x'=4,'z'=8,'y'=2] {'x'}, dimensions={0} | all-to-all | bytes 491520 | tf_op jit(solution)/shard_map/all_to_all | solution.py:376
  29.5 8.5 %all-to-all-start.1 = ((bf16[8,32,2304]{2,1,0:T(8,128)(2,1)}), bf16[8,32,2304]{2,1,0:T(8,128)(2,1)S(1)}, u32[]{:S(2)}, u32[]{:S(2)}) async-start(bf16[8,32,2304]{2,1,0:T(8,128)(2,1)} %fusion.1), calls=%async_computation.1 | async-start | bytes 2359296 | tf_op jit(solution)/shard_map/all_to_all | solution.py:382
  41.7 4.6 %shard_map.122 = (bf16[432,896]{1,0:T(8,128)(2,1)}, bf16[432,896]{1,0:T(8,128)(2,1)}, bf16[432,896]{1,0:T(8,128)(2,1)}, bf16[432,896]{1,0:T(8,128)(2,1)}) custom-call(s32[4]{0:T(128)} %pad_add_fusion.at, bf16[144,7168]{1,0:T(8,128)(2,1)} %bitcast.36, bf16[144,7168]{1,0:T(8,128)(2,1)} %bitcast.37, bf16[144,7168]{1,0:T(8,128)(2,1)} %down), custom_call_target="tpu_custom_call" | custom-call | bytes 6193152 | tf_op jit(solution)/shard_map/pallas_call | solution.py:72
  46.9 2.7 %collective-permute-start.11 = (bf16[432,896]{1,0:T(8,128)(2,1)}, bf16[432,896]{1,0:T(8,128)(2,1)S(1)}, u32[]{:S(2)}, u32[]{:S(2)}) collective-permute-start(bf16[432,896]{1,0:T(8,128)(2,1)} %get-tuple-element.41), channel_id=1, source_target_pairs={{0,48},{16,0},{32,16},{48,32},{1,49},{17,1},{33,17},{49,33},{2,50}... | collective-permute-start | bytes 2322440 | tf_op jit(solution)/shard_map/ppermute | solution.py:312
  49.6 9.4 %collective-permute-done.5.side = bf16[448,1024]{1,0:T(8,128)(2,1)S(1)} collective-permute-done((bf16[448,1024]{1,0:T(8,128)(2,1)}, bf16[448,1024]{1,0:T(8,128)(2,1)S(1)}, u32[]{:S(2)}, u32[]{:S(2)}) %collective-permute-start.5) | collective-permute-done | bytes 917536 | tf_op jit(solution)/shard_map/ppermute | solution.py:312
  59.0 3.9 %collective-permute-done.10.refs_1_ = bf16[432,896]{1,0:T(8,128)(2,1)S(1)} collective-permute-done((bf16[432,896]{1,0:T(8,128)(2,1)}, bf16[432,896]{1,0:T(8,128)(2,1)S(1)}, u32[]{:S(2)}, u32[]{:S(2)}) %collective-permute-start.10) | collective-permute-done | bytes 774176 | tf_op jit(solution)/shard_map/ppermute | solution.py:312
  62.9 7.7 %collective-permute-done.11.refs_1_ = bf16[432,896]{1,0:T(8,128)(2,1)S(1)} collective-permute-done((bf16[432,896]{1,0:T(8,128)(2,1)}, bf16[432,896]{1,0:T(8,128)(2,1)S(1)}, u32[]{:S(2)}, u32[]{:S(2)}) %collective-permute-start.11) | collective-permute-done | bytes 774176 | tf_op jit(solution)/shard_map/ppermute | solution.py:312
  70.6 2.8 %shard_map.123.w0 = bf16[864,896]{1,0:T(8,128)(2,1)} custom-call(bf16[432,896]{1,0:T(8,128)(2,1)} %get-tuple-element.38.refs_0_, bf16[432,896]{1,0:T(8,128)(2,1)} %copy-done.11), custom_call_target="tpu_custom_call" | custom-call | bytes 3096576 | tf_op jit(solution)/shard_map/pallas_call | solution.py:155
  76.7 4.9 %shard_map.120 = (f32[224,256]{1,0:T(8,128)}, bf16[224,256]{1,0:T(8,128)(2,1)}, bf16[224,256]{1,0:T(8,128)(2,1)}, bf16[224,256]{1,0:T(8,128)(2,1)}) custom-call(s32[4]{0:T(128)} %pad_add_fusion.at, bf16[256,2304]{1,0:T(8,128)(2,1)} %bitcast.33, bf16[448,1024]{1,0:T(8,128)(2,1)} %shard_map.119.near, bf16[448,1024]{1,0:T(8,128)(2,1)} %copy-done.9, ...), custom_call_target="tpu_custom_call" | custom-call | flops 939524096 | bytes 7340032 | tf_op jit(solution)/shard_map/pallas_call | solution.py:390
  81.6 5.1 %collective-permute-done.12.refs_0_ = bf16[432,896]{1,0:T(8,128)(2,1)} collective-permute-done((bf16[432,896]{1,0:T(8,128)(2,1)}, bf16[432,896]{1,0:T(8,128)(2,1)}, u32[]{:S(2)}, u32[]{:S(2)}) %collective-permute-start.12) | collective-permute-done | bytes 774176 | tf_op jit(solution)/shard_map/ppermute | solution.py:312
  86.7 2.7 %shard_map.124.w1 = bf16[864,896]{1,0:T(8,128)(2,1)} custom-call(bf16[432,896]{1,0:T(8,128)(2,1)} %collective-permute-done.12.refs_0_, bf16[432,896]{1,0:T(8,128)(2,1)} %copy-done.10), custom_call_target="tpu_custom_call" | custom-call | bytes 3096576 | tf_op jit(solution)/shard_map/pallas_call | solution.py:155
  89.9 3.5 %collective-permute-start.7 = (bf16[224,256]{1,0:T(8,128)(2,1)S(1)}, bf16[224,256]{1,0:T(8,128)(2,1)S(1)}, u32[]{:S(2)}, u32[]{:S(2)}) collective-permute-start(bf16[224,256]{1,0:T(8,128)(2,1)S(1)} %copy-done.21), channel_id=1, source_target_pairs={{0,48},{16,0},{32,16},{48,32},{1,49},{17,1},{33,17},{49,33},{2,50}... | collective-permute-start | bytes 344072 | tf_op jit(solution)/shard_map/ppermute | solution.py:312
  97.1 2.8 %collective-permute-done.8.r2 = bf16[224,256]{1,0:T(8,128)(2,1)S(1)} collective-permute-done((bf16[224,256]{1,0:T(8,128)(2,1)S(1)}, bf16[224,256]{1,0:T(8,128)(2,1)S(1)}, u32[]{:S(2)}, u32[]{:S(2)}) %collective-permute-start.8) | collective-permute-done | bytes 114720 | tf_op jit(solution)/shard_map/ppermute | solution.py:312
  102.0 6.9 %all-to-all-start.2 = ((bf16[8,240,256]{2,1,0:T(8,128)(2,1)}), bf16[8,240,256]{2,1,0:T(8,128)(2,1)}, u32[]{:S(2)}, u32[]{:S(2)}) async-start(bf16[8,240,256]{2,1,0:T(8,128)(2,1)} %copy-done.4), calls=%async_computation.2 | async-start | bytes 1966080 | tf_op jit(solution)/shard_map/all_to_all | solution.py:418
  112.0 15.3 %all-to-all-done.2.second = bf16[8,240,256]{2,1,0:T(8,128)(2,1)} async-done(((bf16[8,240,256]{2,1,0:T(8,128)(2,1)}), bf16[8,240,256]{2,1,0:T(8,128)(2,1)}, u32[]{:S(2)}, u32[]{:S(2)}) %all-to-all-start.2) | async-done | bytes 983072 | tf_op jit(solution)/shard_map/all_to_all | solution.py:418
  127.3 7.6 %shard_map.125 = (f32[64,2432]{1,0:T(8,128)S(1)}, bf16[64,2432]{1,0:T(8,128)(2,1)S(1)}, bf16[64,2432]{1,0:T(8,128)(2,1)S(1)}, bf16[64,2432]{1,0:T(8,128)(2,1)S(1)}) custom-call(s32[4]{0:T(128)S(1)} %copy-done.6, bf16[8,240,256]{2,1,0:T(8,128)(2,1)} %all-to-all-done.2.second, bf16[864,896]{1,0:T(8,128)(2,1)S(1)} %copy-done, bf16[864,896]{1,0:T(8,128)(2,1)S(1)} %copy-done.1, ...), custom_call_target="tpu_custom_call" | custom-call | flops 2113929216 | bytes 16515072 | tf_op jit(solution)/shard_map/pallas_call | solution.py:421
  138.7 10.7 %collective-permute-done.19.refs_1_ = bf16[64,2432]{1,0:T(8,128)(2,1)S(1)} collective-permute-done((bf16[64,2432]{1,0:T(8,128)(2,1)S(1)}, bf16[64,2432]{1,0:T(8,128)(2,1)S(1)}, u32[]{:S(2)}, u32[]{:S(2)}) %collective-permute-start.19) | collective-permute-done | bytes 311328 | tf_op jit(solution)/shard_map/ppermute | solution.py:312
  150.2 2.7 %collective-permute-start.24 = (bf16[64,1152]{1,0:T(8,128)(2,1)S(1)}, bf16[64,1152]{1,0:T(8,128)(2,1)S(1)}, u32[]{:S(2)}, u32[]{:S(2)}) collective-permute-start(bf16[64,1152]{1,0:T(8,128)(2,1)S(1)} %shard_map.126.h0), channel_id=1, source_target_pairs={{0,48},{16,0},{32,16},{48,32},{1,49},{17,1},{33,17},{49,33},{2,50}... | collective-permute-start | bytes 442376 | tf_op jit(solution)/shard_map/ppermute | solution.py:312
  153.8 3.3 %collective-permute-done.24.h3 = bf16[64,1152]{1,0:T(8,128)(2,1)S(1)} collective-permute-done((bf16[64,1152]{1,0:T(8,128)(2,1)S(1)}, bf16[64,1152]{1,0:T(8,128)(2,1)S(1)}, u32[]{:S(2)}, u32[]{:S(2)}) %collective-permute-start.24) | collective-permute-done | bytes 147488 | tf_op jit(solution)/shard_map/ppermute | solution.py:312
  161.0 4.3 %shard_map.127 = bf16[256,1792]{1,0:T(8,128)(2,1)S(1)} custom-call(s32[4]{0:T(128)S(1)} %copy-done.6, bf16[64,1152]{1,0:T(8,128)(2,1)S(1)} %shard_map.126.h0, bf16[64,1152]{1,0:T(8,128)(2,1)S(1)} %collective-permute-done.22.h1, bf16[64,1152]{1,0:T(8,128)(2,1)S(1)} %collective-permute-done.23.h2, bf16[64,1152]{1,0:T(8,128)(2,1)S(1)} %collective-permute-done.24.h3, ...), custom_call_target="tpu_custom_call" | custom-call | flops 1056964608 | bytes 8257536 | tf_op jit(solution)/shard_map/pallas_call | solution.py:445
  165.3 32.0 %all_to_all.21 = bf16[32,8,1792]{2,1,0:T(8,128)(2,1)S(1)} all-to-all(bf16[32,8,1792]{2,1,0:T(8,128)(2,1)S(1)} %bitcast.35), channel_id=1, replica_groups=mesh['role'=2,'pair'=2,'x'=4,'z'=8,'y'=2] {'x','z'}, dimensions={0} | all-to-all | bytes 1835008 | tf_op jit(solution)/shard_map/all_to_all | solution.py:459
  (104 shorter events, 37.1 us)
Async XLA Ops:
  0.0 14.6 %collective-permute-start.3 = (f32[112]{0:T(128)}, f32[112]{0:T(128)S(1)}, u32[]{:S(2)}, u32[]{:S(2)}) collective-permute-start(f32[112]{0:T(128)} %param.20), channel_id=1, source_target_pairs={{0,1},{1,0},{2,3},{3,2},{4,5},{5,4},{6,7},{7,6},{8,9},{9,8},{10,11... | collective-permute-start | bytes 1352 | tf_op jit(solution)/shard_map/ppermute | solution.py:312
  3.3 12.3 %collective-permute-start.2 = (bf16[112,1024]{1,0:T(8,128)(2,1)S(1)}, bf16[112,1024]{1,0:T(8,128)(2,1)S(1)}, u32[]{:S(2)}, u32[]{:S(2)}) collective-permute-start(bf16[112,1024]{1,0:T(8,128)(2,1)S(1)} %get-tuple-element.53), channel_id=1, source_target_pairs={{0,48},{16,0},{32,16},{48,32},{1,49},{17,1},{33,17},{49,33},{2,50}... | collective-permute-start | bytes 688136 | tf_op jit(solution)/shard_map/ppermute | solution.py:312
  6.1 12.9 %collective-permute-start = (bf16[112,1024]{1,0:T(8,128)(2,1)S(1)}, bf16[112,1024]{1,0:T(8,128)(2,1)S(1)}, u32[]{:S(2)}, u32[]{:S(2)}) collective-permute-start(bf16[112,1024]{1,0:T(8,128)(2,1)S(1)} %get-tuple-element.54), channel_id=1, source_target_pairs={{0,16},{16,32},{32,48},{48,0},{1,17},{17,33},{33,49},{49,1},{2,18}... | collective-permute-start | bytes 688136 | tf_op jit(solution)/shard_map/ppermute | solution.py:312
  6.1 12.9 %collective-permute-start.1 = (bf16[112,1024]{1,0:T(8,128)(2,1)S(1)}, bf16[112,1024]{1,0:T(8,128)(2,1)S(1)}, u32[]{:S(2)}, u32[]{:S(2)}) collective-permute-start(bf16[112,1024]{1,0:T(8,128)(2,1)S(1)} %get-tuple-element.56), channel_id=1, source_target_pairs={{0,32},{16,48},{32,0},{48,16},{1,33},{17,49},{33,1},{49,17},{2,34}... | collective-permute-start | bytes 688136 | tf_op jit(solution)/shard_map/ppermute | solution.py:312
  29.5 46.2 %all-to-all-start.1 = ((bf16[8,32,2304]{2,1,0:T(8,128)(2,1)}), bf16[8,32,2304]{2,1,0:T(8,128)(2,1)S(1)}, u32[]{:S(2)}, u32[]{:S(2)}) async-start(bf16[8,32,2304]{2,1,0:T(8,128)(2,1)} %fusion.1), calls=%async_computation.1 | async-start | bytes 2359296 | tf_op jit(solution)/shard_map/all_to_all | solution.py:382
  40.2 18.7 %collective-permute-start.5 = (bf16[448,1024]{1,0:T(8,128)(2,1)}, bf16[448,1024]{1,0:T(8,128)(2,1)S(1)}, u32[]{:S(2)}, u32[]{:S(2)}) collective-permute-start(bf16[448,1024]{1,0:T(8,128)(2,1)} %shard_map.119.near), channel_id=1, source_target_pairs={{0,1},{1,0},{2,3},{3,2},{4,5},{5,4},{6,7},{7,6},{8,9},{9,8},{10,11... | collective-permute-start | bytes 2752520 | tf_op jit(solution)/shard_map/ppermute | solution.py:312
  46.3 16.6 %collective-permute-start.10 = (bf16[432,896]{1,0:T(8,128)(2,1)}, bf16[432,896]{1,0:T(8,128)(2,1)S(1)}, u32[]{:S(2)}, u32[]{:S(2)}) collective-permute-start(bf16[432,896]{1,0:T(8,128)(2,1)} %get-tuple-element.39), channel_id=1, source_target_pairs={{0,16},{16,32},{32,48},{48,0},{1,17},{17,33},{33,49},{49,1},{2,18}... | collective-permute-start | bytes 2322440 | tf_op jit(solution)/shard_map/ppermute | solution.py:312
  46.9 23.6 %collective-permute-start.11 = (bf16[432,896]{1,0:T(8,128)(2,1)}, bf16[432,896]{1,0:T(8,128)(2,1)S(1)}, u32[]{:S(2)}, u32[]{:S(2)}) collective-permute-start(bf16[432,896]{1,0:T(8,128)(2,1)} %get-tuple-element.41), channel_id=1, source_target_pairs={{0,48},{16,0},{32,16},{48,32},{1,49},{17,1},{33,17},{49,33},{2,50}... | collective-permute-start | bytes 2322440 | tf_op jit(solution)/shard_map/ppermute | solution.py:312
  49.6 25.2 %collective-permute-start.4 = (bf16[448,1024]{1,0:T(8,128)(2,1)S(1)}, bf16[448,1024]{1,0:T(8,128)(2,1)S(1)}, u32[]{:S(2)}, u32[]{:S(2)}) collective-permute-start(bf16[448,1024]{1,0:T(8,128)(2,1)S(1)} %copy-done.7), channel_id=1, source_target_pairs={{0,64},{64,0},{1,65},{65,1},{2,66},{66,2},{3,67},{67,3},{4,68},{68... | collective-permute-start | bytes 2752520 | tf_op jit(solution)/shard_map/ppermute | solution.py:312
  59.0 16.8 %collective-permute-start.6 = (bf16[448,1024]{1,0:T(8,128)(2,1)S(1)}, bf16[448,1024]{1,0:T(8,128)(2,1)}, u32[]{:S(2)}, u32[]{:S(2)}) collective-permute-start(bf16[448,1024]{1,0:T(8,128)(2,1)S(1)} %collective-permute-done.5.side), channel_id=1, source_target_pairs={{0,64},{64,0},{1,65},{65,1},{2,66},{66,2},{3,67},{67,3},{4,68},{68... | collective-permute-start | bytes 2752520 | tf_op jit(solution)/shard_map/ppermute | solution.py:312
  70.6 16.2 %collective-permute-start.12 = (bf16[432,896]{1,0:T(8,128)(2,1)}, bf16[432,896]{1,0:T(8,128)(2,1)}, u32[]{:S(2)}, u32[]{:S(2)}) collective-permute-start(bf16[432,896]{1,0:T(8,128)(2,1)} %get-tuple-element.42), channel_id=1, source_target_pairs={{0,32},{16,48},{32,0},{48,16},{1,33},{17,49},{33,1},{49,17},{2,34}... | collective-permute-start | bytes 2322440 | tf_op jit(solution)/shard_map/ppermute | solution.py:312
  73.4 35.5 %collective-permute-start.13 = (bf16[864,896]{1,0:T(8,128)(2,1)}, bf16[864,896]{1,0:T(8,128)(2,1)}, u32[]{:S(2)}, u32[]{:S(2)}) collective-permute-start(bf16[864,896]{1,0:T(8,128)(2,1)} %shard_map.123.w0), channel_id=1, source_target_pairs={{0,1},{1,128},{128,129},{129,0},{2,3},{3,130},{130,131},{131,2},{4... | collective-permute-start | bytes 4644872 | tf_op jit(solution)/shard_map/ppermute | solution.py:319
  89.4 21.6 %collective-permute-start.14 = (bf16[864,896]{1,0:T(8,128)(2,1)}, bf16[864,896]{1,0:T(8,128)(2,1)}, u32[]{:S(2)}, u32[]{:S(2)}) collective-permute-start(bf16[864,896]{1,0:T(8,128)(2,1)} %shard_map.124.w1), channel_id=1, source_target_pairs={{1,0},{128,1},{129,128},{0,129},{3,2},{130,3},{131,130},{2,131},{5... | collective-permute-start | bytes 4644872 | tf_op jit(solution)/shard_map/ppermute | solution.py:320
  89.9 7.1 %collective-permute-start.7 = (bf16[224,256]{1,0:T(8,128)(2,1)S(1)}, bf16[224,256]{1,0:T(8,128)(2,1)S(1)}, u32[]{:S(2)}, u32[]{:S(2)}) collective-permute-start(bf16[224,256]{1,0:T(8,128)(2,1)S(1)} %copy-done.21), channel_id=1, source_target_pairs={{0,48},{16,0},{32,16},{48,32},{1,49},{17,1},{33,17},{49,33},{2,50}... | collective-permute-start | bytes 344072 | tf_op jit(solution)/shard_map/ppermute | solution.py:312
  93.5 7.3 %collective-permute-start.9 = (bf16[224,256]{1,0:T(8,128)(2,1)S(1)}, bf16[224,256]{1,0:T(8,128)(2,1)S(1)}, u32[]{:S(2)}, u32[]{:S(2)}) collective-permute-start(bf16[224,256]{1,0:T(8,128)(2,1)S(1)} %copy-done.19), channel_id=1, source_target_pairs={{0,16},{16,32},{32,48},{48,0},{1,17},{17,33},{33,49},{49,1},{2,18}... | collective-permute-start | bytes 344072 | tf_op jit(solution)/shard_map/ppermute | solution.py:312
  102.0 25.3 %all-to-all-start.2 = ((bf16[8,240,256]{2,1,0:T(8,128)(2,1)}), bf16[8,240,256]{2,1,0:T(8,128)(2,1)}, u32[]{:S(2)}, u32[]{:S(2)}) async-start(bf16[8,240,256]{2,1,0:T(8,128)(2,1)} %copy-done.4), calls=%async_computation.2 | async-start | bytes 1966080 | tf_op jit(solution)/shard_map/all_to_all | solution.py:418
  111.0 16.3 %collective-permute-start.15 = (bf16[864,896]{1,0:T(8,128)(2,1)S(1)}, bf16[864,896]{1,0:T(8,128)(2,1)}, u32[]{:S(2)}, u32[]{:S(2)}) collective-permute-start(bf16[864,896]{1,0:T(8,128)(2,1)S(1)} %copy-done), channel_id=1, source_target_pairs={{0,64},{64,0},{1,65},{65,1},{2,66},{66,2},{3,67},{67,3},{4,68},{68... | collective-permute-start | bytes 4644872 | tf_op jit(solution)/shard_map/ppermute | solution.py:312
  111.0 16.3 %collective-permute-start.16 = (bf16[864,896]{1,0:T(8,128)(2,1)S(1)}, bf16[864,896]{1,0:T(8,128)(2,1)}, u32[]{:S(2)}, u32[]{:S(2)}) collective-permute-start(bf16[864,896]{1,0:T(8,128)(2,1)S(1)} %copy-done.1), channel_id=1, source_target_pairs={{0,64},{64,0},{1,65},{65,1},{2,66},{66,2},{3,67},{67,3},{4,68},{68... | collective-permute-start | bytes 4644872 | tf_op jit(solution)/shard_map/ppermute | solution.py:312
  111.5 15.8 %collective-permute-start.17 = (bf16[864,896]{1,0:T(8,128)(2,1)}, bf16[864,896]{1,0:T(8,128)(2,1)}, u32[]{:S(2)}, u32[]{:S(2)}) collective-permute-start(bf16[864,896]{1,0:T(8,128)(2,1)} %collective-permute-done.13.w2), channel_id=1, source_target_pairs={{0,64},{64,0},{1,65},{65,1},{2,66},{66,2},{3,67},{67,3},{4,68},{68... | collective-permute-start | bytes 4644872 | tf_op jit(solution)/shard_map/ppermute | solution.py:312
  111.6 15.7 %collective-permute-start.18 = (bf16[864,896]{1,0:T(8,128)(2,1)}, bf16[864,896]{1,0:T(8,128)(2,1)}, u32[]{:S(2)}, u32[]{:S(2)}) collective-permute-start(bf16[864,896]{1,0:T(8,128)(2,1)} %collective-permute-done.14.w3), channel_id=1, source_target_pairs={{0,64},{64,0},{1,65},{65,1},{2,66},{66,2},{3,67},{67,3},{4,68},{68... | collective-permute-start | bytes 4644872 | tf_op jit(solution)/shard_map/ppermute | solution.py:312
  134.9 14.5 %collective-permute-start.19 = (bf16[64,2432]{1,0:T(8,128)(2,1)S(1)}, bf16[64,2432]{1,0:T(8,128)(2,1)S(1)}, u32[]{:S(2)}, u32[]{:S(2)}) collective-permute-start(bf16[64,2432]{1,0:T(8,128)(2,1)S(1)} %get-tuple-element.49), channel_id=1, source_target_pairs={{0,16},{16,32},{32,48},{48,0},{1,17},{17,33},{33,49},{49,1},{2,18}... | collective-permute-start | bytes 933896 | tf_op jit(solution)/shard_map/ppermute | solution.py:312
  135.0 14.4 %collective-permute-start.20 = (bf16[64,2432]{1,0:T(8,128)(2,1)S(1)}, bf16[64,2432]{1,0:T(8,128)(2,1)S(1)}, u32[]{:S(2)}, u32[]{:S(2)}) collective-permute-start(bf16[64,2432]{1,0:T(8,128)(2,1)S(1)} %get-tuple-element.50), channel_id=1, source_target_pairs={{0,32},{16,48},{32,0},{48,16},{1,33},{17,49},{33,1},{49,17},{2,34}... | collective-permute-start | bytes 933896 | tf_op jit(solution)/shard_map/ppermute | solution.py:312
  137.2 12.7 %collective-permute-start.21 = (bf16[64,2432]{1,0:T(8,128)(2,1)S(1)}, bf16[64,2432]{1,0:T(8,128)(2,1)S(1)}, u32[]{:S(2)}, u32[]{:S(2)}) collective-permute-start(bf16[64,2432]{1,0:T(8,128)(2,1)S(1)} %get-tuple-element.51), channel_id=1, source_target_pairs={{0,48},{16,0},{32,16},{48,32},{1,49},{17,1},{33,17},{49,33},{2,50}... | collective-permute-start | bytes 933896 | tf_op jit(solution)/shard_map/ppermute | solution.py:312
  153.1 7.9 %collective-permute-start.22 = (bf16[64,1152]{1,0:T(8,128)(2,1)S(1)}, bf16[64,1152]{1,0:T(8,128)(2,1)S(1)}, u32[]{:S(2)}, u32[]{:S(2)}) collective-permute-start(bf16[64,1152]{1,0:T(8,128)(2,1)S(1)} %shard_map.126.h0), channel_id=1, source_target_pairs={{0,16},{16,32},{32,48},{48,0},{1,17},{17,33},{33,49},{49,1},{2,18}... | collective-permute-start | bytes 442376 | tf_op jit(solution)/shard_map/ppermute | solution.py:312
  (25 other events, 256.0 us)

commit v8 on v7

--- a/solution.py
+++ b/solution.py
@@ -371,7 +371,7 @@
     first = jnp.concatenate(
         [attended.reshape(rows, X, heads), hidden_in.reshape(rows, X, slab)], axis=2
     ).transpose(1, 0, 2)
-    first = after(first, (out_pieces, gain))
+    first = after(first, (out_pieces[1], out_pieces[3], gain))
     pieces = cut(at, *after((gate_t, up_t, down_weight), first))
     first = lax.all_to_all(first, "x", 0, 0, tiled=True).reshape(X * rows, heads + slab)
     resid = first[:, heads:].reshape(X * rows, Z, cols).transpose(1, 0, 2)

time: 200 us -> 198 us (0.990)
  blocking collectives: 41 us -> 31.9 us
  starting transfers between devices: 40.9 us -> 45.9 us
    all_to_all x1 -> x0, blocking collectives: 8.97 us -> none  [per_device(): lax.all_to_all(first, 'x', 0, 0, tiled=True).reshape(X * rows, heads + slab)]
    all_to_all x0 -> x1, waiting for transfers between devices: none -> 4.44 us  [per_device(): lax.all_to_all(first, 'x', 0, 0, tiled=True).reshape(X * rows, heads + slab)]
    all_to_all x0 -> x1, starting transfers between devices: none -> 3.82 us  [per_device(): lax.all_to_all(first, 'x', 0, 0, tiled=True).reshape(X * rows, heads + slab)]
    ppermute x23, waiting for transfers between devices: 54.7 us -> 51.1 us  [shifted(): lax.ppermute(value, axis, [(i, (i + step) % size) for i in range(size)])]
  transfers between devices with their start and end apart: 27 -> 28, of which waited for: 16 -> 16; matrix products, arithmetic and copies ran while one was open for 2% -> 4% of each run, Pallas kernels for 11% -> 11%
where the time goes in v8:
time: 198 us; the launch traced here: 196 us
  waiting for transfers between devices  72.9 us (37%)
  starting transfers between devices  45.9 us (23%)
  Pallas kernels  34 us (17%)
  blocking collectives  31.9 us (16%)
  local copies, waits for them, and re-layouts  8.02 us (4%)
  other arithmetic  3.39 us (2%)
    ppermute x23, waiting for transfers between devices, shifted(): lax.ppermute(value, axis, [(i, (i + step) % size) for i in range(size)])  51.1 us
    all_to_all x1, blocking collectives, per_device(): lax.all_to_all(result, ('x', 'z'), 0, 0, tiled=True)  31.9 us
    ppermute x23, starting transfers between devices, shifted(): lax.ppermute(value, axis, [(i, (i + step) % size) for i in range(size)])  24.8 us
    all_to_all x1, waiting for transfers between devices, per_device(): second = lax.all_to_all(second, 'z', 0, 0, tiled=True)  15.3 us
    all_to_all x1, starting transfers between devices, per_device(): lax.all_to_all(first, 'z', 0, 0, tiled=True).reshape(chunk, heads + 256)  8.47 us
    pallas_call x3, Pallas kernels, join(): call(join_kernel, jax.ShapeDtypeStruct(shape, bf16), [anywhere()] * len(p...  7.75 us
    pallas_call x1, Pallas kernels, per_device(): call(gate_up_kernel, [jax.ShapeDtypeStruct(message, t) for t in (f32, bf1...  7.58 us
    all_to_all x1, starting transfers between devices, per_device(): second = lax.all_to_all(second, 'z', 0, 0, tiled=True)  6.93 us
  transfers between devices with their start and end apart: 28, of which 16 were waited for; matrix products, arithmetic and copies ran while one was open for 4% of the time, Pallas kernels for 11%

profile of v8, /device:TPU:16, one launch (start us, length us, event | category | flops | bytes accessed | tf_op | source)
XLA Modules:
  0.0 196.4 jit_solution(7859790327790255092)
XLA Ops:
  3.3 2.8 %collective-permute-start.1 = (bf16[112,1024]{1,0:T(8,128)(2,1)S(1)}, bf16[112,1024]{1,0:T(8,128)(2,1)S(1)}, u32[]{:S(2)}, u32[]{:S(2)}) collective-permute-start(bf16[112,1024]{1,0:T(8,128)(2,1)S(1)} %get-tuple-element.54), channel_id=1, source_target_pairs={{0,48},{16,0},{32,16},{48,32},{1,49},{17,1},{33,17},{49,33},{2,50}... | collective-permute-start | bytes 688136 | tf_op jit(solution)/shard_map/ppermute | solution.py:312
  6.8 4.4 %shard_map.118 = bf16[8,32,256]{2,1,0:T(8,128)(2,1)} custom-call(s32[1,8]{1,0:T(1,128)} %counts.1, s32[8]{0:T(128)} %tails.1, s32[1,16]{1,0:T(1,128)} %order.1, bf16[8,32,256]{2,1,0:T(8,128)(2,1)} %bitcast.42, bf16[8,512]{1,0:T(8,128)(2,1)} %new_ref.1, bf16[16,256,512]{2,1,0:T(8,128)(2,1)} %kv_ref.1), custom_call_target="tpu_custom_call" | custom-call | flops 134217728 | bytes 4194304 | tf_op jit(solution)/shard_map/pallas_call | solution.py:128
  14.1 3.8 %all-to-all-start = ((bf16[4,8,3840]{2,1,0:T(8,128)(2,1)}), bf16[4,8,3840]{2,1,0:T(8,128)(2,1)S(1)}, u32[]{:S(2)}, u32[]{:S(2)}) async-start(bf16[4,8,3840]{2,1,0:T(8,128)(2,1)} %maximum_bitcast_fusion), calls=%async_computation | async-start | bytes 491520 | tf_op jit(solution)/shard_map/all_to_all | solution.py:376
  17.9 3.5 %collective-permute-start.3 = (bf16[112,1024]{1,0:T(8,128)(2,1)S(1)}, bf16[112,1024]{1,0:T(8,128)(2,1)S(1)}, u32[]{:S(2)}, u32[]{:S(2)}) collective-permute-start(bf16[112,1024]{1,0:T(8,128)(2,1)S(1)} %get-tuple-element.53), channel_id=1, source_target_pairs={{0,32},{16,48},{32,0},{48,16},{1,33},{17,49},{33,1},{49,17},{2,34}... | collective-permute-start | bytes 688136 | tf_op jit(solution)/shard_map/ppermute | solution.py:312
  21.4 4.4 %all-to-all-done = bf16[4,8,3840]{2,1,0:T(8,128)(2,1)S(1)} async-done(((bf16[4,8,3840]{2,1,0:T(8,128)(2,1)}), bf16[4,8,3840]{2,1,0:T(8,128)(2,1)S(1)}, u32[]{:S(2)}, u32[]{:S(2)}) %all-to-all-start) | async-done | bytes 245792 | tf_op jit(solution)/shard_map/all_to_all | solution.py:376
  27.4 8.5 %all-to-all-start.1 = ((bf16[8,32,2304]{2,1,0:T(8,128)(2,1)}), bf16[8,32,2304]{2,1,0:T(8,128)(2,1)S(1)}, u32[]{:S(2)}, u32[]{:S(2)}) async-start(bf16[8,32,2304]{2,1,0:T(8,128)(2,1)} %fusion.1), calls=%async_computation.1 | async-start | bytes 2359296 | tf_op jit(solution)/shard_map/all_to_all | solution.py:382
  40.3 4.6 %shard_map.122 = (bf16[432,896]{1,0:T(8,128)(2,1)}, bf16[432,896]{1,0:T(8,128)(2,1)}, bf16[432,896]{1,0:T(8,128)(2,1)}, bf16[432,896]{1,0:T(8,128)(2,1)}) custom-call(s32[4]{0:T(128)} %pad_add_fusion.at, bf16[144,7168]{1,0:T(8,128)(2,1)} %bitcast.36, bf16[144,7168]{1,0:T(8,128)(2,1)} %bitcast.37, bf16[144,7168]{1,0:T(8,128)(2,1)} %down), custom_call_target="tpu_custom_call" | custom-call | bytes 6193152 | tf_op jit(solution)/shard_map/pallas_call | solution.py:72
  48.2 9.1 %collective-permute-done.5.side = bf16[448,1024]{1,0:T(8,128)(2,1)S(1)} collective-permute-done((bf16[448,1024]{1,0:T(8,128)(2,1)}, bf16[448,1024]{1,0:T(8,128)(2,1)S(1)}, u32[]{:S(2)}, u32[]{:S(2)}) %collective-permute-start.5) | collective-permute-done | bytes 917536 | tf_op jit(solution)/shard_map/ppermute | solution.py:312
  57.3 3.9 %collective-permute-done.10.refs_1_ = bf16[432,896]{1,0:T(8,128)(2,1)S(1)} collective-permute-done((bf16[432,896]{1,0:T(8,128)(2,1)}, bf16[432,896]{1,0:T(8,128)(2,1)S(1)}, u32[]{:S(2)}, u32[]{:S(2)}) %collective-permute-start.10) | collective-permute-done | bytes 774176 | tf_op jit(solution)/shard_map/ppermute | solution.py:312
  61.2 7.7 %collective-permute-done.11.refs_1_ = bf16[432,896]{1,0:T(8,128)(2,1)S(1)} collective-permute-done((bf16[432,896]{1,0:T(8,128)(2,1)}, bf16[432,896]{1,0:T(8,128)(2,1)S(1)}, u32[]{:S(2)}, u32[]{:S(2)}) %collective-permute-start.11) | collective-permute-done | bytes 774176 | tf_op jit(solution)/shard_map/ppermute | solution.py:312
  68.9 2.8 %shard_map.123.w0 = bf16[864,896]{1,0:T(8,128)(2,1)} custom-call(bf16[432,896]{1,0:T(8,128)(2,1)} %get-tuple-element.38.refs_0_, bf16[432,896]{1,0:T(8,128)(2,1)} %copy-done.11), custom_call_target="tpu_custom_call" | custom-call | bytes 3096576 | tf_op jit(solution)/shard_map/pallas_call | solution.py:155
  75.1 4.9 %shard_map.120 = (f32[224,256]{1,0:T(8,128)}, bf16[224,256]{1,0:T(8,128)(2,1)}, bf16[224,256]{1,0:T(8,128)(2,1)}, bf16[224,256]{1,0:T(8,128)(2,1)}) custom-call(s32[4]{0:T(128)} %pad_add_fusion.at, bf16[256,2304]{1,0:T(8,128)(2,1)} %bitcast.33, bf16[448,1024]{1,0:T(8,128)(2,1)} %shard_map.119.near, bf16[448,1024]{1,0:T(8,128)(2,1)} %copy-done.9, ...), custom_call_target="tpu_custom_call" | custom-call | flops 939524096 | bytes 7340032 | tf_op jit(solution)/shard_map/pallas_call | solution.py:390
  80.0 5.1 %collective-permute-done.12.refs_0_ = bf16[432,896]{1,0:T(8,128)(2,1)} collective-permute-done((bf16[432,896]{1,0:T(8,128)(2,1)}, bf16[432,896]{1,0:T(8,128)(2,1)}, u32[]{:S(2)}, u32[]{:S(2)}) %collective-permute-start.12) | collective-permute-done | bytes 774176 | tf_op jit(solution)/shard_map/ppermute | solution.py:312
  85.1 2.7 %shard_map.124.w1 = bf16[864,896]{1,0:T(8,128)(2,1)} custom-call(bf16[432,896]{1,0:T(8,128)(2,1)} %collective-permute-done.12.refs_0_, bf16[432,896]{1,0:T(8,128)(2,1)} %copy-done.10), custom_call_target="tpu_custom_call" | custom-call | bytes 3096576 | tf_op jit(solution)/shard_map/pallas_call | solution.py:155
  88.3 3.5 %collective-permute-start.7 = (bf16[224,256]{1,0:T(8,128)(2,1)S(1)}, bf16[224,256]{1,0:T(8,128)(2,1)S(1)}, u32[]{:S(2)}, u32[]{:S(2)}) collective-permute-start(bf16[224,256]{1,0:T(8,128)(2,1)S(1)} %copy-done.21), channel_id=1, source_target_pairs={{0,48},{16,0},{32,16},{48,32},{1,49},{17,1},{33,17},{49,33},{2,50}... | collective-permute-start | bytes 344072 | tf_op jit(solution)/shard_map/ppermute | solution.py:312
  95.4 2.8 %collective-permute-done.8.r2 = bf16[224,256]{1,0:T(8,128)(2,1)S(1)} collective-permute-done((bf16[224,256]{1,0:T(8,128)(2,1)S(1)}, bf16[224,256]{1,0:T(8,128)(2,1)S(1)}, u32[]{:S(2)}, u32[]{:S(2)}) %collective-permute-start.8) | collective-permute-done | bytes 114720 | tf_op jit(solution)/shard_map/ppermute | solution.py:312
  100.3 6.9 %all-to-all-start.2 = ((bf16[8,240,256]{2,1,0:T(8,128)(2,1)}), bf16[8,240,256]{2,1,0:T(8,128)(2,1)}, u32[]{:S(2)}, u32[]{:S(2)}) async-start(bf16[8,240,256]{2,1,0:T(8,128)(2,1)} %copy-done.4), calls=%async_computation.2 | async-start | bytes 1966080 | tf_op jit(solution)/shard_map/all_to_all | solution.py:418
  110.3 15.3 %all-to-all-done.2.second = bf16[8,240,256]{2,1,0:T(8,128)(2,1)} async-done(((bf16[8,240,256]{2,1,0:T(8,128)(2,1)}), bf16[8,240,256]{2,1,0:T(8,128)(2,1)}, u32[]{:S(2)}, u32[]{:S(2)}) %all-to-all-start.2) | async-done | bytes 983072 | tf_op jit(solution)/shard_map/all_to_all | solution.py:418
  125.7 7.6 %shard_map.125 = (f32[64,2432]{1,0:T(8,128)S(1)}, bf16[64,2432]{1,0:T(8,128)(2,1)S(1)}, bf16[64,2432]{1,0:T(8,128)(2,1)S(1)}, bf16[64,2432]{1,0:T(8,128)(2,1)S(1)}) custom-call(s32[4]{0:T(128)S(1)} %copy-done.6, bf16[8,240,256]{2,1,0:T(8,128)(2,1)} %all-to-all-done.2.second, bf16[864,896]{1,0:T(8,128)(2,1)S(1)} %copy-done, bf16[864,896]{1,0:T(8,128)(2,1)S(1)} %copy-done.1, ...), custom_call_target="tpu_custom_call" | custom-call | flops 2113929216 | bytes 16515072 | tf_op jit(solution)/shard_map/pallas_call | solution.py:421
  137.0 10.7 %collective-permute-done.19.refs_1_ = bf16[64,2432]{1,0:T(8,128)(2,1)S(1)} collective-permute-done((bf16[64,2432]{1,0:T(8,128)(2,1)S(1)}, bf16[64,2432]{1,0:T(8,128)(2,1)S(1)}, u32[]{:S(2)}, u32[]{:S(2)}) %collective-permute-start.19) | collective-permute-done | bytes 311328 | tf_op jit(solution)/shard_map/ppermute | solution.py:312
  148.6 2.7 %collective-permute-start.24 = (bf16[64,1152]{1,0:T(8,128)(2,1)S(1)}, bf16[64,1152]{1,0:T(8,128)(2,1)S(1)}, u32[]{:S(2)}, u32[]{:S(2)}) collective-permute-start(bf16[64,1152]{1,0:T(8,128)(2,1)S(1)} %shard_map.126.h0), channel_id=1, source_target_pairs={{0,48},{16,0},{32,16},{48,32},{1,49},{17,1},{33,17},{49,33},{2,50}... | collective-permute-start | bytes 442376 | tf_op jit(solution)/shard_map/ppermute | solution.py:312
  152.2 3.3 %collective-permute-done.24.h3 = bf16[64,1152]{1,0:T(8,128)(2,1)S(1)} collective-permute-done((bf16[64,1152]{1,0:T(8,128)(2,1)S(1)}, bf16[64,1152]{1,0:T(8,128)(2,1)S(1)}, u32[]{:S(2)}, u32[]{:S(2)}) %collective-permute-start.24) | collective-permute-done | bytes 147488 | tf_op jit(solution)/shard_map/ppermute | solution.py:312
  159.4 4.3 %shard_map.127 = bf16[256,1792]{1,0:T(8,128)(2,1)S(1)} custom-call(s32[4]{0:T(128)S(1)} %copy-done.6, bf16[64,1152]{1,0:T(8,128)(2,1)S(1)} %shard_map.126.h0, bf16[64,1152]{1,0:T(8,128)(2,1)S(1)} %collective-permute-done.22.h1, bf16[64,1152]{1,0:T(8,128)(2,1)S(1)} %collective-permute-done.23.h2, bf16[64,1152]{1,0:T(8,128)(2,1)S(1)} %collective-permute-done.24.h3, ...), custom_call_target="tpu_custom_call" | custom-call | flops 1056964608 | bytes 8257536 | tf_op jit(solution)/shard_map/pallas_call | solution.py:445
  163.7 31.9 %all_to_all.20 = bf16[32,8,1792]{2,1,0:T(8,128)(2,1)S(1)} all-to-all(bf16[32,8,1792]{2,1,0:T(8,128)(2,1)S(1)} %bitcast.35), channel_id=1, replica_groups=mesh['role'=2,'pair'=2,'x'=4,'z'=8,'y'=2] {'x','z'}, dimensions={0} | all-to-all | bytes 1835008 | tf_op jit(solution)/shard_map/all_to_all | solution.py:459
  (105 shorter events, 38.9 us)
Async XLA Ops:
  0.0 12.9 %collective-permute-start.2 = (f32[112]{0:T(128)}, f32[112]{0:T(128)S(1)}, u32[]{:S(2)}, u32[]{:S(2)}) collective-permute-start(f32[112]{0:T(128)} %param.20), channel_id=1, source_target_pairs={{0,1},{1,0},{2,3},{3,2},{4,5},{5,4},{6,7},{7,6},{8,9},{9,8},{10,11... | collective-permute-start | bytes 1352 | tf_op jit(solution)/shard_map/ppermute | solution.py:312
  3.3 10.0 %collective-permute-start.1 = (bf16[112,1024]{1,0:T(8,128)(2,1)S(1)}, bf16[112,1024]{1,0:T(8,128)(2,1)S(1)}, u32[]{:S(2)}, u32[]{:S(2)}) collective-permute-start(bf16[112,1024]{1,0:T(8,128)(2,1)S(1)} %get-tuple-element.54), channel_id=1, source_target_pairs={{0,48},{16,0},{32,16},{48,32},{1,49},{17,1},{33,17},{49,33},{2,50}... | collective-permute-start | bytes 688136 | tf_op jit(solution)/shard_map/ppermute | solution.py:312
  6.1 8.0 %collective-permute-start = (bf16[112,1024]{1,0:T(8,128)(2,1)S(1)}, bf16[112,1024]{1,0:T(8,128)(2,1)S(1)}, u32[]{:S(2)}, u32[]{:S(2)}) collective-permute-start(bf16[112,1024]{1,0:T(8,128)(2,1)S(1)} %get-tuple-element.55), channel_id=1, source_target_pairs={{0,16},{16,32},{32,48},{48,0},{1,17},{17,33},{33,49},{49,1},{2,18}... | collective-permute-start | bytes 688136 | tf_op jit(solution)/shard_map/ppermute | solution.py:312
  14.1 11.8 %all-to-all-start = ((bf16[4,8,3840]{2,1,0:T(8,128)(2,1)}), bf16[4,8,3840]{2,1,0:T(8,128)(2,1)S(1)}, u32[]{:S(2)}, u32[]{:S(2)}) async-start(bf16[4,8,3840]{2,1,0:T(8,128)(2,1)} %maximum_bitcast_fusion), calls=%async_computation | async-start | bytes 491520 | tf_op jit(solution)/shard_map/all_to_all | solution.py:376
  17.9 18.0 %collective-permute-start.3 = (bf16[112,1024]{1,0:T(8,128)(2,1)S(1)}, bf16[112,1024]{1,0:T(8,128)(2,1)S(1)}, u32[]{:S(2)}, u32[]{:S(2)}) collective-permute-start(bf16[112,1024]{1,0:T(8,128)(2,1)S(1)} %get-tuple-element.53), channel_id=1, source_target_pairs={{0,32},{16,48},{32,0},{48,16},{1,33},{17,49},{33,1},{49,17},{2,34}... | collective-permute-start | bytes 688136 | tf_op jit(solution)/shard_map/ppermute | solution.py:312
  27.4 46.7 %all-to-all-start.1 = ((bf16[8,32,2304]{2,1,0:T(8,128)(2,1)}), bf16[8,32,2304]{2,1,0:T(8,128)(2,1)S(1)}, u32[]{:S(2)}, u32[]{:S(2)}) async-start(bf16[8,32,2304]{2,1,0:T(8,128)(2,1)} %fusion.1), calls=%async_computation.1 | async-start | bytes 2359296 | tf_op jit(solution)/shard_map/all_to_all | solution.py:382
  38.8 18.5 %collective-permute-start.5 = (bf16[448,1024]{1,0:T(8,128)(2,1)}, bf16[448,1024]{1,0:T(8,128)(2,1)S(1)}, u32[]{:S(2)}, u32[]{:S(2)}) collective-permute-start(bf16[448,1024]{1,0:T(8,128)(2,1)} %shard_map.119.near), channel_id=1, source_target_pairs={{0,1},{1,0},{2,3},{3,2},{4,5},{5,4},{6,7},{7,6},{8,9},{9,8},{10,11... | collective-permute-start | bytes 2752520 | tf_op jit(solution)/shard_map/ppermute | solution.py:312
  44.9 16.3 %collective-permute-start.10 = (bf16[432,896]{1,0:T(8,128)(2,1)}, bf16[432,896]{1,0:T(8,128)(2,1)S(1)}, u32[]{:S(2)}, u32[]{:S(2)}) collective-permute-start(bf16[432,896]{1,0:T(8,128)(2,1)} %get-tuple-element.39), channel_id=1, source_target_pairs={{0,16},{16,32},{32,48},{48,0},{1,17},{17,33},{33,49},{49,1},{2,18}... | collective-permute-start | bytes 2322440 | tf_op jit(solution)/shard_map/ppermute | solution.py:312
  46.7 22.2 %collective-permute-start.11 = (bf16[432,896]{1,0:T(8,128)(2,1)}, bf16[432,896]{1,0:T(8,128)(2,1)S(1)}, u32[]{:S(2)}, u32[]{:S(2)}) collective-permute-start(bf16[432,896]{1,0:T(8,128)(2,1)} %get-tuple-element.41), channel_id=1, source_target_pairs={{0,48},{16,0},{32,16},{48,32},{1,49},{17,1},{33,17},{49,33},{2,50}... | collective-permute-start | bytes 2322440 | tf_op jit(solution)/shard_map/ppermute | solution.py:312
  48.2 24.9 %collective-permute-start.4 = (bf16[448,1024]{1,0:T(8,128)(2,1)S(1)}, bf16[448,1024]{1,0:T(8,128)(2,1)S(1)}, u32[]{:S(2)}, u32[]{:S(2)}) collective-permute-start(bf16[448,1024]{1,0:T(8,128)(2,1)S(1)} %copy-done.7), channel_id=1, source_target_pairs={{0,64},{64,0},{1,65},{65,1},{2,66},{66,2},{3,67},{67,3},{4,68},{68... | collective-permute-start | bytes 2752520 | tf_op jit(solution)/shard_map/ppermute | solution.py:312
  57.3 16.8 %collective-permute-start.6 = (bf16[448,1024]{1,0:T(8,128)(2,1)S(1)}, bf16[448,1024]{1,0:T(8,128)(2,1)}, u32[]{:S(2)}, u32[]{:S(2)}) collective-permute-start(bf16[448,1024]{1,0:T(8,128)(2,1)S(1)} %collective-permute-done.5.side), channel_id=1, source_target_pairs={{0,64},{64,0},{1,65},{65,1},{2,66},{66,2},{3,67},{67,3},{4,68},{68... | collective-permute-start | bytes 2752520 | tf_op jit(solution)/shard_map/ppermute | solution.py:312
  68.9 16.2 %collective-permute-start.12 = (bf16[432,896]{1,0:T(8,128)(2,1)}, bf16[432,896]{1,0:T(8,128)(2,1)}, u32[]{:S(2)}, u32[]{:S(2)}) collective-permute-start(bf16[432,896]{1,0:T(8,128)(2,1)} %get-tuple-element.42), channel_id=1, source_target_pairs={{0,32},{16,48},{32,0},{48,16},{1,33},{17,49},{33,1},{49,17},{2,34}... | collective-permute-start | bytes 2322440 | tf_op jit(solution)/shard_map/ppermute | solution.py:312
  71.8 35.5 %collective-permute-start.13 = (bf16[864,896]{1,0:T(8,128)(2,1)}, bf16[864,896]{1,0:T(8,128)(2,1)}, u32[]{:S(2)}, u32[]{:S(2)}) collective-permute-start(bf16[864,896]{1,0:T(8,128)(2,1)} %shard_map.123.w0), channel_id=1, source_target_pairs={{0,1},{1,128},{128,129},{129,0},{2,3},{3,130},{130,131},{131,2},{4... | collective-permute-start | bytes 4644872 | tf_op jit(solution)/shard_map/ppermute | solution.py:319
  87.7 21.5 %collective-permute-start.14 = (bf16[864,896]{1,0:T(8,128)(2,1)}, bf16[864,896]{1,0:T(8,128)(2,1)}, u32[]{:S(2)}, u32[]{:S(2)}) collective-permute-start(bf16[864,896]{1,0:T(8,128)(2,1)} %shard_map.124.w1), channel_id=1, source_target_pairs={{1,0},{128,1},{129,128},{0,129},{3,2},{130,3},{131,130},{2,131},{5... | collective-permute-start | bytes 4644872 | tf_op jit(solution)/shard_map/ppermute | solution.py:320
  91.8 7.3 %collective-permute-start.9 = (bf16[224,256]{1,0:T(8,128)(2,1)S(1)}, bf16[224,256]{1,0:T(8,128)(2,1)S(1)}, u32[]{:S(2)}, u32[]{:S(2)}) collective-permute-start(bf16[224,256]{1,0:T(8,128)(2,1)S(1)} %copy-done.19), channel_id=1, source_target_pairs={{0,16},{16,32},{32,48},{48,0},{1,17},{17,33},{33,49},{49,1},{2,18}... | collective-permute-start | bytes 344072 | tf_op jit(solution)/shard_map/ppermute | solution.py:312
  100.3 25.3 %all-to-all-start.2 = ((bf16[8,240,256]{2,1,0:T(8,128)(2,1)}), bf16[8,240,256]{2,1,0:T(8,128)(2,1)}, u32[]{:S(2)}, u32[]{:S(2)}) async-start(bf16[8,240,256]{2,1,0:T(8,128)(2,1)} %copy-done.4), calls=%async_computation.2 | async-start | bytes 1966080 | tf_op jit(solution)/shard_map/all_to_all | solution.py:418
  109.3 16.3 %collective-permute-start.15 = (bf16[864,896]{1,0:T(8,128)(2,1)S(1)}, bf16[864,896]{1,0:T(8,128)(2,1)}, u32[]{:S(2)}, u32[]{:S(2)}) collective-permute-start(bf16[864,896]{1,0:T(8,128)(2,1)S(1)} %copy-done), channel_id=1, source_target_pairs={{0,64},{64,0},{1,65},{65,1},{2,66},{66,2},{3,67},{67,3},{4,68},{68... | collective-permute-start | bytes 4644872 | tf_op jit(solution)/shard_map/ppermute | solution.py:312
  109.3 16.3 %collective-permute-start.16 = (bf16[864,896]{1,0:T(8,128)(2,1)S(1)}, bf16[864,896]{1,0:T(8,128)(2,1)}, u32[]{:S(2)}, u32[]{:S(2)}) collective-permute-start(bf16[864,896]{1,0:T(8,128)(2,1)S(1)} %copy-done.1), channel_id=1, source_target_pairs={{0,64},{64,0},{1,65},{65,1},{2,66},{66,2},{3,67},{67,3},{4,68},{68... | collective-permute-start | bytes 4644872 | tf_op jit(solution)/shard_map/ppermute | solution.py:312
  109.8 15.8 %collective-permute-start.17 = (bf16[864,896]{1,0:T(8,128)(2,1)}, bf16[864,896]{1,0:T(8,128)(2,1)}, u32[]{:S(2)}, u32[]{:S(2)}) collective-permute-start(bf16[864,896]{1,0:T(8,128)(2,1)} %collective-permute-done.13.w2), channel_id=1, source_target_pairs={{0,64},{64,0},{1,65},{65,1},{2,66},{66,2},{3,67},{67,3},{4,68},{68... | collective-permute-start | bytes 4644872 | tf_op jit(solution)/shard_map/ppermute | solution.py:312
  109.9 15.7 %collective-permute-start.18 = (bf16[864,896]{1,0:T(8,128)(2,1)}, bf16[864,896]{1,0:T(8,128)(2,1)}, u32[]{:S(2)}, u32[]{:S(2)}) collective-permute-start(bf16[864,896]{1,0:T(8,128)(2,1)} %collective-permute-done.14.w3), channel_id=1, source_target_pairs={{0,64},{64,0},{1,65},{65,1},{2,66},{66,2},{3,67},{67,3},{4,68},{68... | collective-permute-start | bytes 4644872 | tf_op jit(solution)/shard_map/ppermute | solution.py:312
  133.2 14.5 %collective-permute-start.19 = (bf16[64,2432]{1,0:T(8,128)(2,1)S(1)}, bf16[64,2432]{1,0:T(8,128)(2,1)S(1)}, u32[]{:S(2)}, u32[]{:S(2)}) collective-permute-start(bf16[64,2432]{1,0:T(8,128)(2,1)S(1)} %get-tuple-element.49), channel_id=1, source_target_pairs={{0,16},{16,32},{32,48},{48,0},{1,17},{17,33},{33,49},{49,1},{2,18}... | collective-permute-start | bytes 933896 | tf_op jit(solution)/shard_map/ppermute | solution.py:312
  133.3 14.4 %collective-permute-start.20 = (bf16[64,2432]{1,0:T(8,128)(2,1)S(1)}, bf16[64,2432]{1,0:T(8,128)(2,1)S(1)}, u32[]{:S(2)}, u32[]{:S(2)}) collective-permute-start(bf16[64,2432]{1,0:T(8,128)(2,1)S(1)} %get-tuple-element.50), channel_id=1, source_target_pairs={{0,32},{16,48},{32,0},{48,16},{1,33},{17,49},{33,1},{49,17},{2,34}... | collective-permute-start | bytes 933896 | tf_op jit(solution)/shard_map/ppermute | solution.py:312
  135.6 12.7 %collective-permute-start.21 = (bf16[64,2432]{1,0:T(8,128)(2,1)S(1)}, bf16[64,2432]{1,0:T(8,128)(2,1)S(1)}, u32[]{:S(2)}, u32[]{:S(2)}) collective-permute-start(bf16[64,2432]{1,0:T(8,128)(2,1)S(1)} %get-tuple-element.51), channel_id=1, source_target_pairs={{0,48},{16,0},{32,16},{48,32},{1,49},{17,1},{33,17},{49,33},{2,50}... | collective-permute-start | bytes 933896 | tf_op jit(solution)/shard_map/ppermute | solution.py:312
  151.5 7.9 %collective-permute-start.22 = (bf16[64,1152]{1,0:T(8,128)(2,1)S(1)}, bf16[64,1152]{1,0:T(8,128)(2,1)S(1)}, u32[]{:S(2)}, u32[]{:S(2)}) collective-permute-start(bf16[64,1152]{1,0:T(8,128)(2,1)S(1)} %shard_map.126.h0), channel_id=1, source_target_pairs={{0,16},{16,32},{32,48},{48,0},{1,17},{17,33},{33,49},{49,1},{2,18}... | collective-permute-start | bytes 442376 | tf_op jit(solution)/shard_map/ppermute | solution.py:312
  (26 other events, 254.6 us)
